TPU v7x, 32 devices: a whole 2x2x4 slice. The times are simulated.
32 devices in a mesh: dp: 16 (over z, x, core), ctx: 2 (over y).
Axes of the slice: x: 2, y: 2, z: 4, core: 2. Of those that a mesh axis runs over, the one named last changes fastest.
Arguments:
- queries: bfloat16 [16384, 1024], P(('dp', 'ctx')), may hold values from -6 to 6
- keys_values: bfloat16 [16384, 1, 2, 128], P(('dp', 'ctx')), may hold values from -6 to 6
- routing: int32 [16384, 2], P(('dp', 'ctx')), may hold values from 0 to 511, as said below
- documents: int32 [16384], P(('dp', 'ctx')), may hold values from 0 to 16383, as said below
Outputs:
- attended: bfloat16 [16384, 1024], P(('dp', 'ctx'))
Inputs may be any that keep to these rules, and one draw needn't show every extreme that they name: routing[r, 0] is the packed sequence and routing[r, 1] the position inside the 512-token block (the block at the owner's index along ctx) to which owner row r goes; every position is filled exactly once. Each aligned block of 64 rows of one owner goes, in order, to 64 consecutive positions of one destination, and different blocks of one owner go to different destinations. `documents`: A token's document id is 1024 times its packed sequence plus the position in that sequence at which its document begins; in every draw some sequence other than the last is one whole document, and every other sequence ends with a one-token document.
All inputs are finite; a program needn't handle non-finite values.
Results may differ from a plain program's by a relative error of at most 0.0045.
Values may be sent and summed in bfloat16 or wider, within the bound.
No kernel may reach another device: no remote copies, remote signals or barrier semaphores. Data moves between devices by JAX's collectives and lax.ppermute only.
A program may use at most 64 MiB of HBM per device.

v0:
```python
import math

import jax
import jax.numpy as jnp
from jax import lax
from jax.sharding import PartitionSpec as P


def attend_rows(local_q, local_kv, local_doc):
    rows_dev = local_q.shape[0]
    groups = local_q.shape[1]
    head_dim = local_kv.shape[2] // 2
    per_group = local_q.shape[2] // head_dim
    query_heads = local_q.reshape(rows_dev, groups, per_group, head_dim)
    query_pos = lax.axis_index("ctx") * rows_dev + jnp.arange(rows_dev, dtype=jnp.int32)
    factor = 1.0 / math.sqrt(head_dim)

    def update(state_now, block_kv, block_doc, begin_at):
        width = block_kv.shape[0]
        key_pos = begin_at + jnp.arange(width, dtype=jnp.int32)
        allowed = (local_doc[:, None] == block_doc[None, :]) & (
            key_pos[None, :] <= query_pos[:, None]
        )
        wide_mask = allowed[:, None, None, :]
        peaks, totals, mixed = state_now
        scores = (
            jnp.einsum(
                "tgqd,kgd->tgqk",
                query_heads,
                block_kv[:, :, :head_dim],
                preferred_element_type=jnp.float32,
            )
            * factor
        )
        scores = jnp.where(wide_mask, scores, -1e30)
        new_peaks = jnp.maximum(peaks, jnp.max(scores, axis=-1))
        weights = jnp.where(wide_mask, jnp.exp(scores - new_peaks[..., None]), 0.0)
        decay = jnp.exp(peaks - new_peaks)
        new_totals = totals * decay + jnp.sum(weights, axis=-1)
        product = jnp.einsum(
            "tgqk,kgd->tgqd",
            weights.astype(jnp.bfloat16),
            block_kv[:, :, head_dim:],
            preferred_element_type=jnp.float32,
        )
        return (new_peaks, new_totals, mixed * decay[..., None] + product)

    initial = (
        jnp.full((rows_dev, groups, per_group), -1e30, jnp.float32),
        jnp.zeros((rows_dev, groups, per_group), jnp.float32),
        jnp.zeros((rows_dev, groups, per_group, head_dim), jnp.float32),
    )
    block_kv = lax.all_gather(local_kv, "ctx", axis=0, tiled=True)
    block_doc = lax.all_gather(local_doc, "ctx", axis=0, tiled=True)
    width = block_kv.shape[0]
    count = width // rows_dev
    split_kv = block_kv.reshape(count, rows_dev, groups, 2 * head_dim)
    split_doc = block_doc.reshape(count, rows_dev)
    offsets = rows_dev * jnp.arange(count, dtype=jnp.int32)

    def step(state_in, parts):
        return (update(state_in, parts[0], parts[1], parts[2]), None)

    state_out, unused = lax.scan(step, initial, (split_kv, split_doc, offsets))
    peaks, totals, mixed = state_out
    result = mixed / totals[..., None]
    return result.reshape(rows_dev, groups, per_group * head_dim).astype(jnp.bfloat16)


def local(queries, keys_values, routing, documents):
    rows_dev = queries.shape[0]
    owners = lax.axis_size("dp")
    capacity = 2 * rows_dev // owners
    kv_heads = keys_values.shape[1]
    head_dim = keys_values.shape[3]
    full_width = queries.shape[1]
    group_width = full_width // kv_heads
    buckets = routing[:, 0] * capacity + jnp.arange(rows_dev, dtype=jnp.int32) % capacity
    send_q = jnp.zeros((owners * capacity, full_width), jnp.bfloat16).at[buckets].set(queries)
    send_kv = (
        jnp.zeros((owners * capacity, kv_heads, 2 * head_dim), jnp.bfloat16)
        .at[buckets]
        .set(keys_values.reshape(rows_dev, kv_heads, 2 * head_dim))
    )
    empty_labels = jnp.stack(
        [
            jnp.full((owners * capacity,), rows_dev, jnp.int32),
            jnp.full((owners * capacity,), -1, jnp.int32),
        ],
        axis=1,
    )
    labels = empty_labels.at[buckets].set(jnp.stack([routing[:, 1], documents], axis=1))
    parcel_q = send_q.reshape(owners, capacity, kv_heads, group_width)
    parcel_kv = send_kv.reshape(owners, capacity, kv_heads, 2 * head_dim)
    parcel_labels = labels.reshape(owners, capacity, 1, 2)
    in_q = lax.all_to_all(parcel_q, "dp", split_axis=0, concat_axis=0, tiled=True)
    in_kv = lax.all_to_all(parcel_kv, "dp", split_axis=0, concat_axis=0, tiled=True)
    in_labels = lax.all_to_all(parcel_labels, "dp", split_axis=0, concat_axis=0, tiled=True)
    groups = in_q.shape[2]
    total_rows = in_q.shape[0] * in_q.shape[1]
    targets = in_labels[:, :, 0, 0].reshape(total_rows)
    doc_in = in_labels[:, :, 0, 1].reshape(total_rows)
    local_q = (
        jnp.zeros((rows_dev, groups, group_width), jnp.bfloat16)
        .at[targets]
        .set(in_q.reshape(total_rows, groups, group_width), mode="drop")
    )
    local_kv = (
        jnp.zeros((rows_dev, groups, 2 * head_dim), jnp.bfloat16)
        .at[targets]
        .set(in_kv.reshape(total_rows, groups, 2 * head_dim), mode="drop")
    )
    local_doc = jnp.full((rows_dev,), -1, jnp.int32).at[targets].set(doc_in, mode="drop")
    attended = attend_rows(local_q, local_kv, local_doc)
    return attended.reshape(rows_dev, full_width)


def solution(mesh):
    placed = (
        P(("dp", "ctx"), None),
        P(("dp", "ctx"), None, None, None),
        P(("dp", "ctx"), None),
        P(("dp", "ctx")),
    )
    return jax.shard_map(
        local, mesh=mesh, in_specs=placed, out_specs=P(("dp", "ctx"), None), check_vma=False
    )
```

profile of v0, /device:TPU:11, one launch (start us, length us, event | category | flops | bytes accessed | tf_op | source)
XLA Modules:
  0.0 132.5 jit_solution(14414017710360872236)
XLA Ops:
  0.0 0.8 fusion.30
  0.8 0.7 pad_add_fusion
  1.5 0.1 copy.24
  1.6 1.0 copy.56
  2.7 1.9 %scatter_fusion = s32[1024,2]{1,0:T(8,128)S(1)} fusion(s32[1024,2]{1,0:T(8,128)S(1)} %copy.56, s32[512]{0:T(512)S(1)} %bitcast.122, s32[512,2]{1,0:T(8,128)S(1)} %copy.24), kind=kCustom, calls=%fused_computation | custom fusion | bytes 14336 | tf_op jit(solution)/shard_map/scatter | solution.py:92
  4.6 0.2 copy.25
  4.8 0.7 reshape.266
  5.5 6.6 %all-to-all-start = ((s32[16,1,128]{2,1,0:T(1,128)}), s32[16,1,128]{2,1,0:T(1,128)S(1)}, u32[]{:S(2)}, u32[]{:S(2)}) async-start(s32[16,1,128]{2,1,0:T(1,128)} %reshape.266), calls=%async_computation | async-start | bytes 16384 | tf_op jit(solution)/shard_map/all_to_all | solution.py:98
  12.1 0.0 copy-done.2
  12.1 3.1 %scatter_custom_fusion.2 = bf16[1024,256]{1,0:T(8,128)(2,1)} fusion(s32[512]{0:T(512)S(1)} %bitcast.123, bf16[64,8,2,128]{3,2,1,0:T(2,128)(2,1)S(1)} %bitcast.116, bf16[]{:T(256)} %constant.28.clone.1), kind=kCustom, calls=%fused_computation.39 | custom fusion | bytes 786434 | tf_op jit(solution)/shard_map/scatter | solution.py:83
  15.2 0.7 all-to-all-done
  15.9 6.1 %all-to-all-start.1 = ((bf16[16,64,1,256]{3,1,2,0:T(8,128)(2,1)}), bf16[16,64,1,256]{3,1,2,0:T(8,128)(2,1)S(1)}, u32[]{:S(2)}, u32[]{:S(2)}) async-start(bf16[16,64,1,256]{3,1,2,0:T(8,128)(2,1)} %bitcast.5), calls=%async_computation.1 | async-start | bytes 1048576 | tf_op jit(solution)/shard_map/all_to_all | solution.py:97
  22.0 4.8 %scatter_custom_fusion.4 = bf16[1024,1024]{1,0:T(8,128)(2,1)} fusion(s32[512]{0:T(512)S(1)} %bitcast.124, bf16[512,1024]{1,0:T(8,128)(2,1)} %param.6, bf16[]{:T(256)} %constant.28.clone.1), kind=kCustom, calls=%fused_computation.35 | custom fusion | bytes 2097664 | tf_op jit(solution)/shard_map/scatter | solution.py:79
  26.8 8.8 %all-to-all-done.1 = bf16[16,64,1,256]{3,1,2,0:T(8,128)(2,1)S(1)} async-done(((bf16[16,64,1,256]{3,1,2,0:T(8,128)(2,1)}), bf16[16,64,1,256]{3,1,2,0:T(8,128)(2,1)S(1)}, u32[]{:S(2)}, u32[]{:S(2)}) %all-to-all-start.1) | async-done | bytes 524320 | tf_op jit(solution)/shard_map/all_to_all | solution.py:97
  35.6 4.9 %all-to-all-start.2 = ((bf16[16,64,1,1024]{3,1,2,0:T(8,128)(2,1)}), bf16[16,64,1,1024]{3,1,2,0:T(8,128)(2,1)S(1)}, u32[]{:S(2)}, u32[]{:S(2)}) async-start(bf16[16,64,1,1024]{3,1,2,0:T(8,128)(2,1)} %bitcast.9), calls=%async_computation.2 | async-start | bytes 4194304 | tf_op jit(solution)/shard_map/all_to_all | solution.py:96
  40.5 0.5 broadcast.170
  41.1 0.6 reduce.10
  41.7 0.1 reshape.267
  41.8 0.1 reshape_squeeze.6
  41.9 0.1 reshape.186
  42.0 4.3 %scatter_custom_fusion.1 = s32[512]{0:T(512)S(1)} fusion(s32[1024]{0:T(1024)S(1)} %bitcast.125, s32[1024]{0:T(1024)S(1)} %reshape.186, s32[]{:T(128)} %constant.15.clone.1), kind=kCustom, calls=%fused_computation.53 | custom fusion | bytes 2052 | tf_op jit(solution)/shard_map/scatter | solution.py:113
  46.3 3.4 %all-gather.1 = s32[2,1,512]{2,1,0:T(1,128)S(1)} all-gather(s32[1,1,512]{2,1,0:T(1,128)S(1)} %bitcast.118), channel_id=1, replica_groups=mesh['dp'=16,'ctx'=2] {'ctx'}, dimensions={0}, use_global_device_ids=true | all-gather | bytes 6144 | tf_op jit(solution)/shard_map/all_gather | solution.py:54
  49.7 5.0 %scatter_custom_fusion.3 = bf16[512,256]{1,0:T(8,128)(2,1)S(1)} fusion(s32[1024]{0:T(1024)S(1)} %bitcast.126, bf16[1024,256]{1,0:T(8,128)(2,1)S(1)} %bitcast.115, bf16[]{:T(256)} %constant.28.clone.1), kind=kCustom, calls=%fused_computation.43 | custom fusion | bytes 262146 | tf_op jit(solution)/shard_map/scatter | solution.py:111
  54.7 7.4 %all-gather = bf16[1024,256]{1,0:T(8,128)(2,1)S(1)} all-gather(bf16[512,256]{1,0:T(8,128)(2,1)S(1)} %scatter_custom_fusion.3), channel_id=2, replica_groups=mesh['dp'=16,'ctx'=2] {'ctx'}, dimensions={0}, use_global_device_ids=true | all-gather | bytes 786432 | tf_op jit(solution)/shard_map/all_gather | solution.py:53
  62.0 25.9 %all-to-all-done.2 = bf16[16,64,1,1024]{3,1,2,0:T(8,128)(2,1)S(1)} async-done(((bf16[16,64,1,1024]{3,1,2,0:T(8,128)(2,1)}), bf16[16,64,1,1024]{3,1,2,0:T(8,128)(2,1)S(1)}, u32[]{:S(2)}, u32[]{:S(2)}) %all-to-all-start.2) | async-done | bytes 2097184 | tf_op jit(solution)/shard_map/all_to_all | solution.py:96
  87.9 1.3 %copy-done.1 = bf16[16,64,1,1024]{3,1,2,0:T(8,128)(2,1)} copy-done((bf16[16,64,1,1024]{3,1,2,0:T(8,128)(2,1)}, bf16[16,64,1,1024]{3,1,2,0:T(8,128)(2,1)S(1)}, u32[]{:S(2)}) %copy-start.1) | copy-done | bytes 2097176
  89.3 6.2 %scatter_custom_fusion.5 = bf16[512,1024]{1,0:T(8,128)(2,1)S(1)} fusion(s32[1024]{0:T(1024)S(1)} %bitcast.127, bf16[1024,1024]{1,0:T(8,128)(2,1)} %bitcast.113, bf16[]{:T(256)} %constant.28.clone.1), kind=kCustom, calls=%fused_computation.37 | custom fusion | bytes 1049088 | tf_op jit(solution)/shard_map/scatter | solution.py:106
  95.4 0.5 copy.27
  96.0 0.7 copy.28
  96.7 32.6 %while.15 = (s32[]{:T(128)}, f32[512,1,8]{0,2,1:T(8,128)S(1)}, f32[512,1,8]{0,2,1:T(8,128)S(1)}, f32[512,1,8,128]{0,3,2,1:T(8,128)}, s32[512]{0:T(512)S(1)}, /*i...) while((s32[]{:T(128)}, f32[512,1,8]{0,2,1:T(8,128)S(1)}, ...), condition=%wide.region_9.10_spmd.clone, body=%wide.region_6.9_spmd.clone.sunk | while | flops 1103389696 | bytes 66076856 | solution.py:64
  96.7 0.7 dynamic_slice.22
  97.3 0.7 iota_add_fusion.3
  98.0 0.3 compare_and_fusion.2
  98.4 4.7 %fusion.36 = (f32[512,8]{0,1:T(8,128)S(1)}, f32[512,512,8]{1,0,2:T(8,128)}) fusion(pred[512,512]{0,1:T(8,128)(4,1)S(1)} %compare_and_fusion.2, bf16[512,1,8,128]{3,0,2,1:T(8,128)(2,1)S(1)} %get-tuple-element.261, bf16[512,1,256]{2,0,1:T(8,128)(2,1)S(1)} %dynamic-slice_bitcast_fusion.2), kind=kOutput, calls=%fused_computation.9.clone.1 | convolution fusion | flops 543158272 | bytes 9846784 | tf_op jit(solution)/shard_map/while/body/eval_jaxpr/tgqd,kgd->tgqk/dot_general | solution.py:27
  103.1 0.0 copy-start
  103.1 7.5 %bitcast_add_fusion.5 = f32[512,1,8,128]{0,3,2,1:T(8,128)} fusion(f32[512,1,8,128]{0,3,2,1:T(8,128)} %get-tuple-element.244, f32[512,512,8]{1,0,2:T(8,128)} %get-tuple-element.227, f32[512,8]{0,1:T(8,128)S(1)} %bitcast.108, pred[512,512]{0,1:T(8,128)(4,1)S(1)} %compare_and_fusion.2, f32[512,8]{0,1:T(8,128)S(1)} %get-tuple-element.228, ...), kind=kOutput, calls=%fused_computation.15.clone.1 | convolution fusion | flops 548929536 | bytes 13008897 | tf_op jit(solution)/shard_map/while/body/eval_jaxpr/tgqk,kgd->tgqd/dot_general | solution.py:40
  110.6 0.0 copy-done
  110.6 2.0 %fusion.38 = f32[512,8]{0,1:T(8,128)S(1)} fusion(f32[512,512,8]{1,0,2:T(8,128)S(1)} %copy-done, f32[512,8]{0,1:T(8,128)S(1)} %bitcast.109, pred[512,512]{0,1:T(8,128)(4,1)S(1)} %compare_and_fusion.2), kind=kLoop, calls=%fused_computation.11.clone.1 | loop fusion | flops 10481664 | bytes 8683520 | tf_op jit(solution)/shard_map/while/body/eval_jaxpr/reduce_sum | solution.py:39
  112.7 0.7 dynamic_slice.22
  113.4 0.7 iota_add_fusion.3
  114.1 0.3 compare_and_fusion.2
  114.4 4.7 %fusion.36 = (f32[512,8]{0,1:T(8,128)S(1)}, f32[512,512,8]{1,0,2:T(8,128)}) fusion(pred[512,512]{0,1:T(8,128)(4,1)S(1)} %compare_and_fusion.2, bf16[512,1,8,128]{3,0,2,1:T(8,128)(2,1)S(1)} %get-tuple-element.261, bf16[512,1,256]{2,0,1:T(8,128)(2,1)S(1)} %dynamic-slice_bitcast_fusion.2), kind=kOutput, calls=%fused_computation.9.clone.1 | convolution fusion | flops 543158272 | bytes 9846784 | tf_op jit(solution)/shard_map/while/body/eval_jaxpr/tgqd,kgd->tgqk/dot_general | solution.py:27
  119.1 0.0 copy-start
  119.1 8.1 %bitcast_add_fusion.5 = f32[512,1,8,128]{0,3,2,1:T(8,128)} fusion(f32[512,1,8,128]{0,3,2,1:T(8,128)} %get-tuple-element.244, f32[512,512,8]{1,0,2:T(8,128)} %get-tuple-element.227, f32[512,8]{0,1:T(8,128)S(1)} %bitcast.108, pred[512,512]{0,1:T(8,128)(4,1)S(1)} %compare_and_fusion.2, f32[512,8]{0,1:T(8,128)S(1)} %get-tuple-element.228, ...), kind=kOutput, calls=%fused_computation.15.clone.1 | convolution fusion | flops 548929536 | bytes 13008897 | tf_op jit(solution)/shard_map/while/body/eval_jaxpr/tgqk,kgd->tgqd/dot_general | solution.py:40
  127.2 0.0 copy-done
  127.2 2.0 %fusion.38 = f32[512,8]{0,1:T(8,128)S(1)} fusion(f32[512,512,8]{1,0,2:T(8,128)S(1)} %copy-done, f32[512,8]{0,1:T(8,128)S(1)} %bitcast.109, pred[512,512]{0,1:T(8,128)(4,1)S(1)} %compare_and_fusion.2), kind=kLoop, calls=%fused_computation.11.clone.1 | loop fusion | flops 10481664 | bytes 8683520 | tf_op jit(solution)/shard_map/while/body/eval_jaxpr/reduce_sum | solution.py:39
  129.3 1.9 %divide_convert_fusion = bf16[512,1,8,128]{0,3,2,1:T(8,128)(2,1)S(1)} fusion(f32[512,1,8,128]{0,3,2,1:T(8,128)} %get-tuple-element.58, f32[512,8]{0,1:T(8,128)S(1)} %bitcast.114), kind=kLoop, calls=%fused_computation.34 | loop fusion | flops 1048576 | bytes 3162112 | tf_op jit(solution)/shard_map/convert_element_type | solution.py:67
  131.2 1.3 copy.32
  (19 shorter events, 0.2 us)
Async XLA Ops:
  0.0 12.1 %copy-start.2 = (bf16[512,1,2,128]{3,2,1,0:T(2,128)(2,1)S(1)}, bf16[512,1,2,128]{3,2,1,0:T(2,128)(2,1)}, u32[]{:S(2)}) copy-start(bf16[512,1,2,128]{3,2,1,0:T(2,128)(2,1)} %param.7) | copy-start | bytes 786436
  5.5 10.4 %all-to-all-start = ((s32[16,1,128]{2,1,0:T(1,128)}), s32[16,1,128]{2,1,0:T(1,128)S(1)}, u32[]{:S(2)}, u32[]{:S(2)}) async-start(s32[16,1,128]{2,1,0:T(1,128)} %reshape.266), calls=%async_computation | async-start | bytes 16384 | tf_op jit(solution)/shard_map/all_to_all | solution.py:98
  15.9 19.7 %all-to-all-start.1 = ((bf16[16,64,1,256]{3,1,2,0:T(8,128)(2,1)}), bf16[16,64,1,256]{3,1,2,0:T(8,128)(2,1)S(1)}, u32[]{:S(2)}, u32[]{:S(2)}) async-start(bf16[16,64,1,256]{3,1,2,0:T(8,128)(2,1)} %bitcast.5), calls=%async_computation.1 | async-start | bytes 1048576 | tf_op jit(solution)/shard_map/all_to_all | solution.py:97
  35.6 52.3 %all-to-all-start.2 = ((bf16[16,64,1,1024]{3,1,2,0:T(8,128)(2,1)}), bf16[16,64,1,1024]{3,1,2,0:T(8,128)(2,1)S(1)}, u32[]{:S(2)}, u32[]{:S(2)}) async-start(bf16[16,64,1,1024]{3,1,2,0:T(8,128)(2,1)} %bitcast.9), calls=%async_computation.2 | async-start | bytes 4194304 | tf_op jit(solution)/shard_map/all_to_all | solution.py:96
  87.9 1.4 %copy-start.1 = (bf16[16,64,1,1024]{3,1,2,0:T(8,128)(2,1)}, bf16[16,64,1,1024]{3,1,2,0:T(8,128)(2,1)S(1)}, u32[]{:S(2)}) copy-start(bf16[16,64,1,1024]{3,1,2,0:T(8,128)(2,1)S(1)} %all-to-all-done.2) | copy-start | bytes 6291460
  103.1 7.5 %copy-start = (f32[512,512,8]{1,0,2:T(8,128)S(1)}, f32[512,512,8]{1,0,2:T(8,128)}, u32[]{:S(2)}) copy-start(f32[512,512,8]{1,0,2:T(8,128)} %get-tuple-element.227) | copy-start | bytes 25165828 | tf_op jit(solution)/shard_map/while
  119.1 8.1 %copy-start = (f32[512,512,8]{1,0,2:T(8,128)S(1)}, f32[512,512,8]{1,0,2:T(8,128)}, u32[]{:S(2)}) copy-start(f32[512,512,8]{1,0,2:T(8,128)} %get-tuple-element.227) | copy-start | bytes 25165828 | tf_op jit(solution)/shard_map/while
where the time goes:
time: 133 us
  waiting for transfers between devices  35.3 us (27%)
  local copies, waits for them, and re-layouts  33.5 us (25%)
  matrix products  25.1 us (19%)
  starting transfers between devices  17.6 us (13%)
  blocking collectives  10.8 us (8%)
  other arithmetic  9.99 us (8%)
    all_to_all x1, waiting for transfers between devices, local(): lax.all_to_all(parcel_q, 'dp', split_axis=0, concat_axis=0, tiled=True)  25.9 us
    dot_general x2, matrix products, update(): jnp.einsum('tgqk,kgd->tgqd', weights.astype(jnp.bfloat16), block_kv[:, :,...  15.6 us
    dot_general x2, matrix products, update(): jnp.einsum('tgqd,kgd->tgqk', query_heads, block_kv[:, :, :head_dim], pref...  9.41 us
    all_to_all x1, waiting for transfers between devices, local(): lax.all_to_all(parcel_kv, 'dp', split_axis=0, concat_axis=0, tiled=True)  8.79 us
    all_gather x1, blocking collectives, attend_rows(): block_kv = lax.all_gather(local_kv, 'ctx', axis=0, tiled=True)  7.36 us
    scatter x2, local copies, waits for them, and re-layouts, local(): local_q = jnp.zeros((rows_dev, groups, group_width), jnp.bfloat16).at[tar...  6.7 us
    all_to_all x1, starting transfers between devices, local(): lax.all_to_all(parcel_labels, 'dp', split_axis=0, concat_axis=0, tiled=True)  6.55 us
    all_to_all x1, starting transfers between devices, local(): lax.all_to_all(parcel_kv, 'dp', split_axis=0, concat_axis=0, tiled=True)  6.1 us
  transfers between devices with their start and end apart: 3, of which 3 were waited for; matrix products, arithmetic and copies ran while one was open for 14% of the time, Pallas kernels for 0%

commit v1 on v0

v1 whole, which is shorter than its diff:
```python
import functools
import math

import jax
import jax.numpy as jnp
from jax import lax
from jax.experimental import pallas as pl
from jax.experimental.pallas import tpu as pltpu
from jax.sharding import PartitionSpec as P

LANES = 128
LABEL_ROWS = 16
DIGIT = 64
TOGETHER = 4
APART = 16384.0
NEVER = -1e30
ANY = pl.BlockSpec(memory_space=pl.ANY)
VMEM = pl.BlockSpec(memory_space=pltpu.VMEM)
SMEM = pl.BlockSpec(memory_space=pltpu.SMEM)


def params(mib):
    return pltpu.CompilerParams(vmem_limit_bytes=mib * 1024 * 1024)


def hbm(*arrays):
    return [pltpu.with_memory_space_constraint(array, pltpu.HBM) for array in arrays]


def pack_kv(routing, documents, kv, owners, seq_len):
    rows = kv.shape[0] // 2
    cap = 2 * rows // owners
    blocks = rows // cap
    per_group = LANES // cap

    def kernel(routing_any, doc_any, kv_any, out_ref, routing_ref, doc_ref, kv_ref, label_ref, held_ref, in_sem, sem, label_sem):
        fetches = [
            pltpu.make_async_copy(source, target, in_sem.at[index])
            for index, (source, target) in enumerate(
                ((routing_any, routing_ref), (doc_any, doc_ref), (kv_any, kv_ref))
            )
        ]
        for fetch in fetches:
            fetch.start()
        fetches[0].wait()
        for slot in range(owners):
            held_ref[slot] = blocks
        for block in range(blocks):
            held_ref[routing_ref[0, block * cap]] = block
        fetches[1].wait()
        row_at = lax.broadcasted_iota(jnp.int32, (LABEL_ROWS, LANES), 0)
        label_ref[blocks] = jnp.full((LABEL_ROWS, LANES), 255.0, jnp.bfloat16)
        for block in range(blocks):
            group, part = divmod(block, per_group)
            begin = doc_ref[group : group + 1, :] - routing_ref[0, block * cap] * seq_len
            place = routing_ref[1, block * cap] // cap
            label = jnp.where(row_at == 0, begin // DIGIT, jnp.where(row_at == 1, begin % DIGIT, part))
            label = jnp.where(row_at == 2, place, label)
            label_ref[block] = label.astype(jnp.float32).astype(jnp.bfloat16)
        copies = [
            pltpu.make_async_copy(
                label_ref.at[held_ref[slot]], out_ref.at[slot, pl.ds(0, LABEL_ROWS)], label_sem.at[slot]
            )
            for slot in range(owners)
        ]
        for block in range(blocks):
            copies.append(
                pltpu.make_async_copy(
                    kv_ref.at[pl.ds(block * 2 * cap, 2 * cap)],
                    out_ref.at[routing_ref[0, block * cap], pl.ds(LABEL_ROWS, 2 * cap)],
                    sem.at[block],
                )
            )
        fetches[2].wait()
        for copy in copies:
            copy.start()
        for copy in copies:
            copy.wait()

    return pl.pallas_call(
        kernel,
        out_shape=pltpu.HBM((owners, LABEL_ROWS + 2 * cap, LANES), kv.dtype),
        in_specs=[ANY] * 3,
        out_specs=ANY,
        scratch_shapes=[
            pltpu.SMEM(routing.shape, jnp.int32),
            pltpu.VMEM(documents.shape, jnp.int32),
            pltpu.VMEM(kv.shape, kv.dtype),
            pltpu.VMEM((blocks + 1, LABEL_ROWS, LANES), jnp.bfloat16),
            pltpu.SMEM((owners,), jnp.int32),
            pltpu.SemaphoreType.DMA((3,)),
            pltpu.SemaphoreType.DMA((blocks,)),
            pltpu.SemaphoreType.DMA((owners,)),
        ],
        compiler_params=params(16),
        name="pack_kv",
    )(*hbm(routing, documents, kv))


def pack_q(routing, queries, earlier, owners):
    rows, width = queries.shape
    cap = 2 * rows // owners
    blocks = rows // cap
    half = owners // 2

    def kernel(routing_any, q_any, earlier_ref, near_ref, *rest):
        far_refs = rest[:half]
        routing_ref, q_ref, held_ref, in_sem, q_sem, sem = rest[half:]
        me = lax.axis_index("dp")
        fetch = pltpu.make_async_copy(routing_any, routing_ref, in_sem)
        fetch.start()
        fetch_q = pltpu.make_async_copy(q_any, q_ref, q_sem)
        fetch_q.start()
        fetch.wait()
        for slot in range(owners):
            held_ref[slot] = blocks
        for block in range(blocks):
            held_ref[routing_ref[0, block * cap]] = block
        copies = []
        for step in range(owners):
            slot = me ^ step
            block = held_ref[slot]
            q_rows = pl.ds(pl.multiple_of(jnp.minimum(block, blocks - 1) * cap, cap), cap)
            target = far_refs[step - half] if step >= half else near_ref.at[lax.rem(slot, half)]
            copies.append((block < blocks, pltpu.make_async_copy(q_ref.at[q_rows], target, sem.at[step])))
        fetch_q.wait()
        for held, copy in copies:
            pl.when(held)(copy.start)
        for held, copy in copies:
            pl.when(held)(copy.wait)

    return pl.pallas_call(
        kernel,
        out_shape=[
            pltpu.HBM((half, cap, width), queries.dtype),
            *[jax.ShapeDtypeStruct((cap, width), queries.dtype)] * half,
        ],
        in_specs=[ANY] * 3,
        out_specs=[ANY] * (1 + half),
        scratch_shapes=[
            pltpu.SMEM(routing.shape, jnp.int32),
            pltpu.VMEM(queries.shape, queries.dtype),
            pltpu.SMEM((owners,), jnp.int32),
            pltpu.SemaphoreType.DMA,
            pltpu.SemaphoreType.DMA,
            pltpu.SemaphoreType.DMA((owners,)),
        ],
        compiler_params=params(16),
        name="pack_q",
    )(*hbm(routing, queries, earlier))


def place_kv(source, parcels, begins, rows, cap):
    blocks = rows // cap

    def kernel(source_ref, in_ref, begin_ref, out_ref, sem):
        copies = [
            pltpu.make_async_copy(
                in_ref.at[source_ref[place], pl.ds(LABEL_ROWS, 2 * cap)],
                out_ref.at[pl.ds(place * 2 * cap, 2 * cap)],
                sem.at[place],
            )
            for place in range(blocks)
        ]
        copies.append(
            pltpu.make_async_copy(begin_ref, out_ref.at[pl.ds(2 * rows, begin_ref.shape[0])], sem.at[blocks])
        )
        for copy in copies:
            copy.start()
        for copy in copies:
            copy.wait()

    return pl.pallas_call(
        kernel,
        out_shape=jax.ShapeDtypeStruct((2 * rows + begins.shape[0], LANES), parcels.dtype),
        in_specs=[SMEM, ANY, ANY],
        out_specs=ANY,
        scratch_shapes=[pltpu.SemaphoreType.DMA((blocks + 1,))],
        compiler_params=params(16),
        name="place_kv",
    )(source, parcels, begins)


def attend(meta, first, near, far, own, past, out):
    rows = own[0].shape[0]
    cap, width = far[0].shape
    blocks = rows // cap
    heads = width // LANES
    half = rows // 2
    count = past[0].shape[0]
    slots = 0 if near is None else near.shape[0]
    parcels = slots + len(far)
    factor = math.log2(math.e) / math.sqrt(LANES)
    arrays = ([] if near is None else [near]) + far

    def kernel(meta_ref, qd_ref, ok_ref, od_ref, ov_ref, pk_ref, pd_ref, pv_ref, *rest):
        array_refs = rest[: len(arrays)]
        out_any, stage_ref, result_ref, sem = rest[-4:]

        def keys(k_ref, d_ref):
            return jnp.concatenate([k_ref, d_ref], axis=1)

        def values(v):
            return jnp.concatenate([v, jnp.ones(v.shape, v.dtype)], axis=1)

        def scores(tile_q, tile_k):
            return lax.dot_general(tile_q, tile_k, (((1,), (1,)), ((), ())), preferred_element_type=jnp.float32)

        def top(raw):
            return jnp.max(raw, axis=-1, keepdims=True)

        def mix(raw, peak, tile_v):
            weights = jnp.exp2((raw - peak) * factor).astype(jnp.bfloat16)
            return jnp.dot(weights, tile_v, preferred_element_type=jnp.float32)

        def place_of(index):
            return meta_ref[1 + first + index]

        def result_copy(index):
            at = pl.multiple_of(jnp.minimum(place_of(index), blocks - 1) * cap, cap)
            return pltpu.make_async_copy(result_ref.at[index], out_any.at[pl.ds(at, cap)], sem.at[index])

        def one_block(index, place, lower, with_past):
            block_q = stage_ref[index]
            same = qd_ref[pl.ds(pl.multiple_of(place * cap, cap), cap), :]
            same = jnp.concatenate([same] * TOGETHER, axis=0)
            row_at = lax.broadcasted_iota(jnp.int32, (cap, half), 0) + (place * cap - lower * half)
            seen = lax.broadcasted_iota(jnp.int32, (cap, half), 1) <= row_at
            last = pl.ds(lower * half, half)

            def causal(raw):
                return jnp.where(seen[None], raw.reshape(TOGETHER, cap, half), NEVER).reshape(TOGETHER * cap, half)

            tile_qs = []
            for begin in range(0, heads, TOGETHER):
                tiles = [block_q[:, head * LANES : (head + 1) * LANES] for head in range(begin, begin + TOGETHER)]
                tile_qs.append(jnp.concatenate([jnp.concatenate(tiles, axis=0), same], axis=1))
            raws = [[causal(scores(tile_q, keys(ok_ref[last], od_ref[last])))] for tile_q in tile_qs]
            tile_vs = [ov_ref[last]]
            if lower:
                for several, tile_q in zip(raws, tile_qs):
                    several.append(scores(tile_q, keys(ok_ref[:half], od_ref[:half])))
                tile_vs.append(ov_ref[:half])
            if with_past:
                for several, tile_q in zip(raws, tile_qs):
                    several.append(scores(tile_q, keys(pk_ref[0], pd_ref[0])))
                tile_vs.append(pv_ref[0])
            peaks = [functools.reduce(jnp.maximum, [top(raw) for raw in several]) for several in raws]
            mixes = [
                sum(mix(raw, peak, values(tile_v)) for raw, tile_v in zip(several, tile_vs))
                for several, peak in zip(raws, peaks)
            ]
            if count > 1:

                def step(earlier, state):
                    result = []
                    for (peak, mixed), tile_q in zip(state, tile_qs):
                        raw = scores(tile_q, keys(pk_ref[earlier], pd_ref[earlier]))
                        higher = jnp.maximum(peak, top(raw))
                        decay = jnp.exp2((peak - higher) * factor)
                        result.append((higher, mixed * decay + mix(raw, higher, values(pv_ref[earlier]))))
                    return result

                mixes = [mixed for _, mixed in lax.fori_loop(0, meta_ref[0], step, list(zip(peaks, mixes)))]
            for at, mixed in enumerate(mixes):
                result = (mixed[:, :LANES] / mixed[:, LANES:]).astype(jnp.bfloat16)
                for head in range(TOGETHER):
                    column = (at * TOGETHER + head) * LANES
                    result_ref[index, :, column : column + LANES] = result[head * cap : (head + 1) * cap]

        def body(index, carry):
            place = place_of(index)
            for lower in (0, 1):
                here = (place < blocks) & (place >= blocks // 2) if lower else place < blocks // 2
                if count > 1:
                    pl.when(here)(functools.partial(one_block, index, place, lower, False))
                else:
                    for column in (0, 1):
                        pl.when(here & (meta_ref[0] == column))(
                            functools.partial(one_block, index, place, lower, column == 1)
                        )
            pl.when(place < blocks)(result_copy(index).start)
            return carry

        for index in range(parcels):

            @pl.when(place_of(index) < blocks)
            def _():
                stage_ref[index] = array_refs[0][index] if index < slots else array_refs[index - slots + (slots > 0)][...]

        lax.fori_loop(0, parcels, body, 0)
        for index in range(parcels):
            pl.when(place_of(index) < blocks)(result_copy(index).wait)

    operands = [meta, *own, *past, *arrays]
    specs = [SMEM] + [VMEM] * (len(operands) - 1)
    aliases = {}
    if out is not None:
        aliases = {len(operands): 0}
        operands.append(out)
        specs.append(ANY)
    area = max(1, parcels // 2) * heads * cap * (count + 1) * rows
    return pl.pallas_call(
        kernel,
        out_shape=jax.ShapeDtypeStruct((rows, width), jnp.bfloat16),
        in_specs=specs,
        out_specs=ANY,
        input_output_aliases=aliases,
        scratch_shapes=[
            pltpu.VMEM((parcels, cap, width), jnp.bfloat16),
            pltpu.VMEM((parcels, cap, width), jnp.bfloat16),
            pltpu.SemaphoreType.DMA((parcels,)),
        ],
        compiler_params=params(28),
        cost_estimate=pl.CostEstimate(
            flops=8 * area * LANES, bytes_accessed=4 * parcels * cap * width, transcendentals=area
        ),
        name="attend",
    )(*operands)


def digits(begin):
    lane = jnp.arange(LANES, dtype=jnp.int32)
    digit = jnp.where(lane < DIGIT, begin[..., None] // DIGIT, begin[..., None] % DIGIT)
    hit = digit == lane % DIGIT
    return jnp.where(hit, 1.0, 0.0).astype(jnp.bfloat16), jnp.where(hit, 0.0, -APART).astype(jnp.bfloat16)


def local(queries, keys_values, routing, documents):
    rows, width = queries.shape
    owners = lax.axis_size("dp")
    columns = lax.axis_size("ctx")
    kv_heads, pair, head_dim = keys_values.shape[1:]
    assert kv_heads == 1 and pair == 2 and head_dim == LANES
    cap = 2 * rows // owners
    blocks = rows // cap
    seq_len = rows * columns
    assert seq_len <= DIGIT * DIGIT
    half = owners // 2
    assert owners & (owners - 1) == 0
    column = lax.axis_index("ctx")
    me = lax.axis_index("dp")

    routing = routing.T
    send_kv = pack_kv(routing, documents.reshape(-1, LANES), keys_values.reshape(2 * rows, LANES), owners, seq_len)
    parcels = lax.all_to_all(send_kv, "dp", split_axis=0, concat_axis=0, tiled=True)
    near, *far = pack_q(routing, queries, send_kv, owners)
    groups = [list(range(half)), list(range(half, owners))]
    near = lax.all_to_all(near, "dp", split_axis=0, concat_axis=0, axis_index_groups=groups, tiled=True)
    label = parcels[:, :4].astype(jnp.float32).astype(jnp.int32)
    place, part = label[:, 2, 0], label[:, 3, 0]
    begin = (label[:, 0] * DIGIT + label[:, 1]).reshape(owners, LANES // cap, cap)
    slots = jnp.arange(blocks, dtype=jnp.int32)
    every = jnp.arange(owners, dtype=jnp.int32)
    chosen = place[None, :] == slots[:, None]
    source = jnp.sum(jnp.where(chosen, every[None, :], 0), axis=1)
    senders = jnp.concatenate([me // half * half + every[:half], me ^ every[half:]])
    places = jnp.sum(jnp.where(senders[:, None] == every[None, :], place[None, :], 0), axis=1)
    wanted = chosen[:, :, None] & (part[None, :, None] == jnp.arange(LANES // cap, dtype=jnp.int32))
    doc = jnp.sum(jnp.where(wanted[..., None], begin[None], 0), axis=(1, 2)).reshape(rows)

    split = jnp.concatenate([doc // DIGIT, doc % DIGIT]).astype(jnp.float32).astype(jnp.bfloat16).reshape(-1, LANES)
    split = jnp.pad(split, ((0, -split.shape[0] % LABEL_ROWS), (0, 0)))
    own_kv = place_kv(source, parcels, split, rows, cap)
    past_kv = lax.ppermute(own_kv, "ctx", [(0, 1)])[None] if columns == 2 else lax.all_gather(own_kv, "ctx")
    same, apart = digits(doc)
    own = (same, own_kv[: 2 * rows].reshape(rows, 2, LANES)[:, 0], apart, own_kv[: 2 * rows].reshape(rows, 2, LANES)[:, 1])
    past_doc = past_kv[:, 2 * rows :][:, : 2 * rows // LANES].reshape(-1, 2, rows).astype(jnp.float32).astype(jnp.int32)
    past_apart = digits(past_doc[:, 0] * DIGIT + past_doc[:, 1])[1]
    past_rows = past_kv[:, : 2 * rows].reshape(-1, rows, 2, LANES)
    past = (past_rows[:, :, 0], past_apart, past_rows[:, :, 1])

    ties = [None] * 3 + [parcels] * (half - 6) + [own_kv] * 2 + [past_kv]
    for index, tie in enumerate(ties):
        parcel = far[index] if tie is None else lax.optimization_barrier((far[index], tie))[0]
        far[index] = lax.ppermute(parcel, "dp", [(owner, owner ^ (half + index)) for owner in range(owners)])

    meta = jnp.concatenate([column[None], places])
    cuts = [0, half - 6, half - 3, half - 1, half]
    out = None
    for begin, end in zip(cuts[:-1], cuts[1:]):
        out = attend(
            meta, half + begin if begin else 0, None if begin else near, far[begin:end], own, past, out
        )
    return out


def solution(mesh):
    placed = (
        P(("dp", "ctx"), None),
        P(("dp", "ctx"), None, None, None),
        P(("dp", "ctx"), None),
        P(("dp", "ctx")),
    )
    return jax.shard_map(
        local, mesh=mesh, in_specs=placed, out_specs=P(("dp", "ctx"), None), check_vma=False
    )
```

time: 133 us -> 79.6 us (0.60)
  the two profiles are of different devices: /device:TPU:11 before, /device:TPU:5 now
where the time goes in v1:
time: 79.6 us; the launch traced here: 79.3 us
  starting transfers between devices  31.6 us (40%)
  waiting for transfers between devices  26.5 us (33%)
  Pallas kernels  18 us (23%)
  local copies, waits for them, and re-layouts  1.77 us (2%)
  other arithmetic  1.17 us (1%)
    ppermute x8, starting transfers between devices, local(): lax.ppermute(parcel, 'dp', [(owner, owner ^ half + index) for owner in ra...  19.5 us
    all_to_all x1, waiting for transfers between devices, local(): lax.all_to_all(send_kv, 'dp', split_axis=0, concat_axis=0, tiled=True)  14.7 us
    pallas_call x4, Pallas kernels, attend(): pl.pallas_call(kernel, out_shape=jax.ShapeDtypeStruct((rows, width), jnp....  12.8 us
    ppermute x8, waiting for transfers between devices, local(): lax.ppermute(parcel, 'dp', [(owner, owner ^ half + index) for owner in ra...  7.64 us
    all_to_all x1, starting transfers between devices, local(): lax.all_to_all(send_kv, 'dp', split_axis=0, concat_axis=0, tiled=True)  6.5 us
    all_to_all x1, starting transfers between devices, local(): lax.all_to_all(near, 'dp', split_axis=0, concat_axis=0, axis_index_groups...  4.32 us
    ppermute x1, waiting for transfers between devices, local(): lax.ppermute(own_kv, 'ctx', [(0, 1)])[None]  4.15 us
    pallas_call x1, Pallas kernels, pack_q(): pl.pallas_call(kernel, out_shape=[pltpu.HBM((half, cap, width), queries.d...  2.25 us
  transfers between devices with their start and end apart: 11, of which 3 were waited for; matrix products, arithmetic and copies ran while one was open for 4% of the time, Pallas kernels for 17%

profile of v1, /device:TPU:5, one launch (start us, length us, event | category | flops | bytes accessed | tf_op | source)
XLA Modules:
  0.0 79.3 jit_solution(2213548171858544635)
XLA Ops:
  0.0 2.0 %pack_kv.1.earlier_ref = bf16[16,144,128]{2,1,0:T(8,128)(2,1)} custom-call(s32[2,512]{1,0:T(2,128)} %bitcast.21, s32[4,128]{1,0:T(4,128)} %bitcast.24, bf16[1024,128]{1,0:T(8,128)(2,1)} %bitcast.20), custom_call_target="tpu_custom_call" | custom-call | tf_op jit(solution)/shard_map/pack_kv/pallas_call | solution.py:80
  2.0 6.5 %all-to-all-start = ((bf16[16,144,128]{2,1,0:T(8,128)(2,1)}), bf16[16,144,128]{2,1,0:T(8,128)(2,1)S(1)}, u32[]{:S(2)}, u32[]{:S(2)}) async-start(bf16[16,144,128]{2,1,0:T(8,128)(2,1)} %pack_kv.1.earlier_ref), calls=%async_computation | async-start | bytes 1179648 | tf_op jit(solution)/shard_map/all_to_all | solution.py:346
  8.5 2.3 %pack_q.1 = (bf16[8,64,1024]{2,1,0:T(8,128)(2,1)}, bf16[64,1024]{1,0:T(8,128)(2,1)S(1)}, bf16[64,1024]{1,0:T(8,128)(2,1)S(1)}, bf16[64,1024]{1,0:T(8,128)(2,1)S(...) custom-call(s32[2,512]{1,0:T(2,128)} %bitcast.22, ...), custom_call_target="tpu_custom_call" | custom-call | tf_op jit(solution)/shard_map/pack_q/pallas_call | solution.py:132
  10.7 3.2 %collective-permute-start.4 = (bf16[64,1024]{1,0:T(8,128)(2,1)S(1)}, bf16[64,1024]{1,0:T(8,128)(2,1)S(1)}, u32[]{:S(2)}, u32[]{:S(2)}) collective-permute-start(bf16[64,1024]{1,0:T(8,128)(2,1)S(1)} %get-tuple-element.25), channel_id=1, source_target_pairs={{0,20},{2,22},{4,16},{6,18},{8,28},{10,30},{12,24},{14,26},{16,4},... | collective-permute-start | bytes 393224 | tf_op jit(solution)/shard_map/ppermute | solution.py:376
  14.0 0.3 collective-permute-start.7
  14.2 2.9 %collective-permute-start.8 = (bf16[64,1024]{1,0:T(8,128)(2,1)S(1)}, bf16[64,1024]{1,0:T(8,128)(2,1)}, u32[]{:S(2)}, u32[]{:S(2)}) collective-permute-start(bf16[64,1024]{1,0:T(8,128)(2,1)S(1)} %get-tuple-element.32), channel_id=1, source_target_pairs={{0,18},{2,16},{4,22},{6,20},{8,26},{10,24},{12,30},{14,28},{16,2},... | collective-permute-start | bytes 393224 | tf_op jit(solution)/shard_map/ppermute | solution.py:376
  17.1 0.1 slice_xor_fusion
  17.2 0.1 pad_add_fusion
  17.3 14.7 %all-to-all-done.in_ref = bf16[16,144,128]{2,1,0:T(8,128)(2,1)S(1)} async-done(((bf16[16,144,128]{2,1,0:T(8,128)(2,1)}), bf16[16,144,128]{2,1,0:T(8,128)(2,1)S(1)}, u32[]{:S(2)}, u32[]{:S(2)}) %all-to-all-start) | async-done | bytes 589856 | tf_op jit(solution)/shard_map/all_to_all | solution.py:346
  32.0 4.3 %all-to-all-start.1 = ((bf16[8,64,1024]{2,1,0:T(8,128)(2,1)}), bf16[8,64,1024]{2,1,0:T(8,128)(2,1)S(1)}, u32[]{:S(2)}, u32[]{:S(2)}) async-start(bf16[8,64,1024]{2,1,0:T(8,128)(2,1)} %get-tuple-element.30), calls=%async_computation.1 | async-start | bytes 2097152 | tf_op jit(solution)/shard_map/all_to_all | solution.py:349
  36.4 0.7 slice_reduce_fusion
  37.1 0.1 select_reduce_fusion.2.source_ref
  37.2 0.1 add.112
  37.3 0.1 select_reduce_fusion
  37.4 0.1 reshape.420
  37.5 0.1 broadcast_in_dim_reshape.2
  37.6 1.0 %place_kv.1 = bf16[1040,128]{1,0:T(8,128)(2,1)S(1)} custom-call(s32[8]{0:T(128)S(1)} %select_reduce_fusion.2.source_ref, bf16[16,144,128]{2,1,0:T(8,128)(2,1)S(1)} %all-to-all-done.in_ref, bf16[16,128]{1,0:T(8,128)(2,1)S(1)} %pad.4.begin_ref), custom_call_target="tpu_custom_call" | custom-call | tf_op jit(solution)/shard_map/place_kv/pallas_call | solution.py:173
  38.7 1.3 %collective-permute-start = (bf16[1040,128]{1,0:T(8,128)(2,1)S(1)}, bf16[1040,128]{1,0:T(8,128)(2,1)S(1)}, u32[]{:S(2)}, u32[]{:S(2)}) collective-permute-start(bf16[1040,128]{1,0:T(8,128)(2,1)S(1)} %place_kv.1), channel_id=1, source_target_pairs={{0,1},{2,3},{4,5},{6,7},{8,9},{10,11},{12,13},{14,15},{16,17},{18,... | collective-permute-start | bytes 798728 | tf_op jit(solution)/shard_map/ppermute | solution.py:365
  40.0 0.4 fusion.6
  40.3 3.6 %collective-permute-start.6 = (bf16[64,1024]{1,0:T(8,128)(2,1)S(1)}, bf16[64,1024]{1,0:T(8,128)(2,1)S(1)}, u32[]{:S(2)}, u32[]{:S(2)}) collective-permute-start(bf16[64,1024]{1,0:T(8,128)(2,1)S(1)} %get-tuple-element.29), channel_id=1, source_target_pairs={{0,24},{2,26},{4,28},{6,30},{8,16},{10,18},{12,20},{14,22},{16,8},... | collective-permute-start | bytes 393224 | tf_op jit(solution)/shard_map/ppermute | solution.py:376
  43.9 0.2 select_convert_fusion.1
  44.1 0.2 select_reduce_fusion.1
  44.3 0.1 pad_add_fusion.1.meta_ref
  44.4 4.1 %collective-permute-done = bf16[1040,128]{1,0:T(8,128)(2,1)S(1)} collective-permute-done((bf16[1040,128]{1,0:T(8,128)(2,1)S(1)}, bf16[1040,128]{1,0:T(8,128)(2,1)S(1)}, u32[]{:S(2)}, u32[]{:S(2)}) %collective-permute-start) | collective-permute-done | bytes 266272 | tf_op jit(solution)/shard_map/ppermute | solution.py:365
  48.6 4.2 %collective-permute-start.5 = (bf16[64,1024]{1,0:T(8,128)(2,1)S(1)}, bf16[64,1024]{1,0:T(8,128)(2,1)S(1)}, u32[]{:S(2)}, u32[]{:S(2)}) collective-permute-start(bf16[64,1024]{1,0:T(8,128)(2,1)S(1)} %get-tuple-element.27), channel_id=1, source_target_pairs={{0,22},{2,20},{4,18},{6,16},{8,30},{10,28},{12,26},{14,24},{16,6},... | collective-permute-start | bytes 393224 | tf_op jit(solution)/shard_map/ppermute | solution.py:376
  52.8 0.4 fusion.5
  53.2 0.2 select_convert_fusion.pd_ref
  53.4 0.0 collective-permute-done.4.rest_0_
  53.5 0.9 %collective-permute-start.3 = (bf16[64,1024]{1,0:T(8,128)(2,1)S(1)}, bf16[64,1024]{1,0:T(8,128)(2,1)S(1)}, u32[]{:S(2)}, u32[]{:S(2)}) collective-permute-start(bf16[64,1024]{1,0:T(8,128)(2,1)S(1)} %get-tuple-element.24), channel_id=1, source_target_pairs={{0,28},{2,30},{4,24},{6,26},{8,20},{10,22},{12,16},{14,18},{16,12}... | collective-permute-start | bytes 393224 | tf_op jit(solution)/shard_map/ppermute | solution.py:376
  54.4 0.0 collective-permute-done.7.rest_1_
  54.4 2.0 %collective-permute-start.2 = (bf16[64,1024]{1,0:T(8,128)(2,1)S(1)}, bf16[64,1024]{1,0:T(8,128)(2,1)S(1)}, u32[]{:S(2)}, u32[]{:S(2)}) collective-permute-start(bf16[64,1024]{1,0:T(8,128)(2,1)S(1)} %get-tuple-element.22), channel_id=1, source_target_pairs={{0,26},{2,24},{4,30},{6,28},{8,18},{10,16},{12,22},{14,20},{16,10}... | collective-permute-start | bytes 393224 | tf_op jit(solution)/shard_map/ppermute | solution.py:376
  56.4 0.0 collective-permute-done.8.rest_2_
  56.4 2.4 %collective-permute-start.1 = (bf16[64,1024]{1,0:T(8,128)(2,1)S(1)}, bf16[64,1024]{1,0:T(8,128)(2,1)S(1)}, u32[]{:S(2)}, u32[]{:S(2)}) collective-permute-start(bf16[64,1024]{1,0:T(8,128)(2,1)S(1)} %get-tuple-element.20), channel_id=1, source_target_pairs={{0,30},{2,28},{4,26},{6,24},{8,22},{10,20},{12,18},{14,16},{16,14}... | collective-permute-start | bytes 393224 | tf_op jit(solution)/shard_map/ppermute | solution.py:376
  58.8 0.0 all-to-all-done.1.rest_0_
  58.9 3.7 %attend.4.rest_3_ = bf16[512,1024]{1,0:T(8,128)(2,1)} custom-call(s32[17]{0:T(128)S(1)} %pad_add_fusion.1.meta_ref, bf16[512,128]{1,0:T(8,128)(2,1)S(1)} %get-tuple-element.40.qd_ref, bf16[512,128]{1,0:T(8,128)(2,1)S(1)} %get-tuple-element.50.ok_ref, bf16[512,128]{1,0:T(8,128)(2,1)S(1)} %get-tuple-element.39.od_ref, ...), custom_call_target="tpu_custom_call" | custom-call | flops 2684354560 | bytes 2621440 | tf_op jit(solution)/shard_map/attend/pallas_call | solution.py:303
  62.5 0.0 collective-permute-done.6.rest_2_
  62.5 7.6 %collective-permute-done.5.rest_1_ = bf16[64,1024]{1,0:T(8,128)(2,1)S(1)} collective-permute-done((bf16[64,1024]{1,0:T(8,128)(2,1)S(1)}, bf16[64,1024]{1,0:T(8,128)(2,1)S(1)}, u32[]{:S(2)}, u32[]{:S(2)}) %collective-permute-start.5) | collective-permute-done | bytes 131104 | tf_op jit(solution)/shard_map/ppermute | solution.py:376
  70.2 3.9 %attend.5.rest_2_ = bf16[512,1024]{1,0:T(8,128)(2,1)} custom-call(s32[17]{0:T(128)S(1)} %pad_add_fusion.1.meta_ref, bf16[512,128]{1,0:T(8,128)(2,1)S(1)} %get-tuple-element.40.qd_ref, bf16[512,128]{1,0:T(8,128)(2,1)S(1)} %get-tuple-element.50.ok_ref, bf16[512,128]{1,0:T(8,128)(2,1)S(1)} %get-tuple-element.39.od_ref, ...), custom_call_target="tpu_custom_call", output_to_operand_aliasing={{}: (11, {})} | custom-call | flops 536870912 | bytes 786432 | tf_op jit(solution)/shard_map/attend/pallas_call | solution.py:303
  74.0 0.0 collective-permute-done.3.rest_1_
  74.1 0.0 collective-permute-done.2.rest_0_
  74.1 3.0 %attend.6.rest_1_ = bf16[512,1024]{1,0:T(8,128)(2,1)} custom-call(s32[17]{0:T(128)S(1)} %pad_add_fusion.1.meta_ref, bf16[512,128]{1,0:T(8,128)(2,1)S(1)} %get-tuple-element.40.qd_ref, bf16[512,128]{1,0:T(8,128)(2,1)S(1)} %get-tuple-element.50.ok_ref, bf16[512,128]{1,0:T(8,128)(2,1)S(1)} %get-tuple-element.39.od_ref, ...), custom_call_target="tpu_custom_call", output_to_operand_aliasing={{}: (10, {})} | custom-call | flops 536870912 | bytes 524288 | tf_op jit(solution)/shard_map/attend/pallas_call | solution.py:303
  77.1 0.0 collective-permute-done.1.rest_0_
  77.1 2.2 %attend.7 = bf16[512,1024]{1,0:T(8,128)(2,1)} custom-call(s32[17]{0:T(128)S(1)} %pad_add_fusion.1.meta_ref, bf16[512,128]{1,0:T(8,128)(2,1)S(1)} %get-tuple-element.40.qd_ref, bf16[512,128]{1,0:T(8,128)(2,1)S(1)} %get-tuple-element.50.ok_ref, bf16[512,128]{1,0:T(8,128)(2,1)S(1)} %get-tuple-element.39.od_ref, ...), custom_call_target="tpu_custom_call", output_to_operand_aliasing={{}: (9, {})} | custom-call | flops 536870912 | bytes 262144 | tf_op jit(solution)/shard_map/attend/pallas_call | solution.py:303
  (22 shorter events, 0.3 us)
Async XLA Ops:
  2.0 30.1 %all-to-all-start = ((bf16[16,144,128]{2,1,0:T(8,128)(2,1)}), bf16[16,144,128]{2,1,0:T(8,128)(2,1)S(1)}, u32[]{:S(2)}, u32[]{:S(2)}) async-start(bf16[16,144,128]{2,1,0:T(8,128)(2,1)} %pack_kv.1.earlier_ref), calls=%async_computation | async-start | bytes 1179648 | tf_op jit(solution)/shard_map/all_to_all | solution.py:346
  10.7 42.7 %collective-permute-start.4 = (bf16[64,1024]{1,0:T(8,128)(2,1)S(1)}, bf16[64,1024]{1,0:T(8,128)(2,1)S(1)}, u32[]{:S(2)}, u32[]{:S(2)}) collective-permute-start(bf16[64,1024]{1,0:T(8,128)(2,1)S(1)} %get-tuple-element.25), channel_id=1, source_target_pairs={{0,20},{2,22},{4,16},{6,18},{8,28},{10,30},{12,24},{14,26},{16,4},... | collective-permute-start | bytes 393224 | tf_op jit(solution)/shard_map/ppermute | solution.py:376
  14.0 40.4 %collective-permute-start.7 = (bf16[64,1024]{1,0:T(8,128)(2,1)S(1)}, bf16[64,1024]{1,0:T(8,128)(2,1)S(1)}, u32[]{:S(2)}, u32[]{:S(2)}) collective-permute-start(bf16[64,1024]{1,0:T(8,128)(2,1)S(1)} %get-tuple-element.31), channel_id=1, source_target_pairs={{0,16},{2,18},{4,20},{6,22},{8,24},{10,26},{12,28},{14,30},{16,0},... | collective-permute-start | bytes 393224 | tf_op jit(solution)/shard_map/ppermute | solution.py:376
  14.2 42.2 %collective-permute-start.8 = (bf16[64,1024]{1,0:T(8,128)(2,1)S(1)}, bf16[64,1024]{1,0:T(8,128)(2,1)}, u32[]{:S(2)}, u32[]{:S(2)}) collective-permute-start(bf16[64,1024]{1,0:T(8,128)(2,1)S(1)} %get-tuple-element.32), channel_id=1, source_target_pairs={{0,18},{2,16},{4,22},{6,20},{8,26},{10,24},{12,30},{14,28},{16,2},... | collective-permute-start | bytes 393224 | tf_op jit(solution)/shard_map/ppermute | solution.py:376
  32.0 26.8 %all-to-all-start.1 = ((bf16[8,64,1024]{2,1,0:T(8,128)(2,1)}), bf16[8,64,1024]{2,1,0:T(8,128)(2,1)S(1)}, u32[]{:S(2)}, u32[]{:S(2)}) async-start(bf16[8,64,1024]{2,1,0:T(8,128)(2,1)} %get-tuple-element.30), calls=%async_computation.1 | async-start | bytes 2097152 | tf_op jit(solution)/shard_map/all_to_all | solution.py:349
  38.7 9.9 %collective-permute-start = (bf16[1040,128]{1,0:T(8,128)(2,1)S(1)}, bf16[1040,128]{1,0:T(8,128)(2,1)S(1)}, u32[]{:S(2)}, u32[]{:S(2)}) collective-permute-start(bf16[1040,128]{1,0:T(8,128)(2,1)S(1)} %place_kv.1), channel_id=1, source_target_pairs={{0,1},{2,3},{4,5},{6,7},{8,9},{10,11},{12,13},{14,15},{16,17},{18,... | collective-permute-start | bytes 798728 | tf_op jit(solution)/shard_map/ppermute | solution.py:365
  40.3 22.2 %collective-permute-start.6 = (bf16[64,1024]{1,0:T(8,128)(2,1)S(1)}, bf16[64,1024]{1,0:T(8,128)(2,1)S(1)}, u32[]{:S(2)}, u32[]{:S(2)}) collective-permute-start(bf16[64,1024]{1,0:T(8,128)(2,1)S(1)} %get-tuple-element.29), channel_id=1, source_target_pairs={{0,24},{2,26},{4,28},{6,30},{8,16},{10,18},{12,20},{14,22},{16,8},... | collective-permute-start | bytes 393224 | tf_op jit(solution)/shard_map/ppermute | solution.py:376
  48.6 21.6 %collective-permute-start.5 = (bf16[64,1024]{1,0:T(8,128)(2,1)S(1)}, bf16[64,1024]{1,0:T(8,128)(2,1)S(1)}, u32[]{:S(2)}, u32[]{:S(2)}) collective-permute-start(bf16[64,1024]{1,0:T(8,128)(2,1)S(1)} %get-tuple-element.27), channel_id=1, source_target_pairs={{0,22},{2,20},{4,18},{6,16},{8,30},{10,28},{12,26},{14,24},{16,6},... | collective-permute-start | bytes 393224 | tf_op jit(solution)/shard_map/ppermute | solution.py:376
  53.5 20.6 %collective-permute-start.3 = (bf16[64,1024]{1,0:T(8,128)(2,1)S(1)}, bf16[64,1024]{1,0:T(8,128)(2,1)S(1)}, u32[]{:S(2)}, u32[]{:S(2)}) collective-permute-start(bf16[64,1024]{1,0:T(8,128)(2,1)S(1)} %get-tuple-element.24), channel_id=1, source_target_pairs={{0,28},{2,30},{4,24},{6,26},{8,20},{10,22},{12,16},{14,18},{16,12}... | collective-permute-start | bytes 393224 | tf_op jit(solution)/shard_map/ppermute | solution.py:376
  54.4 19.7 %collective-permute-start.2 = (bf16[64,1024]{1,0:T(8,128)(2,1)S(1)}, bf16[64,1024]{1,0:T(8,128)(2,1)S(1)}, u32[]{:S(2)}, u32[]{:S(2)}) collective-permute-start(bf16[64,1024]{1,0:T(8,128)(2,1)S(1)} %get-tuple-element.22), channel_id=1, source_target_pairs={{0,26},{2,24},{4,30},{6,28},{8,18},{10,16},{12,22},{14,20},{16,10}... | collective-permute-start | bytes 393224 | tf_op jit(solution)/shard_map/ppermute | solution.py:376
  56.4 20.7 %collective-permute-start.1 = (bf16[64,1024]{1,0:T(8,128)(2,1)S(1)}, bf16[64,1024]{1,0:T(8,128)(2,1)S(1)}, u32[]{:S(2)}, u32[]{:S(2)}) collective-permute-start(bf16[64,1024]{1,0:T(8,128)(2,1)S(1)} %get-tuple-element.20), channel_id=1, source_target_pairs={{0,30},{2,28},{4,26},{6,24},{8,22},{10,20},{12,18},{14,16},{16,14}... | collective-permute-start | bytes 393224 | tf_op jit(solution)/shard_map/ppermute | solution.py:376

commit v2 on v1

--- a/solution.py
+++ b/solution.py
@@ -183,7 +183,7 @@
 
 def attend(meta, first, near, far, own, past, out):
     rows = own[0].shape[0]
-    cap, width = far[0].shape
+    cap, width = near.shape[1:] if far == [] else far[0].shape
     blocks = rows // cap
     heads = width // LANES
     half = rows // 2
@@ -370,18 +370,21 @@
     past_rows = past_kv[:, : 2 * rows].reshape(-1, rows, 2, LANES)
     past = (past_rows[:, :, 0], past_apart, past_rows[:, :, 1])
 
-    ties = [None] * 3 + [parcels] * (half - 6) + [own_kv] * 2 + [past_kv]
-    for index, tie in enumerate(ties):
-        parcel = far[index] if tie is None else lax.optimization_barrier((far[index], tie))[0]
-        far[index] = lax.ppermute(parcel, "dp", [(owner, owner ^ (half + index)) for owner in range(owners)])
+    sent, far = far, []
+    for index, parcel in enumerate(sent):
+        if index >= 3:
+            ties = [far[index - 3], own_kv] if index < half - 2 else [past_kv] if index < half - 1 else [far[index - 4], past_kv]
+            parcel = lax.optimization_barrier((parcel, *ties))[0]
+        far.append(lax.ppermute(parcel, "dp", [(owner, owner ^ (half + index)) for owner in range(owners)]))
 
     meta = jnp.concatenate([column[None], places])
-    cuts = [0, half - 6, half - 3, half - 1, half]
+    cuts = [0, half - 5, half - 3, None, half - 3, half - 1, half]
     out = None
     for begin, end in zip(cuts[:-1], cuts[1:]):
-        out = attend(
-            meta, half + begin if begin else 0, None if begin else near, far[begin:end], own, past, out
-        )
+        if begin is None:
+            out = attend(meta, 0, near, [], own, past, out)
+        elif end is not None:
+            out = attend(meta, half + begin, None, far[begin:end], own, past, out)
     return out
 
 

time: 79.6 us -> 79.5 us (level)
  the two profiles are of different devices: /device:TPU:5 before, /device:TPU:1 now
where the time goes in v2:
time: 79.5 us; the launch traced here: 78.6 us
  starting transfers between devices  44.2 us (56%)
  Pallas kernels  16.5 us (21%)
  waiting for transfers between devices  14.5 us (18%)
  local copies, waits for them, and re-layouts  1.76 us (2%)
  other arithmetic  1.18 us (1%)
    ppermute x8, starting transfers between devices, local(): lax.ppermute(parcel, 'dp', [(owner, owner ^ half + index) for owner in ra...  29.4 us
    all_to_all x1, waiting for transfers between devices, local(): lax.all_to_all(send_kv, 'dp', split_axis=0, concat_axis=0, tiled=True)  14.5 us
    pallas_call x5, Pallas kernels, attend(): pl.pallas_call(kernel, out_shape=jax.ShapeDtypeStruct((rows, width), jnp....  11.1 us
    all_to_all x1, starting transfers between devices, local(): lax.all_to_all(send_kv, 'dp', split_axis=0, concat_axis=0, tiled=True)  7.33 us
    all_to_all x1, starting transfers between devices, local(): lax.all_to_all(near, 'dp', split_axis=0, concat_axis=0, axis_index_groups...  4.32 us
    ppermute x1, starting transfers between devices, local(): lax.ppermute(own_kv, 'ctx', [(0, 1)])[None]  3.16 us
    pallas_call x1, Pallas kernels, pack_q(): pl.pallas_call(kernel, out_shape=[pltpu.HBM((half, cap, width), queries.d...  2.44 us
    pallas_call x1, Pallas kernels, pack_kv(): pl.pallas_call(kernel, out_shape=pltpu.HBM((owners, LABEL_ROWS + 2 * cap,...  1.95 us
  transfers between devices with their start and end apart: 11, of which 1 were waited for; matrix products, arithmetic and copies ran while one was open for 4% of the time, Pallas kernels for 18%

profile of v2, /device:TPU:1, one launch (start us, length us, event | category | flops | bytes accessed | tf_op | source)
XLA Modules:
  0.0 78.6 jit_solution(1443453381684485534)
XLA Ops:
  0.0 2.0 %pack_kv.1.earlier_ref = bf16[16,144,128]{2,1,0:T(8,128)(2,1)} custom-call(s32[2,512]{1,0:T(2,128)} %bitcast.21, s32[4,128]{1,0:T(4,128)} %bitcast.24, bf16[1024,128]{1,0:T(8,128)(2,1)} %bitcast.20), custom_call_target="tpu_custom_call" | custom-call | tf_op jit(solution)/shard_map/pack_kv/pallas_call | solution.py:80
  2.0 7.3 %all-to-all-start = ((bf16[16,144,128]{2,1,0:T(8,128)(2,1)}), bf16[16,144,128]{2,1,0:T(8,128)(2,1)S(1)}, u32[]{:S(2)}, u32[]{:S(2)}) async-start(bf16[16,144,128]{2,1,0:T(8,128)(2,1)} %pack_kv.1.earlier_ref), calls=%async_computation | async-start | bytes 1179648 | tf_op jit(solution)/shard_map/all_to_all | solution.py:346
  9.3 2.4 %pack_q.1 = (bf16[8,64,1024]{2,1,0:T(8,128)(2,1)}, bf16[64,1024]{1,0:T(8,128)(2,1)S(1)}, bf16[64,1024]{1,0:T(8,128)(2,1)S(1)}, bf16[64,1024]{1,0:T(8,128)(2,1)S(...) custom-call(s32[2,512]{1,0:T(2,128)} %bitcast.22, ...), custom_call_target="tpu_custom_call" | custom-call | tf_op jit(solution)/shard_map/pack_q/pallas_call | solution.py:132
  11.7 2.4 %collective-permute-start.1 = (bf16[64,1024]{1,0:T(8,128)(2,1)S(1)}, bf16[64,1024]{1,0:T(8,128)(2,1)S(1)}, u32[]{:S(2)}, u32[]{:S(2)}) collective-permute-start(bf16[64,1024]{1,0:T(8,128)(2,1)S(1)} %get-tuple-element.21), channel_id=1, source_target_pairs={{0,16},{2,18},{4,20},{6,22},{8,24},{10,26},{12,28},{14,30},{16,0},... | collective-permute-start | bytes 393224 | tf_op jit(solution)/shard_map/ppermute | solution.py:378
  14.1 1.2 %collective-permute-start.4 = (bf16[64,1024]{1,0:T(8,128)(2,1)S(1)}, bf16[64,1024]{1,0:T(8,128)(2,1)S(1)}, u32[]{:S(2)}, u32[]{:S(2)}) collective-permute-start(bf16[64,1024]{1,0:T(8,128)(2,1)S(1)} %get-tuple-element.25), channel_id=1, source_target_pairs={{0,20},{2,22},{4,16},{6,18},{8,28},{10,30},{12,24},{14,26},{16,4},... | collective-permute-start | bytes 393224 | tf_op jit(solution)/shard_map/ppermute | solution.py:378
  15.3 2.9 %collective-permute-start.7 = (bf16[64,1024]{1,0:T(8,128)(2,1)S(1)}, bf16[64,1024]{1,0:T(8,128)(2,1)S(1)}, u32[]{:S(2)}, u32[]{:S(2)}) collective-permute-start(bf16[64,1024]{1,0:T(8,128)(2,1)S(1)} %get-tuple-element.31), channel_id=1, source_target_pairs={{0,18},{2,16},{4,22},{6,20},{8,26},{10,24},{12,30},{14,28},{16,2},... | collective-permute-start | bytes 393224 | tf_op jit(solution)/shard_map/ppermute | solution.py:378
  18.2 0.1 slice_xor_fusion
  18.3 0.1 pad_add_fusion
  18.3 14.5 %all-to-all-done.in_ref = bf16[16,144,128]{2,1,0:T(8,128)(2,1)S(1)} async-done(((bf16[16,144,128]{2,1,0:T(8,128)(2,1)}), bf16[16,144,128]{2,1,0:T(8,128)(2,1)S(1)}, u32[]{:S(2)}, u32[]{:S(2)}) %all-to-all-start) | async-done | bytes 589856 | tf_op jit(solution)/shard_map/all_to_all | solution.py:346
  32.9 4.3 %all-to-all-start.1 = ((bf16[8,64,1024]{2,1,0:T(8,128)(2,1)}), bf16[8,64,1024]{2,1,0:T(8,128)(2,1)S(1)}, u32[]{:S(2)}, u32[]{:S(2)}) async-start(bf16[8,64,1024]{2,1,0:T(8,128)(2,1)} %get-tuple-element.29), calls=%async_computation.1 | async-start | bytes 2097152 | tf_op jit(solution)/shard_map/all_to_all | solution.py:349
  37.2 0.7 slice_reduce_fusion
  37.9 0.1 add.112
  38.0 0.1 select_reduce_fusion
  38.1 0.1 reshape.420
  38.2 0.1 broadcast_in_dim_reshape.2
  38.3 0.1 select_reduce_fusion.2.source_ref
  38.4 1.0 %place_kv.1 = bf16[1040,128]{1,0:T(8,128)(2,1)S(1)} custom-call(s32[8]{0:T(128)S(1)} %select_reduce_fusion.2.source_ref, bf16[16,144,128]{2,1,0:T(8,128)(2,1)S(1)} %all-to-all-done.in_ref, bf16[16,128]{1,0:T(8,128)(2,1)S(1)} %pad.4.begin_ref), custom_call_target="tpu_custom_call" | custom-call | tf_op jit(solution)/shard_map/place_kv/pallas_call | solution.py:173
  39.5 3.2 %collective-permute-start = (bf16[1040,128]{1,0:T(8,128)(2,1)S(1)}, bf16[1040,128]{1,0:T(8,128)(2,1)S(1)}, u32[]{:S(2)}, u32[]{:S(2)}) collective-permute-start(bf16[1040,128]{1,0:T(8,128)(2,1)S(1)} %place_kv.1), channel_id=1, source_target_pairs={{0,1},{2,3},{4,5},{6,7},{8,9},{10,11},{12,13},{14,15},{16,17},{18,... | collective-permute-start | bytes 798728 | tf_op jit(solution)/shard_map/ppermute | solution.py:365
  42.6 0.0 collective-permute-done.1.rest_0_
  42.6 4.1 %collective-permute-start.2 = (bf16[64,1024]{1,0:T(8,128)(2,1)S(1)}, bf16[64,1024]{1,0:T(8,128)(2,1)S(1)}, u32[]{:S(2)}, u32[]{:S(2)}) collective-permute-start(bf16[64,1024]{1,0:T(8,128)(2,1)S(1)} %get-tuple-element.22), channel_id=1, source_target_pairs={{0,22},{2,20},{4,18},{6,16},{8,30},{10,28},{12,26},{14,24},{16,6},... | collective-permute-start | bytes 393224 | tf_op jit(solution)/shard_map/ppermute | solution.py:378
  46.7 0.4 fusion.6
  47.1 0.0 collective-permute-done.4.rest_2_
  47.1 0.7 collective-permute-start.5
  47.8 0.0 collective-permute-done.7.rest_1_
  47.8 2.4 %collective-permute-start.8 = (bf16[64,1024]{1,0:T(8,128)(2,1)S(1)}, bf16[64,1024]{1,0:T(8,128)(2,1)S(1)}, u32[]{:S(2)}, u32[]{:S(2)}) collective-permute-start(bf16[64,1024]{1,0:T(8,128)(2,1)S(1)} %get-tuple-element.32), channel_id=1, source_target_pairs={{0,24},{2,26},{4,28},{6,30},{8,16},{10,18},{12,20},{14,22},{16,8},... | collective-permute-start | bytes 393224 | tf_op jit(solution)/shard_map/ppermute | solution.py:378
  50.3 0.2 select_convert_fusion.1
  50.5 0.2 select_reduce_fusion.1
  50.7 0.1 pad_add_fusion.1.meta_ref
  50.8 0.0 collective-permute-done
  50.9 1.7 %collective-permute-start.6 = (bf16[64,1024]{1,0:T(8,128)(2,1)S(1)}, bf16[64,1024]{1,0:T(8,128)(2,1)S(1)}, u32[]{:S(2)}, u32[]{:S(2)}) collective-permute-start(bf16[64,1024]{1,0:T(8,128)(2,1)S(1)} %get-tuple-element.28), channel_id=1, source_target_pairs={{0,28},{2,30},{4,24},{6,26},{8,20},{10,22},{12,16},{14,18},{16,12}... | collective-permute-start | bytes 393224 | tf_op jit(solution)/shard_map/ppermute | solution.py:378
  52.5 0.0 collective-permute-done.2.rest_0_
  52.5 14.0 %collective-permute-start.3 = (bf16[64,1024]{1,0:T(8,128)(2,1)S(1)}, bf16[64,1024]{1,0:T(8,128)(2,1)S(1)}, u32[]{:S(2)}, u32[]{:S(2)}) collective-permute-start(bf16[64,1024]{1,0:T(8,128)(2,1)S(1)} %get-tuple-element.23), channel_id=1, source_target_pairs={{0,30},{2,28},{4,26},{6,24},{8,22},{10,20},{12,18},{14,16},{16,14}... | collective-permute-start | bytes 393224 | tf_op jit(solution)/shard_map/ppermute | solution.py:378
  66.6 0.4 fusion.5
  67.0 0.2 select_convert_fusion.pd_ref
  67.2 1.8 %attend.5.rest_2_ = bf16[512,1024]{1,0:T(8,128)(2,1)} custom-call(s32[17]{0:T(128)S(1)} %pad_add_fusion.1.meta_ref, bf16[512,128]{1,0:T(8,128)(2,1)S(1)} %get-tuple-element.40.qd_ref, bf16[512,128]{1,0:T(8,128)(2,1)S(1)} %get-tuple-element.50.ok_ref, bf16[512,128]{1,0:T(8,128)(2,1)S(1)} %get-tuple-element.39.od_ref, ...), custom_call_target="tpu_custom_call" | custom-call | flops 536870912 | bytes 786432 | tf_op jit(solution)/shard_map/attend/pallas_call | solution.py:303
  69.1 0.0 collective-permute-done.8.rest_1_
  69.1 2.5 %attend.6.rest_1_ = bf16[512,1024]{1,0:T(8,128)(2,1)} custom-call(s32[17]{0:T(128)S(1)} %pad_add_fusion.1.meta_ref, bf16[512,128]{1,0:T(8,128)(2,1)S(1)} %get-tuple-element.40.qd_ref, bf16[512,128]{1,0:T(8,128)(2,1)S(1)} %get-tuple-element.50.ok_ref, bf16[512,128]{1,0:T(8,128)(2,1)S(1)} %get-tuple-element.39.od_ref, ...), custom_call_target="tpu_custom_call", output_to_operand_aliasing={{}: (10, {})} | custom-call | flops 536870912 | bytes 524288 | tf_op jit(solution)/shard_map/attend/pallas_call | solution.py:303
  71.6 0.0 all-to-all-done.1.rest_0_
  71.6 4.0 %attend.7.rest_2_ = bf16[512,1024]{1,0:T(8,128)(2,1)} custom-call(s32[17]{0:T(128)S(1)} %pad_add_fusion.1.meta_ref, bf16[512,128]{1,0:T(8,128)(2,1)S(1)} %get-tuple-element.40.qd_ref, bf16[512,128]{1,0:T(8,128)(2,1)S(1)} %get-tuple-element.50.ok_ref, bf16[512,128]{1,0:T(8,128)(2,1)S(1)} %get-tuple-element.39.od_ref, ...), custom_call_target="tpu_custom_call", output_to_operand_aliasing={{}: (9, {})} | custom-call | flops 2147483648 | bytes 2097152 | tf_op jit(solution)/shard_map/attend/pallas_call | solution.py:303
  75.6 0.0 collective-permute-done.5.rest_0_
  75.7 0.0 collective-permute-done.6.rest_1_
  75.7 2.2 %attend.8.rest_1_ = bf16[512,1024]{1,0:T(8,128)(2,1)} custom-call(s32[17]{0:T(128)S(1)} %pad_add_fusion.1.meta_ref, bf16[512,128]{1,0:T(8,128)(2,1)S(1)} %get-tuple-element.40.qd_ref, bf16[512,128]{1,0:T(8,128)(2,1)S(1)} %get-tuple-element.50.ok_ref, bf16[512,128]{1,0:T(8,128)(2,1)S(1)} %get-tuple-element.39.od_ref, ...), custom_call_target="tpu_custom_call", output_to_operand_aliasing={{}: (10, {})} | custom-call | flops 536870912 | bytes 524288 | tf_op jit(solution)/shard_map/attend/pallas_call | solution.py:303
  77.8 0.0 collective-permute-done.3.rest_0_
  77.8 0.6 attend.9
  (22 shorter events, 0.3 us)
Async XLA Ops:
  2.0 30.9 %all-to-all-start = ((bf16[16,144,128]{2,1,0:T(8,128)(2,1)}), bf16[16,144,128]{2,1,0:T(8,128)(2,1)S(1)}, u32[]{:S(2)}, u32[]{:S(2)}) async-start(bf16[16,144,128]{2,1,0:T(8,128)(2,1)} %pack_kv.1.earlier_ref), calls=%async_computation | async-start | bytes 1179648 | tf_op jit(solution)/shard_map/all_to_all | solution.py:346
  11.7 30.9 %collective-permute-start.1 = (bf16[64,1024]{1,0:T(8,128)(2,1)S(1)}, bf16[64,1024]{1,0:T(8,128)(2,1)S(1)}, u32[]{:S(2)}, u32[]{:S(2)}) collective-permute-start(bf16[64,1024]{1,0:T(8,128)(2,1)S(1)} %get-tuple-element.21), channel_id=1, source_target_pairs={{0,16},{2,18},{4,20},{6,22},{8,24},{10,26},{12,28},{14,30},{16,0},... | collective-permute-start | bytes 393224 | tf_op jit(solution)/shard_map/ppermute | solution.py:378
  14.1 33.0 %collective-permute-start.4 = (bf16[64,1024]{1,0:T(8,128)(2,1)S(1)}, bf16[64,1024]{1,0:T(8,128)(2,1)S(1)}, u32[]{:S(2)}, u32[]{:S(2)}) collective-permute-start(bf16[64,1024]{1,0:T(8,128)(2,1)S(1)} %get-tuple-element.25), channel_id=1, source_target_pairs={{0,20},{2,22},{4,16},{6,18},{8,28},{10,30},{12,24},{14,26},{16,4},... | collective-permute-start | bytes 393224 | tf_op jit(solution)/shard_map/ppermute | solution.py:378
  15.3 32.5 %collective-permute-start.7 = (bf16[64,1024]{1,0:T(8,128)(2,1)S(1)}, bf16[64,1024]{1,0:T(8,128)(2,1)S(1)}, u32[]{:S(2)}, u32[]{:S(2)}) collective-permute-start(bf16[64,1024]{1,0:T(8,128)(2,1)S(1)} %get-tuple-element.31), channel_id=1, source_target_pairs={{0,18},{2,16},{4,22},{6,20},{8,26},{10,24},{12,30},{14,28},{16,2},... | collective-permute-start | bytes 393224 | tf_op jit(solution)/shard_map/ppermute | solution.py:378
  32.9 38.7 %all-to-all-start.1 = ((bf16[8,64,1024]{2,1,0:T(8,128)(2,1)}), bf16[8,64,1024]{2,1,0:T(8,128)(2,1)S(1)}, u32[]{:S(2)}, u32[]{:S(2)}) async-start(bf16[8,64,1024]{2,1,0:T(8,128)(2,1)} %get-tuple-element.29), calls=%async_computation.1 | async-start | bytes 2097152 | tf_op jit(solution)/shard_map/all_to_all | solution.py:349
  39.5 11.3 %collective-permute-start = (bf16[1040,128]{1,0:T(8,128)(2,1)S(1)}, bf16[1040,128]{1,0:T(8,128)(2,1)S(1)}, u32[]{:S(2)}, u32[]{:S(2)}) collective-permute-start(bf16[1040,128]{1,0:T(8,128)(2,1)S(1)} %place_kv.1), channel_id=1, source_target_pairs={{0,1},{2,3},{4,5},{6,7},{8,9},{10,11},{12,13},{14,15},{16,17},{18,... | collective-permute-start | bytes 798728 | tf_op jit(solution)/shard_map/ppermute | solution.py:365
  42.6 9.9 %collective-permute-start.2 = (bf16[64,1024]{1,0:T(8,128)(2,1)S(1)}, bf16[64,1024]{1,0:T(8,128)(2,1)S(1)}, u32[]{:S(2)}, u32[]{:S(2)}) collective-permute-start(bf16[64,1024]{1,0:T(8,128)(2,1)S(1)} %get-tuple-element.22), channel_id=1, source_target_pairs={{0,22},{2,20},{4,18},{6,16},{8,30},{10,28},{12,26},{14,24},{16,6},... | collective-permute-start | bytes 393224 | tf_op jit(solution)/shard_map/ppermute | solution.py:378
  47.1 28.5 %collective-permute-start.5 = (bf16[64,1024]{1,0:T(8,128)(2,1)S(1)}, bf16[64,1024]{1,0:T(8,128)(2,1)S(1)}, u32[]{:S(2)}, u32[]{:S(2)}) collective-permute-start(bf16[64,1024]{1,0:T(8,128)(2,1)S(1)} %get-tuple-element.26), channel_id=1, source_target_pairs={{0,26},{2,24},{4,30},{6,28},{8,18},{10,16},{12,22},{14,20},{16,10}... | collective-permute-start | bytes 393224 | tf_op jit(solution)/shard_map/ppermute | solution.py:378
  47.8 21.2 %collective-permute-start.8 = (bf16[64,1024]{1,0:T(8,128)(2,1)S(1)}, bf16[64,1024]{1,0:T(8,128)(2,1)S(1)}, u32[]{:S(2)}, u32[]{:S(2)}) collective-permute-start(bf16[64,1024]{1,0:T(8,128)(2,1)S(1)} %get-tuple-element.32), channel_id=1, source_target_pairs={{0,24},{2,26},{4,28},{6,30},{8,16},{10,18},{12,20},{14,22},{16,8},... | collective-permute-start | bytes 393224 | tf_op jit(solution)/shard_map/ppermute | solution.py:378
  50.9 24.8 %collective-permute-start.6 = (bf16[64,1024]{1,0:T(8,128)(2,1)S(1)}, bf16[64,1024]{1,0:T(8,128)(2,1)S(1)}, u32[]{:S(2)}, u32[]{:S(2)}) collective-permute-start(bf16[64,1024]{1,0:T(8,128)(2,1)S(1)} %get-tuple-element.28), channel_id=1, source_target_pairs={{0,28},{2,30},{4,24},{6,26},{8,20},{10,22},{12,16},{14,18},{16,12}... | collective-permute-start | bytes 393224 | tf_op jit(solution)/shard_map/ppermute | solution.py:378
  52.5 25.3 %collective-permute-start.3 = (bf16[64,1024]{1,0:T(8,128)(2,1)S(1)}, bf16[64,1024]{1,0:T(8,128)(2,1)S(1)}, u32[]{:S(2)}, u32[]{:S(2)}) collective-permute-start(bf16[64,1024]{1,0:T(8,128)(2,1)S(1)} %get-tuple-element.23), channel_id=1, source_target_pairs={{0,30},{2,28},{4,26},{6,24},{8,22},{10,20},{12,18},{14,16},{16,14}... | collective-permute-start | bytes 393224 | tf_op jit(solution)/shard_map/ppermute | solution.py:378

commit v3 on v2

--- a/solution.py
+++ b/solution.py
@@ -195,7 +195,8 @@
 
     def kernel(meta_ref, qd_ref, ok_ref, od_ref, ov_ref, pk_ref, pd_ref, pv_ref, *rest):
         array_refs = rest[: len(arrays)]
-        out_any, stage_ref, result_ref, sem = rest[-4:]
+        out_any, token_ref, stage_ref, result_ref, sem = rest[-5:]
+        token_ref[...] = jnp.zeros_like(token_ref)
 
         def keys(k_ref, d_ref):
             return jnp.concatenate([k_ref, d_ref], axis=1)
@@ -302,9 +303,12 @@
     area = max(1, parcels // 2) * heads * cap * (count + 1) * rows
     return pl.pallas_call(
         kernel,
-        out_shape=jax.ShapeDtypeStruct((rows, width), jnp.bfloat16),
+        out_shape=[
+            jax.ShapeDtypeStruct((rows, width), jnp.bfloat16),
+            jax.ShapeDtypeStruct((8, LANES), jnp.int32),
+        ],
         in_specs=specs,
-        out_specs=ANY,
+        out_specs=[ANY, VMEM],
         input_output_aliases=aliases,
         scratch_shapes=[
             pltpu.VMEM((parcels, cap, width), jnp.bfloat16),
@@ -370,21 +374,19 @@
     past_rows = past_kv[:, : 2 * rows].reshape(-1, rows, 2, LANES)
     past = (past_rows[:, :, 0], past_apart, past_rows[:, :, 1])
 
+    meta = jnp.concatenate([column[None], places])
     sent, far = far, []
+    out = token = None
     for index, parcel in enumerate(sent):
+        if index == half - 2:
+            out, token = attend(meta, half, None, far[: half - 5], own, past, None)
         if index >= 3:
-            ties = [far[index - 3], own_kv] if index < half - 2 else [past_kv] if index < half - 1 else [far[index - 4], past_kv]
+            ties = (token,) if index >= half - 2 else (far[index - 3], own_kv if index > 3 else parcels)
             parcel = lax.optimization_barrier((parcel, *ties))[0]
         far.append(lax.ppermute(parcel, "dp", [(owner, owner ^ (half + index)) for owner in range(owners)]))
-
-    meta = jnp.concatenate([column[None], places])
-    cuts = [0, half - 5, half - 3, None, half - 3, half - 1, half]
-    out = None
-    for begin, end in zip(cuts[:-1], cuts[1:]):
-        if begin is None:
-            out = attend(meta, 0, near, [], own, past, out)
-        elif end is not None:
-            out = attend(meta, half + begin, None, far[begin:end], own, past, out)
+    out, _ = attend(meta, 0, near, [], own, past, out)
+    for begin, end in ((half - 5, half - 2), (half - 2, half)):
+        out, _ = attend(meta, half + begin, None, far[begin:end], own, past, out)
     return out
 
 

time: 79.5 us -> 79.4 us (level)
  the two profiles are of different devices: /device:TPU:1 before, /device:TPU:5 now
where the time goes in v3:
time: 79.4 us; the launch traced here: 79.1 us
  starting transfers between devices  31.9 us (40%)
  waiting for transfers between devices  23.8 us (30%)
  Pallas kernels  20.2 us (25%)
  local copies, waits for them, and re-layouts  1.76 us (2%)
  other arithmetic  1.18 us (1%)
    ppermute x8, starting transfers between devices, local(): lax.ppermute(parcel, 'dp', [(owner, owner ^ half + index) for owner in ra...  19.8 us
    pallas_call x4, Pallas kernels, attend(): pl.pallas_call(kernel, out_shape=[jax.ShapeDtypeStruct((rows, width), jnp...  15 us
    all_to_all x1, waiting for transfers between devices, local(): lax.all_to_all(send_kv, 'dp', split_axis=0, concat_axis=0, tiled=True)  14.8 us
    all_to_all x1, waiting for transfers between devices, local(): lax.all_to_all(near, 'dp', split_axis=0, concat_axis=0, axis_index_groups...  8.83 us
    all_to_all x1, starting transfers between devices, local(): lax.all_to_all(send_kv, 'dp', split_axis=0, concat_axis=0, tiled=True)  6.5 us
    all_to_all x1, starting transfers between devices, local(): lax.all_to_all(near, 'dp', split_axis=0, concat_axis=0, axis_index_groups...  4.32 us
    pallas_call x1, Pallas kernels, pack_q(): pl.pallas_call(kernel, out_shape=[pltpu.HBM((half, cap, width), queries.d...  2.25 us
    pallas_call x1, Pallas kernels, pack_kv(): pl.pallas_call(kernel, out_shape=pltpu.HBM((owners, LABEL_ROWS + 2 * cap,...  1.95 us
  transfers between devices with their start and end apart: 11, of which 3 were waited for; matrix products, arithmetic and copies ran while one was open for 4% of the time, Pallas kernels for 19%

profile of v3, /device:TPU:5, one launch (start us, length us, event | category | flops | bytes accessed | tf_op | source)
XLA Modules:
  0.0 79.1 jit_solution(1790005990272121296)
XLA Ops:
  0.0 2.0 %pack_kv.1.earlier_ref = bf16[16,144,128]{2,1,0:T(8,128)(2,1)} custom-call(s32[2,512]{1,0:T(2,128)} %bitcast.21, s32[4,128]{1,0:T(4,128)} %bitcast.24, bf16[1024,128]{1,0:T(8,128)(2,1)} %bitcast.20), custom_call_target="tpu_custom_call" | custom-call | tf_op jit(solution)/shard_map/pack_kv/pallas_call | solution.py:80
  2.0 6.5 %all-to-all-start = ((bf16[16,144,128]{2,1,0:T(8,128)(2,1)}), bf16[16,144,128]{2,1,0:T(8,128)(2,1)S(1)}, u32[]{:S(2)}, u32[]{:S(2)}) async-start(bf16[16,144,128]{2,1,0:T(8,128)(2,1)} %pack_kv.1.earlier_ref), calls=%async_computation | async-start | bytes 1179648 | tf_op jit(solution)/shard_map/all_to_all | solution.py:350
  8.5 2.2 %pack_q.1 = (bf16[8,64,1024]{2,1,0:T(8,128)(2,1)}, bf16[64,1024]{1,0:T(8,128)(2,1)S(1)}, bf16[64,1024]{1,0:T(8,128)(2,1)S(1)}, bf16[64,1024]{1,0:T(8,128)(2,1)S(...) custom-call(s32[2,512]{1,0:T(2,128)} %bitcast.22, ...), custom_call_target="tpu_custom_call" | custom-call | tf_op jit(solution)/shard_map/pack_q/pallas_call | solution.py:132
  10.7 2.4 %collective-permute-start.1 = (bf16[64,1024]{1,0:T(8,128)(2,1)S(1)}, bf16[64,1024]{1,0:T(8,128)(2,1)S(1)}, u32[]{:S(2)}, u32[]{:S(2)}) collective-permute-start(bf16[64,1024]{1,0:T(8,128)(2,1)S(1)} %get-tuple-element.25), channel_id=1, source_target_pairs={{0,16},{2,18},{4,20},{6,22},{8,24},{10,26},{12,28},{14,30},{16,0},... | collective-permute-start | bytes 393224 | tf_op jit(solution)/shard_map/ppermute | solution.py:386
  13.1 0.3 collective-permute-start.2
  13.4 3.7 %collective-permute-start.3 = (bf16[64,1024]{1,0:T(8,128)(2,1)S(1)}, bf16[64,1024]{1,0:T(8,128)(2,1)S(1)}, u32[]{:S(2)}, u32[]{:S(2)}) collective-permute-start(bf16[64,1024]{1,0:T(8,128)(2,1)S(1)} %get-tuple-element.27), channel_id=1, source_target_pairs={{0,20},{2,22},{4,16},{6,18},{8,28},{10,30},{12,24},{14,26},{16,4},... | collective-permute-start | bytes 393224 | tf_op jit(solution)/shard_map/ppermute | solution.py:386
  17.1 0.1 slice_xor_fusion
  17.2 0.1 pad_add_fusion
  17.2 14.8 %all-to-all-done.in_ref = bf16[16,144,128]{2,1,0:T(8,128)(2,1)S(1)} async-done(((bf16[16,144,128]{2,1,0:T(8,128)(2,1)}), bf16[16,144,128]{2,1,0:T(8,128)(2,1)S(1)}, u32[]{:S(2)}, u32[]{:S(2)}) %all-to-all-start) | async-done | bytes 589856 | tf_op jit(solution)/shard_map/all_to_all | solution.py:350
  32.0 4.3 %all-to-all-start.1 = ((bf16[8,64,1024]{2,1,0:T(8,128)(2,1)}), bf16[8,64,1024]{2,1,0:T(8,128)(2,1)S(1)}, u32[]{:S(2)}, u32[]{:S(2)}) async-start(bf16[8,64,1024]{2,1,0:T(8,128)(2,1)} %get-tuple-element.38), calls=%async_computation.1 | async-start | bytes 2097152 | tf_op jit(solution)/shard_map/all_to_all | solution.py:353
  36.4 0.7 slice_reduce_fusion
  37.1 0.1 add.112
  37.2 0.1 select_reduce_fusion
  37.3 0.1 reshape.420
  37.4 0.1 broadcast_in_dim_reshape.2
  37.5 0.1 select_reduce_fusion.2.source_ref
  37.6 1.0 %place_kv.1 = bf16[1040,128]{1,0:T(8,128)(2,1)S(1)} custom-call(s32[8]{0:T(128)S(1)} %select_reduce_fusion.2.source_ref, bf16[16,144,128]{2,1,0:T(8,128)(2,1)S(1)} %all-to-all-done.in_ref, bf16[16,128]{1,0:T(8,128)(2,1)S(1)} %pad.4.begin_ref), custom_call_target="tpu_custom_call" | custom-call | tf_op jit(solution)/shard_map/place_kv/pallas_call | solution.py:173
  38.6 1.3 %collective-permute-start = (bf16[1040,128]{1,0:T(8,128)(2,1)S(1)}, bf16[1040,128]{1,0:T(8,128)(2,1)S(1)}, u32[]{:S(2)}, u32[]{:S(2)}) collective-permute-start(bf16[1040,128]{1,0:T(8,128)(2,1)S(1)} %place_kv.1), channel_id=1, source_target_pairs={{0,1},{2,3},{4,5},{6,7},{8,9},{10,11},{12,13},{14,15},{16,17},{18,... | collective-permute-start | bytes 798728 | tf_op jit(solution)/shard_map/ppermute | solution.py:369
  39.9 0.0 collective-permute-done.1.rest_0_
  40.0 3.8 %collective-permute-start.6 = (bf16[64,1024]{1,0:T(8,128)(2,1)S(1)}, bf16[64,1024]{1,0:T(8,128)(2,1)S(1)}, u32[]{:S(2)}, u32[]{:S(2)}) collective-permute-start(bf16[64,1024]{1,0:T(8,128)(2,1)S(1)} %get-tuple-element.33), channel_id=1, source_target_pairs={{0,22},{2,20},{4,18},{6,16},{8,30},{10,28},{12,26},{14,24},{16,6},... | collective-permute-start | bytes 393224 | tf_op jit(solution)/shard_map/ppermute | solution.py:386
  43.8 0.4 fusion.6
  44.1 0.0 collective-permute-done.2.rest_1_
  44.1 0.9 %collective-permute-start.7 = (bf16[64,1024]{1,0:T(8,128)(2,1)S(1)}, bf16[64,1024]{1,0:T(8,128)(2,1)S(1)}, u32[]{:S(2)}, u32[]{:S(2)}) collective-permute-start(bf16[64,1024]{1,0:T(8,128)(2,1)S(1)} %get-tuple-element.35), channel_id=1, source_target_pairs={{0,24},{2,26},{4,28},{6,30},{8,16},{10,18},{12,20},{14,22},{16,8},... | collective-permute-start | bytes 393224 | tf_op jit(solution)/shard_map/ppermute | solution.py:386
  45.1 0.0 collective-permute-done.3.rest_2_
  45.1 2.8 %collective-permute-start.8 = (bf16[64,1024]{1,0:T(8,128)(2,1)S(1)}, bf16[64,1024]{1,0:T(8,128)(2,1)S(1)}, u32[]{:S(2)}, u32[]{:S(2)}) collective-permute-start(bf16[64,1024]{1,0:T(8,128)(2,1)S(1)} %get-tuple-element.37), channel_id=1, source_target_pairs={{0,26},{2,24},{4,30},{6,28},{8,18},{10,16},{12,22},{14,20},{16,10}... | collective-permute-start | bytes 393224 | tf_op jit(solution)/shard_map/ppermute | solution.py:386
  47.9 0.2 select_convert_fusion.1
  48.1 0.2 select_reduce_fusion.1
  48.3 0.1 pad_add_fusion.1.meta_ref
  48.4 0.2 collective-permute-done
  48.6 0.2 select_convert_fusion.pd_ref
  48.8 0.4 fusion.5
  49.3 2.9 %attend.4 = (bf16[512,1024]{1,0:T(8,128)(2,1)}, s32[8,128]{1,0:T(8,128)}) custom-call(s32[17]{0:T(128)S(1)} %pad_add_fusion.1.meta_ref, bf16[512,128]{1,0:T(8,128)(2,1)S(1)} %get-tuple-element.50.qd_ref, bf16[512,128]{1,0:T(8,128)(2,1)S(1)} %get-tuple-element.60.ok_ref, bf16[512,128]{1,0:T(8,128)(2,1)S(1)} %get-tuple-element.49.od_ref, ...), custom_call_target="tpu_custom_call" | custom-call | flops 536870912 | bytes 786432 | tf_op jit(solution)/shard_map/attend/pallas_call | solution.py:304
  52.2 3.9 %collective-permute-start.4 = (bf16[64,1024]{1,0:T(8,128)(2,1)S(1)}, bf16[64,1024]{1,0:T(8,128)(2,1)S(1)}, u32[]{:S(2)}, u32[]{:S(2)}) collective-permute-start(bf16[64,1024]{1,0:T(8,128)(2,1)S(1)} %get-tuple-element.29), channel_id=1, source_target_pairs={{0,28},{2,30},{4,24},{6,26},{8,20},{10,22},{12,16},{14,18},{16,12}... | collective-permute-start | bytes 393224 | tf_op jit(solution)/shard_map/ppermute | solution.py:386
  56.1 2.1 %collective-permute-start.5 = (bf16[64,1024]{1,0:T(8,128)(2,1)S(1)}, bf16[64,1024]{1,0:T(8,128)(2,1)S(1)}, u32[]{:S(2)}, u32[]{:S(2)}) collective-permute-start(bf16[64,1024]{1,0:T(8,128)(2,1)S(1)} %get-tuple-element.31), channel_id=1, source_target_pairs={{0,30},{2,28},{4,26},{6,24},{8,22},{10,20},{12,18},{14,16},{16,14}... | collective-permute-start | bytes 393224 | tf_op jit(solution)/shard_map/ppermute | solution.py:386
  58.1 8.8 %all-to-all-done.1.rest_0_ = bf16[8,64,1024]{2,1,0:T(8,128)(2,1)S(1)} async-done(((bf16[8,64,1024]{2,1,0:T(8,128)(2,1)}), bf16[8,64,1024]{2,1,0:T(8,128)(2,1)S(1)}, u32[]{:S(2)}, u32[]{:S(2)}) %all-to-all-start.1) | async-done | bytes 1048608 | tf_op jit(solution)/shard_map/all_to_all | solution.py:353
  67.0 4.8 %attend.5 = (bf16[512,1024]{1,0:T(8,128)(2,1)}, s32[8,128]{1,0:T(8,128)}) custom-call(s32[17]{0:T(128)S(1)} %pad_add_fusion.1.meta_ref, bf16[512,128]{1,0:T(8,128)(2,1)S(1)} %get-tuple-element.50.qd_ref, bf16[512,128]{1,0:T(8,128)(2,1)S(1)} %get-tuple-element.60.ok_ref, ...), custom_call_target="tpu_custom_call", output_to_operand_aliasing={{0}: (9, {})} | custom-call | flops 2147483648 | bytes 2097152 | tf_op jit(solution)/shard_map/attend/pallas_call | solution.py:304
  71.7 0.0 collective-permute-done.6.rest_0_
  71.7 0.0 collective-permute-done.7.rest_1_
  71.8 0.0 collective-permute-done.8.rest_2_
  71.8 4.5 %attend.6 = (bf16[512,1024]{1,0:T(8,128)(2,1)}, s32[8,128]{1,0:T(8,128)}) custom-call(s32[17]{0:T(128)S(1)} %pad_add_fusion.1.meta_ref, bf16[512,128]{1,0:T(8,128)(2,1)S(1)} %get-tuple-element.50.qd_ref, bf16[512,128]{1,0:T(8,128)(2,1)S(1)} %get-tuple-element.60.ok_ref, ...), custom_call_target="tpu_custom_call", output_to_operand_aliasing={{0}: (11, {})} | custom-call | flops 536870912 | bytes 786432 | tf_op jit(solution)/shard_map/attend/pallas_call | solution.py:304
  76.2 0.0 collective-permute-done.4.rest_0_
  76.3 0.0 collective-permute-done.5.rest_1_
  76.3 2.9 %attend.7 = (bf16[512,1024]{1,0:T(8,128)(2,1)}, s32[8,128]{1,0:T(8,128)}) custom-call(s32[17]{0:T(128)S(1)} %pad_add_fusion.1.meta_ref, bf16[512,128]{1,0:T(8,128)(2,1)S(1)} %get-tuple-element.50.qd_ref, bf16[512,128]{1,0:T(8,128)(2,1)S(1)} %get-tuple-element.60.ok_ref, ...), custom_call_target="tpu_custom_call", output_to_operand_aliasing={{0}: (10, {})} | custom-call | flops 536870912 | bytes 524288 | tf_op jit(solution)/shard_map/attend/pallas_call | solution.py:304
  (22 shorter events, 0.3 us)
Async XLA Ops:
  2.0 30.1 %all-to-all-start = ((bf16[16,144,128]{2,1,0:T(8,128)(2,1)}), bf16[16,144,128]{2,1,0:T(8,128)(2,1)S(1)}, u32[]{:S(2)}, u32[]{:S(2)}) async-start(bf16[16,144,128]{2,1,0:T(8,128)(2,1)} %pack_kv.1.earlier_ref), calls=%async_computation | async-start | bytes 1179648 | tf_op jit(solution)/shard_map/all_to_all | solution.py:350
  10.7 29.2 %collective-permute-start.1 = (bf16[64,1024]{1,0:T(8,128)(2,1)S(1)}, bf16[64,1024]{1,0:T(8,128)(2,1)S(1)}, u32[]{:S(2)}, u32[]{:S(2)}) collective-permute-start(bf16[64,1024]{1,0:T(8,128)(2,1)S(1)} %get-tuple-element.25), channel_id=1, source_target_pairs={{0,16},{2,18},{4,20},{6,22},{8,24},{10,26},{12,28},{14,30},{16,0},... | collective-permute-start | bytes 393224 | tf_op jit(solution)/shard_map/ppermute | solution.py:386
  13.1 31.0 %collective-permute-start.2 = (bf16[64,1024]{1,0:T(8,128)(2,1)S(1)}, bf16[64,1024]{1,0:T(8,128)(2,1)S(1)}, u32[]{:S(2)}, u32[]{:S(2)}) collective-permute-start(bf16[64,1024]{1,0:T(8,128)(2,1)S(1)} %get-tuple-element.26), channel_id=1, source_target_pairs={{0,18},{2,16},{4,22},{6,20},{8,26},{10,24},{12,30},{14,28},{16,2},... | collective-permute-start | bytes 393224 | tf_op jit(solution)/shard_map/ppermute | solution.py:386
  13.4 31.7 %collective-permute-start.3 = (bf16[64,1024]{1,0:T(8,128)(2,1)S(1)}, bf16[64,1024]{1,0:T(8,128)(2,1)S(1)}, u32[]{:S(2)}, u32[]{:S(2)}) collective-permute-start(bf16[64,1024]{1,0:T(8,128)(2,1)S(1)} %get-tuple-element.27), channel_id=1, source_target_pairs={{0,20},{2,22},{4,16},{6,18},{8,28},{10,30},{12,24},{14,26},{16,4},... | collective-permute-start | bytes 393224 | tf_op jit(solution)/shard_map/ppermute | solution.py:386
  32.0 34.9 %all-to-all-start.1 = ((bf16[8,64,1024]{2,1,0:T(8,128)(2,1)}), bf16[8,64,1024]{2,1,0:T(8,128)(2,1)S(1)}, u32[]{:S(2)}, u32[]{:S(2)}) async-start(bf16[8,64,1024]{2,1,0:T(8,128)(2,1)} %get-tuple-element.38), calls=%async_computation.1 | async-start | bytes 2097152 | tf_op jit(solution)/shard_map/all_to_all | solution.py:353
  38.6 9.9 %collective-permute-start = (bf16[1040,128]{1,0:T(8,128)(2,1)S(1)}, bf16[1040,128]{1,0:T(8,128)(2,1)S(1)}, u32[]{:S(2)}, u32[]{:S(2)}) collective-permute-start(bf16[1040,128]{1,0:T(8,128)(2,1)S(1)} %place_kv.1), channel_id=1, source_target_pairs={{0,1},{2,3},{4,5},{6,7},{8,9},{10,11},{12,13},{14,15},{16,17},{18,... | collective-permute-start | bytes 798728 | tf_op jit(solution)/shard_map/ppermute | solution.py:369
  40.0 31.8 %collective-permute-start.6 = (bf16[64,1024]{1,0:T(8,128)(2,1)S(1)}, bf16[64,1024]{1,0:T(8,128)(2,1)S(1)}, u32[]{:S(2)}, u32[]{:S(2)}) collective-permute-start(bf16[64,1024]{1,0:T(8,128)(2,1)S(1)} %get-tuple-element.33), channel_id=1, source_target_pairs={{0,22},{2,20},{4,18},{6,16},{8,30},{10,28},{12,26},{14,24},{16,6},... | collective-permute-start | bytes 393224 | tf_op jit(solution)/shard_map/ppermute | solution.py:386
  44.1 27.6 %collective-permute-start.7 = (bf16[64,1024]{1,0:T(8,128)(2,1)S(1)}, bf16[64,1024]{1,0:T(8,128)(2,1)S(1)}, u32[]{:S(2)}, u32[]{:S(2)}) collective-permute-start(bf16[64,1024]{1,0:T(8,128)(2,1)S(1)} %get-tuple-element.35), channel_id=1, source_target_pairs={{0,24},{2,26},{4,28},{6,30},{8,16},{10,18},{12,20},{14,22},{16,8},... | collective-permute-start | bytes 393224 | tf_op jit(solution)/shard_map/ppermute | solution.py:386
  45.1 26.7 %collective-permute-start.8 = (bf16[64,1024]{1,0:T(8,128)(2,1)S(1)}, bf16[64,1024]{1,0:T(8,128)(2,1)S(1)}, u32[]{:S(2)}, u32[]{:S(2)}) collective-permute-start(bf16[64,1024]{1,0:T(8,128)(2,1)S(1)} %get-tuple-element.37), channel_id=1, source_target_pairs={{0,26},{2,24},{4,30},{6,28},{8,18},{10,16},{12,22},{14,20},{16,10}... | collective-permute-start | bytes 393224 | tf_op jit(solution)/shard_map/ppermute | solution.py:386
  52.2 24.1 %collective-permute-start.4 = (bf16[64,1024]{1,0:T(8,128)(2,1)S(1)}, bf16[64,1024]{1,0:T(8,128)(2,1)S(1)}, u32[]{:S(2)}, u32[]{:S(2)}) collective-permute-start(bf16[64,1024]{1,0:T(8,128)(2,1)S(1)} %get-tuple-element.29), channel_id=1, source_target_pairs={{0,28},{2,30},{4,24},{6,26},{8,20},{10,22},{12,16},{14,18},{16,12}... | collective-permute-start | bytes 393224 | tf_op jit(solution)/shard_map/ppermute | solution.py:386
  56.1 20.2 %collective-permute-start.5 = (bf16[64,1024]{1,0:T(8,128)(2,1)S(1)}, bf16[64,1024]{1,0:T(8,128)(2,1)S(1)}, u32[]{:S(2)}, u32[]{:S(2)}) collective-permute-start(bf16[64,1024]{1,0:T(8,128)(2,1)S(1)} %get-tuple-element.31), channel_id=1, source_target_pairs={{0,30},{2,28},{4,26},{6,24},{8,22},{10,20},{12,18},{14,16},{16,14}... | collective-permute-start | bytes 393224 | tf_op jit(solution)/shard_map/ppermute | solution.py:386

commit v4 on v2

--- a/solution.py
+++ b/solution.py
@@ -183,13 +183,14 @@
 
 def attend(meta, first, near, far, own, past, out):
     rows = own[0].shape[0]
-    cap, width = near.shape[1:] if far == [] else far[0].shape
+    cap, width = far[0].shape
     blocks = rows // cap
     heads = width // LANES
     half = rows // 2
     count = past[0].shape[0]
     slots = 0 if near is None else near.shape[0]
     parcels = slots + len(far)
+    lows_at = meta.shape[0] - blocks
     factor = math.log2(math.e) / math.sqrt(LANES)
     arrays = ([] if near is None else [near]) + far
 
@@ -216,11 +217,14 @@
         def place_of(index):
             return meta_ref[1 + first + index]
 
+        def low_of(place):
+            return meta_ref[lows_at + jnp.minimum(place, blocks - 1)]
+
         def result_copy(index):
             at = pl.multiple_of(jnp.minimum(place_of(index), blocks - 1) * cap, cap)
             return pltpu.make_async_copy(result_ref.at[index], out_any.at[pl.ds(at, cap)], sem.at[index])
 
-        def one_block(index, place, lower, with_past):
+        def one_block(index, place, lower, with_low, with_past):
             block_q = stage_ref[index]
             same = qd_ref[pl.ds(pl.multiple_of(place * cap, cap), cap), :]
             same = jnp.concatenate([same] * TOGETHER, axis=0)
@@ -237,7 +241,7 @@
                 tile_qs.append(jnp.concatenate([jnp.concatenate(tiles, axis=0), same], axis=1))
             raws = [[causal(scores(tile_q, keys(ok_ref[last], od_ref[last])))] for tile_q in tile_qs]
             tile_vs = [ov_ref[last]]
-            if lower:
+            if with_low:
                 for several, tile_q in zip(raws, tile_qs):
                     several.append(scores(tile_q, keys(ok_ref[:half], od_ref[:half])))
                 tile_vs.append(ov_ref[:half])
@@ -261,7 +265,8 @@
                         result.append((higher, mixed * decay + mix(raw, higher, values(pv_ref[earlier]))))
                     return result
 
-                mixes = [mixed for _, mixed in lax.fori_loop(0, meta_ref[0], step, list(zip(peaks, mixes)))]
+                least = jnp.maximum(low_of(place) + meta_ref[0] * rows, 0) // rows
+                mixes = [mixed for _, mixed in lax.fori_loop(least, meta_ref[0], step, list(zip(peaks, mixes)))]
             for at, mixed in enumerate(mixes):
                 result = (mixed[:, :LANES] / mixed[:, LANES:]).astype(jnp.bfloat16)
                 for head in range(TOGETHER):
@@ -269,16 +274,19 @@
                     result_ref[index, :, column : column + LANES] = result[head * cap : (head + 1) * cap]
 
         def body(index, carry):
-            place = place_of(index)
-            for lower in (0, 1):
-                here = (place < blocks) & (place >= blocks // 2) if lower else place < blocks // 2
-                if count > 1:
-                    pl.when(here)(functools.partial(one_block, index, place, lower, False))
-                else:
-                    for column in (0, 1):
-                        pl.when(here & (meta_ref[0] == column))(
-                            functools.partial(one_block, index, place, lower, column == 1)
-                        )
+            place, low = place_of(index), low_of(place_of(index))
+            upper = place < blocks // 2
+            lower = (place < blocks) & (place >= blocks // 2)
+            variants = [
+                (upper, 0, False, False),
+                (lower & (low >= half), 1, False, False),
+                (lower & (low < half), 1, True, False),
+            ]
+            if count == 1:
+                variants = [(here & (low >= 0), *what) for here, *what in variants]
+                variants += [(upper & (low < 0), 0, False, True), (lower & (low < 0), 1, True, True)]
+            for here, *what in variants:
+                pl.when(here)(functools.partial(one_block, index, place, *what))
             pl.when(place < blocks)(result_copy(index).start)
             return carry
 
@@ -354,7 +362,7 @@
     every = jnp.arange(owners, dtype=jnp.int32)
     chosen = place[None, :] == slots[:, None]
     source = jnp.sum(jnp.where(chosen, every[None, :], 0), axis=1)
-    senders = jnp.concatenate([me // half * half + every[:half], me ^ every[half:]])
+    senders = jnp.concatenate([me // half * half + every[:half], me ^ jnp.roll(every[half:], 2)])
     places = jnp.sum(jnp.where(senders[:, None] == every[None, :], place[None, :], 0), axis=1)
     wanted = chosen[:, :, None] & (part[None, :, None] == jnp.arange(LANES // cap, dtype=jnp.int32))
     doc = jnp.sum(jnp.where(wanted[..., None], begin[None], 0), axis=(1, 2)).reshape(rows)
@@ -370,22 +378,17 @@
     past_rows = past_kv[:, : 2 * rows].reshape(-1, rows, 2, LANES)
     past = (past_rows[:, :, 0], past_apart, past_rows[:, :, 1])
 
+    lows = jnp.min(doc.reshape(blocks, cap), axis=1) - column * rows
+    meta = jnp.concatenate([column[None], places, lows])
     sent, far = far, []
     for index, parcel in enumerate(sent):
-        if index >= 3:
-            ties = [far[index - 3], own_kv] if index < half - 2 else [past_kv] if index < half - 1 else [far[index - 4], past_kv]
+        if index >= 4:
+            ties = (past_kv,) if index >= half - 2 else (far[index - 4], own_kv)
             parcel = lax.optimization_barrier((parcel, *ties))[0]
         far.append(lax.ppermute(parcel, "dp", [(owner, owner ^ (half + index)) for owner in range(owners)]))
-
-    meta = jnp.concatenate([column[None], places])
-    cuts = [0, half - 5, half - 3, None, half - 3, half - 1, half]
-    out = None
-    for begin, end in zip(cuts[:-1], cuts[1:]):
-        if begin is None:
-            out = attend(meta, 0, near, [], own, past, out)
-        elif end is not None:
-            out = attend(meta, half + begin, None, far[begin:end], own, past, out)
-    return out
+    out = attend(meta, half + 2, None, far[: half - 5], own, past, None)
+    out = attend(meta, half + 2 + half - 5, None, far[half - 5 : half - 2], own, past, out)
+    return attend(meta, 0, near, far[half - 2 :], own, past, out)
 
 
 def solution(mesh):

time: 79.5 us -> 80.4 us (1.011)
  the two profiles are of different devices: /device:TPU:1 before, /device:TPU:13 now
where the time goes in v4:
time: 80.4 us; the launch traced here: 79.9 us
  waiting for transfers between devices  33.2 us (41%)
  starting transfers between devices  23.6 us (29%)
  Pallas kernels  16.4 us (20%)
  local copies, waits for them, and re-layouts  4.41 us (5%)
  other arithmetic  1.98 us (2%)
    all_to_all x1, waiting for transfers between devices, local(): lax.all_to_all(send_kv, 'dp', split_axis=0, concat_axis=0, tiled=True)  18 us
    ppermute x8, starting transfers between devices, local(): lax.ppermute(parcel, 'dp', [(owner, owner ^ half + index) for owner in ra...  11.9 us
    pallas_call x3, Pallas kernels, attend(): pl.pallas_call(kernel, out_shape=jax.ShapeDtypeStruct((rows, width), jnp....  11.2 us
    ppermute x8, waiting for transfers between devices, local(): lax.ppermute(parcel, 'dp', [(owner, owner ^ half + index) for owner in ra...  10.1 us
    all_to_all x1, starting transfers between devices, local(): lax.all_to_all(send_kv, 'dp', split_axis=0, concat_axis=0, tiled=True)  6.59 us
    ppermute x1, waiting for transfers between devices, local(): lax.ppermute(own_kv, 'ctx', [(0, 1)])[None]  5.16 us
    all_to_all x1, starting transfers between devices, local(): lax.all_to_all(near, 'dp', split_axis=0, concat_axis=0, axis_index_groups...  3.84 us
    pallas_call x1, Pallas kernels, pack_q(): pl.pallas_call(kernel, out_shape=[pltpu.HBM((half, cap, width), queries.d...  2.27 us
  transfers between devices with their start and end apart: 11, of which 4 were waited for; matrix products, arithmetic and copies ran while one was open for 6% of the time, Pallas kernels for 10%

profile of v4, /device:TPU:13, one launch (start us, length us, event | category | flops | bytes accessed | tf_op | source)
XLA Modules:
  0.0 79.9 jit_solution(1697572337725736382)
XLA Ops:
  0.0 2.0 %pack_kv.1.earlier_ref = bf16[16,144,128]{2,1,0:T(8,128)(2,1)} custom-call(s32[2,512]{1,0:T(2,128)} %bitcast.19, s32[4,128]{1,0:T(4,128)} %bitcast.22, bf16[1024,128]{1,0:T(8,128)(2,1)} %bitcast.18), custom_call_target="tpu_custom_call" | custom-call | tf_op jit(solution)/shard_map/pack_kv/pallas_call | solution.py:80
  2.0 6.6 %all-to-all-start = ((bf16[16,144,128]{2,1,0:T(8,128)(2,1)}), bf16[16,144,128]{2,1,0:T(8,128)(2,1)S(1)}, u32[]{:S(2)}, u32[]{:S(2)}) async-start(bf16[16,144,128]{2,1,0:T(8,128)(2,1)} %pack_kv.1.earlier_ref), calls=%async_computation | async-start | bytes 1179648 | tf_op jit(solution)/shard_map/all_to_all | solution.py:354
  8.6 2.3 %pack_q.1 = (bf16[8,64,1024]{2,1,0:T(8,128)(2,1)}, bf16[64,1024]{1,0:T(8,128)(2,1)S(1)}, bf16[64,1024]{1,0:T(8,128)(2,1)S(1)}, bf16[64,1024]{1,0:T(8,128)(2,1)S(...) custom-call(s32[2,512]{1,0:T(2,128)} %bitcast.20, ...), custom_call_target="tpu_custom_call" | custom-call | tf_op jit(solution)/shard_map/pack_q/pallas_call | solution.py:132
  10.8 3.2 %collective-permute-start.3 = (bf16[64,1024]{1,0:T(8,128)(2,1)S(1)}, bf16[64,1024]{1,0:T(8,128)(2,1)S(1)}, u32[]{:S(2)}, u32[]{:S(2)}) collective-permute-start(bf16[64,1024]{1,0:T(8,128)(2,1)S(1)} %get-tuple-element.23), channel_id=1, source_target_pairs={{0,22},{2,20},{4,18},{6,16},{8,30},{10,28},{12,26},{14,24},{16,6},... | collective-permute-start | bytes 393224 | tf_op jit(solution)/shard_map/ppermute | solution.py:388
  14.1 0.3 collective-permute-start.4
  14.4 2.4 %collective-permute-start.6 = (bf16[64,1024]{1,0:T(8,128)(2,1)S(1)}, bf16[64,1024]{1,0:T(8,128)(2,1)S(1)}, u32[]{:S(2)}, u32[]{:S(2)}) collective-permute-start(bf16[64,1024]{1,0:T(8,128)(2,1)S(1)} %get-tuple-element.28), channel_id=1, source_target_pairs={{0,18},{2,16},{4,22},{6,20},{8,26},{10,24},{12,30},{14,28},{16,2},... | collective-permute-start | bytes 393224 | tf_op jit(solution)/shard_map/ppermute | solution.py:388
  16.8 0.3 collective-permute-start.8
  17.1 0.1 slice.61
  17.2 0.1 slice.60
  17.3 0.1 add_xor_fusion
  17.3 0.1 pad_add_fusion
  17.4 18.0 %all-to-all-done.in_ref = bf16[16,144,128]{2,1,0:T(8,128)(2,1)S(1)} async-done(((bf16[16,144,128]{2,1,0:T(8,128)(2,1)}), bf16[16,144,128]{2,1,0:T(8,128)(2,1)S(1)}, u32[]{:S(2)}, u32[]{:S(2)}) %all-to-all-start) | async-done | bytes 589856 | tf_op jit(solution)/shard_map/all_to_all | solution.py:354
  35.4 3.8 %all-to-all-start.1 = ((bf16[8,64,1024]{2,1,0:T(8,128)(2,1)}), bf16[8,64,1024]{2,1,0:T(8,128)(2,1)S(1)}, u32[]{:S(2)}, u32[]{:S(2)}) async-start(bf16[8,64,1024]{2,1,0:T(8,128)(2,1)} %get-tuple-element.18), calls=%async_computation.1 | async-start | bytes 2097152 | tf_op jit(solution)/shard_map/all_to_all | solution.py:357
  39.3 0.7 slice_reduce_fusion.1
  40.0 0.1 select_reduce_fusion.2.source_ref
  40.1 0.1 add.112
  40.2 0.1 select_reduce_fusion
  40.3 0.1 reshape.420
  40.4 0.1 broadcast_in_dim_reshape.2
  40.5 1.0 %place_kv.1 = bf16[1040,128]{1,0:T(8,128)(2,1)S(1)} custom-call(s32[8]{0:T(128)S(1)} %select_reduce_fusion.2.source_ref, bf16[16,144,128]{2,1,0:T(8,128)(2,1)S(1)} %all-to-all-done.in_ref, bf16[16,128]{1,0:T(8,128)(2,1)S(1)} %pad.4.begin_ref), custom_call_target="tpu_custom_call" | custom-call | tf_op jit(solution)/shard_map/place_kv/pallas_call | solution.py:173
  41.5 1.3 %collective-permute-start = (bf16[1040,128]{1,0:T(8,128)(2,1)S(1)}, bf16[1040,128]{1,0:T(8,128)(2,1)}, u32[]{:S(2)}, u32[]{:S(2)}) collective-permute-start(bf16[1040,128]{1,0:T(8,128)(2,1)S(1)} %place_kv.1), channel_id=1, source_target_pairs={{0,1},{2,3},{4,5},{6,7},{8,9},{10,11},{12,13},{14,15},{16,17},{18,... | collective-permute-start | bytes 798728 | tf_op jit(solution)/shard_map/ppermute | solution.py:373
  42.8 0.1 reduce_min.9
  43.0 0.4 fusion.6
  43.3 0.0 collective-permute-done.4.rest_0_
  43.3 1.4 %collective-permute-start.5 = (bf16[64,1024]{1,0:T(8,128)(2,1)S(1)}, bf16[64,1024]{1,0:T(8,128)(2,1)S(1)}, u32[]{:S(2)}, u32[]{:S(2)}) collective-permute-start(bf16[64,1024]{1,0:T(8,128)(2,1)S(1)} %get-tuple-element.26), channel_id=1, source_target_pairs={{0,24},{2,26},{4,28},{6,30},{8,16},{10,18},{12,20},{14,22},{16,8},... | collective-permute-start | bytes 393224 | tf_op jit(solution)/shard_map/ppermute | solution.py:388
  44.7 0.0 collective-permute-done.6.rest_1_
  44.7 0.7 collective-permute-start.7
  45.5 0.2 select_convert_fusion.1
  45.7 0.2 select_reduce_fusion.1
  45.9 0.1 pad_add_fusion.1.meta_ref
  46.0 5.2 %collective-permute-done = bf16[1040,128]{1,0:T(8,128)(2,1)} collective-permute-done((bf16[1040,128]{1,0:T(8,128)(2,1)S(1)}, bf16[1040,128]{1,0:T(8,128)(2,1)}, u32[]{:S(2)}, u32[]{:S(2)}) %collective-permute-start) | collective-permute-done | bytes 266272 | tf_op jit(solution)/shard_map/ppermute | solution.py:373
  51.2 1.0 %slice.84 = bf16[1,1024,128]{2,1,0:T(8,128)(2,1)S(1)} slice(bf16[1,1040,128]{2,1,0:T(8,128)(2,1)} %bitcast.7), slice={[0:1], [0:1024], [0:128]} | slice | bytes 524288 | tf_op jit(solution)/shard_map/slice | solution.py:378
  52.1 0.7 convert_convert_fusion.1
  52.8 3.5 %collective-permute-start.2 = (bf16[64,1024]{1,0:T(8,128)(2,1)S(1)}, bf16[64,1024]{1,0:T(8,128)(2,1)S(1)}, u32[]{:S(2)}, u32[]{:S(2)}) collective-permute-start(bf16[64,1024]{1,0:T(8,128)(2,1)S(1)} %get-tuple-element.22), channel_id=1, source_target_pairs={{0,30},{2,28},{4,26},{6,24},{8,22},{10,20},{12,18},{14,16},{16,14}... | collective-permute-start | bytes 393224 | tf_op jit(solution)/shard_map/ppermute | solution.py:388
  56.3 0.4 fusion.5
  56.7 0.0 collective-permute-done.8.rest_2_
  56.7 0.1 collective-permute-start.1
  56.8 0.2 select_convert_fusion.pd_ref
  57.0 2.1 %attend.3.rest_3_ = bf16[512,1024]{1,0:T(8,128)(2,1)} custom-call(s32[25]{0:T(128)S(1)} %pad_add_fusion.1.meta_ref, bf16[512,128]{1,0:T(8,128)(2,1)S(1)} %get-tuple-element.38.qd_ref, bf16[512,128]{1,0:T(8,128)(2,1)S(1)} %get-tuple-element.48.ok_ref, bf16[512,128]{1,0:T(8,128)(2,1)S(1)} %get-tuple-element.37.od_ref, ...), custom_call_target="tpu_custom_call" | custom-call | flops 536870912 | bytes 786432 | tf_op jit(solution)/shard_map/attend/pallas_call | solution.py:311
  59.1 0.0 collective-permute-done.3.rest_0_
  59.1 0.0 collective-permute-done.5.rest_1_
  59.1 0.0 collective-permute-done.7.rest_2_
  59.1 2.3 %attend.4.rest_3_ = bf16[512,1024]{1,0:T(8,128)(2,1)} custom-call(s32[25]{0:T(128)S(1)} %pad_add_fusion.1.meta_ref, bf16[512,128]{1,0:T(8,128)(2,1)S(1)} %get-tuple-element.38.qd_ref, bf16[512,128]{1,0:T(8,128)(2,1)S(1)} %get-tuple-element.48.ok_ref, bf16[512,128]{1,0:T(8,128)(2,1)S(1)} %get-tuple-element.37.od_ref, ...), custom_call_target="tpu_custom_call", output_to_operand_aliasing={{}: (11, {})} | custom-call | flops 536870912 | bytes 786432 | tf_op jit(solution)/shard_map/attend/pallas_call | solution.py:311
  61.4 7.9 %collective-permute-done.2.rest_2_ = bf16[64,1024]{1,0:T(8,128)(2,1)S(1)} collective-permute-done((bf16[64,1024]{1,0:T(8,128)(2,1)S(1)}, bf16[64,1024]{1,0:T(8,128)(2,1)S(1)}, u32[]{:S(2)}, u32[]{:S(2)}) %collective-permute-start.2) | collective-permute-done | bytes 131104 | tf_op jit(solution)/shard_map/ppermute | solution.py:388
  69.3 0.6 copy-done
  69.9 2.2 %collective-permute-done.1.rest_1_ = bf16[64,1024]{1,0:T(8,128)(2,1)S(1)} collective-permute-done((bf16[64,1024]{1,0:T(8,128)(2,1)S(1)}, bf16[64,1024]{1,0:T(8,128)(2,1)S(1)}, u32[]{:S(2)}, u32[]{:S(2)}) %collective-permute-start.1) | collective-permute-done | bytes 131104 | tf_op jit(solution)/shard_map/ppermute | solution.py:388
  72.1 0.9 %copy-done.1 = bf16[64,1024]{1,0:T(8,128)(2,1)S(1)} copy-done((bf16[64,1024]{1,0:T(8,128)(2,1)S(1)}, bf16[64,1024]{1,0:T(8,128)(2,1)}, u32[]{:S(2)}) %copy-start.1) | copy-done | bytes 131096
  73.0 6.9 %attend.5 = bf16[512,1024]{1,0:T(8,128)(2,1)} custom-call(s32[25]{0:T(128)S(1)} %pad_add_fusion.1.meta_ref, bf16[512,128]{1,0:T(8,128)(2,1)S(1)} %get-tuple-element.38.qd_ref, bf16[512,128]{1,0:T(8,128)(2,1)S(1)} %get-tuple-element.48.ok_ref, bf16[512,128]{1,0:T(8,128)(2,1)S(1)} %get-tuple-element.37.od_ref, ...), custom_call_target="tpu_custom_call", output_to_operand_aliasing={{}: (11, {})} | custom-call | flops 2684354560 | bytes 2621440 | tf_op jit(solution)/shard_map/attend/pallas_call | solution.py:311
  (25 shorter events, 0.3 us)
Async XLA Ops:
  2.0 33.4 %all-to-all-start = ((bf16[16,144,128]{2,1,0:T(8,128)(2,1)}), bf16[16,144,128]{2,1,0:T(8,128)(2,1)S(1)}, u32[]{:S(2)}, u32[]{:S(2)}) async-start(bf16[16,144,128]{2,1,0:T(8,128)(2,1)} %pack_kv.1.earlier_ref), calls=%async_computation | async-start | bytes 1179648 | tf_op jit(solution)/shard_map/all_to_all | solution.py:354
  10.8 48.3 %collective-permute-start.3 = (bf16[64,1024]{1,0:T(8,128)(2,1)S(1)}, bf16[64,1024]{1,0:T(8,128)(2,1)S(1)}, u32[]{:S(2)}, u32[]{:S(2)}) collective-permute-start(bf16[64,1024]{1,0:T(8,128)(2,1)S(1)} %get-tuple-element.23), channel_id=1, source_target_pairs={{0,22},{2,20},{4,18},{6,16},{8,30},{10,28},{12,26},{14,24},{16,6},... | collective-permute-start | bytes 393224 | tf_op jit(solution)/shard_map/ppermute | solution.py:388
  14.1 29.3 %collective-permute-start.4 = (bf16[64,1024]{1,0:T(8,128)(2,1)S(1)}, bf16[64,1024]{1,0:T(8,128)(2,1)S(1)}, u32[]{:S(2)}, u32[]{:S(2)}) collective-permute-start(bf16[64,1024]{1,0:T(8,128)(2,1)S(1)} %get-tuple-element.25), channel_id=1, source_target_pairs={{0,16},{2,18},{4,20},{6,22},{8,24},{10,26},{12,28},{14,30},{16,0},... | collective-permute-start | bytes 393224 | tf_op jit(solution)/shard_map/ppermute | solution.py:388
  14.4 30.4 %collective-permute-start.6 = (bf16[64,1024]{1,0:T(8,128)(2,1)S(1)}, bf16[64,1024]{1,0:T(8,128)(2,1)S(1)}, u32[]{:S(2)}, u32[]{:S(2)}) collective-permute-start(bf16[64,1024]{1,0:T(8,128)(2,1)S(1)} %get-tuple-element.28), channel_id=1, source_target_pairs={{0,18},{2,16},{4,22},{6,20},{8,26},{10,24},{12,30},{14,28},{16,2},... | collective-permute-start | bytes 393224 | tf_op jit(solution)/shard_map/ppermute | solution.py:388
  16.8 39.9 %collective-permute-start.8 = (bf16[64,1024]{1,0:T(8,128)(2,1)S(1)}, bf16[64,1024]{1,0:T(8,128)(2,1)S(1)}, u32[]{:S(2)}, u32[]{:S(2)}) collective-permute-start(bf16[64,1024]{1,0:T(8,128)(2,1)S(1)} %get-tuple-element.30), channel_id=1, source_target_pairs={{0,20},{2,22},{4,16},{6,18},{8,28},{10,30},{12,24},{14,26},{16,4},... | collective-permute-start | bytes 393224 | tf_op jit(solution)/shard_map/ppermute | solution.py:388
  35.4 36.7 %all-to-all-start.1 = ((bf16[8,64,1024]{2,1,0:T(8,128)(2,1)}), bf16[8,64,1024]{2,1,0:T(8,128)(2,1)S(1)}, u32[]{:S(2)}, u32[]{:S(2)}) async-start(bf16[8,64,1024]{2,1,0:T(8,128)(2,1)} %get-tuple-element.18), calls=%async_computation.1 | async-start | bytes 2097152 | tf_op jit(solution)/shard_map/all_to_all | solution.py:357
  41.5 9.6 %collective-permute-start = (bf16[1040,128]{1,0:T(8,128)(2,1)S(1)}, bf16[1040,128]{1,0:T(8,128)(2,1)}, u32[]{:S(2)}, u32[]{:S(2)}) collective-permute-start(bf16[1040,128]{1,0:T(8,128)(2,1)S(1)} %place_kv.1), channel_id=1, source_target_pairs={{0,1},{2,3},{4,5},{6,7},{8,9},{10,11},{12,13},{14,15},{16,17},{18,... | collective-permute-start | bytes 798728 | tf_op jit(solution)/shard_map/ppermute | solution.py:373
  43.3 15.8 %collective-permute-start.5 = (bf16[64,1024]{1,0:T(8,128)(2,1)S(1)}, bf16[64,1024]{1,0:T(8,128)(2,1)S(1)}, u32[]{:S(2)}, u32[]{:S(2)}) collective-permute-start(bf16[64,1024]{1,0:T(8,128)(2,1)S(1)} %get-tuple-element.26), channel_id=1, source_target_pairs={{0,24},{2,26},{4,28},{6,30},{8,16},{10,18},{12,20},{14,22},{16,8},... | collective-permute-start | bytes 393224 | tf_op jit(solution)/shard_map/ppermute | solution.py:388
  44.7 14.4 %collective-permute-start.7 = (bf16[64,1024]{1,0:T(8,128)(2,1)S(1)}, bf16[64,1024]{1,0:T(8,128)(2,1)S(1)}, u32[]{:S(2)}, u32[]{:S(2)}) collective-permute-start(bf16[64,1024]{1,0:T(8,128)(2,1)S(1)} %get-tuple-element.29), channel_id=1, source_target_pairs={{0,26},{2,24},{4,30},{6,28},{8,18},{10,16},{12,22},{14,20},{16,10}... | collective-permute-start | bytes 393224 | tf_op jit(solution)/shard_map/ppermute | solution.py:388
  52.8 16.5 %collective-permute-start.2 = (bf16[64,1024]{1,0:T(8,128)(2,1)S(1)}, bf16[64,1024]{1,0:T(8,128)(2,1)S(1)}, u32[]{:S(2)}, u32[]{:S(2)}) collective-permute-start(bf16[64,1024]{1,0:T(8,128)(2,1)S(1)} %get-tuple-element.22), channel_id=1, source_target_pairs={{0,30},{2,28},{4,26},{6,24},{8,22},{10,20},{12,18},{14,16},{16,14}... | collective-permute-start | bytes 393224 | tf_op jit(solution)/shard_map/ppermute | solution.py:388
  56.7 15.4 %collective-permute-start.1 = (bf16[64,1024]{1,0:T(8,128)(2,1)S(1)}, bf16[64,1024]{1,0:T(8,128)(2,1)S(1)}, u32[]{:S(2)}, u32[]{:S(2)}) collective-permute-start(bf16[64,1024]{1,0:T(8,128)(2,1)S(1)} %get-tuple-element.20), channel_id=1, source_target_pairs={{0,28},{2,30},{4,24},{6,26},{8,20},{10,22},{12,16},{14,18},{16,12}... | collective-permute-start | bytes 393224 | tf_op jit(solution)/shard_map/ppermute | solution.py:388
  69.3 0.6 copy-start
  72.1 0.9 %copy-start.1 = (bf16[64,1024]{1,0:T(8,128)(2,1)S(1)}, bf16[64,1024]{1,0:T(8,128)(2,1)}, u32[]{:S(2)}) copy-start(bf16[64,1024]{1,0:T(8,128)(2,1)} %copy-done) | copy-start | bytes 393220

commit v5 on v4

--- a/solution.py
+++ b/solution.py
@@ -183,7 +183,7 @@
 
 def attend(meta, first, near, far, own, past, out):
     rows = own[0].shape[0]
-    cap, width = far[0].shape
+    cap, width = near.shape[1:] if far == [] else far[0].shape
     blocks = rows // cap
     heads = width // LANES
     half = rows // 2
@@ -362,7 +362,7 @@
     every = jnp.arange(owners, dtype=jnp.int32)
     chosen = place[None, :] == slots[:, None]
     source = jnp.sum(jnp.where(chosen, every[None, :], 0), axis=1)
-    senders = jnp.concatenate([me // half * half + every[:half], me ^ jnp.roll(every[half:], 2)])
+    senders = jnp.concatenate([me // half * half + every[:half], me ^ every[half:]])
     places = jnp.sum(jnp.where(senders[:, None] == every[None, :], place[None, :], 0), axis=1)
     wanted = chosen[:, :, None] & (part[None, :, None] == jnp.arange(LANES // cap, dtype=jnp.int32))
     doc = jnp.sum(jnp.where(wanted[..., None], begin[None], 0), axis=(1, 2)).reshape(rows)
@@ -386,9 +386,10 @@
             ties = (past_kv,) if index >= half - 2 else (far[index - 4], own_kv)
             parcel = lax.optimization_barrier((parcel, *ties))[0]
         far.append(lax.ppermute(parcel, "dp", [(owner, owner ^ (half + index)) for owner in range(owners)]))
-    out = attend(meta, half + 2, None, far[: half - 5], own, past, None)
-    out = attend(meta, half + 2 + half - 5, None, far[half - 5 : half - 2], own, past, out)
-    return attend(meta, 0, near, far[half - 2 :], own, past, out)
+    out = attend(meta, half, None, far[: half - 5], own, past, None)
+    out = attend(meta, half + half - 5, None, far[half - 5 : half - 2], own, past, out)
+    out = attend(meta, 0, near, [], own, past, out)
+    return attend(meta, half + half - 2, None, far[half - 2 :], own, past, out)
 
 
 def solution(mesh):

time: 80.4 us -> 77.6 us (0.965)
  the two profiles are of different devices: /device:TPU:13 before, /device:TPU:5 now
where the time goes in v5:
time: 77.6 us; the launch traced here: 76.9 us
  waiting for transfers between devices  28.4 us (37%)
  starting transfers between devices  27.4 us (35%)
  Pallas kernels  16.1 us (21%)
  local copies, waits for them, and re-layouts  2.71 us (3%)
  other arithmetic  1.96 us (3%)
    all_to_all x1, waiting for transfers between devices, local(): lax.all_to_all(send_kv, 'dp', split_axis=0, concat_axis=0, tiled=True)  17.7 us
    ppermute x8, starting transfers between devices, local(): lax.ppermute(parcel, 'dp', [(owner, owner ^ half + index) for owner in ra...  15.3 us
    pallas_call x4, Pallas kernels, attend(): pl.pallas_call(kernel, out_shape=jax.ShapeDtypeStruct((rows, width), jnp....  10.9 us
    all_to_all x1, starting transfers between devices, local(): lax.all_to_all(send_kv, 'dp', split_axis=0, concat_axis=0, tiled=True)  6.5 us
    all_to_all x1, waiting for transfers between devices, local(): lax.all_to_all(near, 'dp', split_axis=0, concat_axis=0, axis_index_groups...  6.16 us
    all_to_all x1, starting transfers between devices, local(): lax.all_to_all(near, 'dp', split_axis=0, concat_axis=0, axis_index_groups...  4.32 us
    ppermute x1, waiting for transfers between devices, local(): lax.ppermute(own_kv, 'ctx', [(0, 1)])[None]  3.79 us
    pallas_call x1, Pallas kernels, pack_q(): pl.pallas_call(kernel, out_shape=[pltpu.HBM((half, cap, width), queries.d...  2.22 us
  transfers between devices with their start and end apart: 11, of which 4 were waited for; matrix products, arithmetic and copies ran while one was open for 6% of the time, Pallas kernels for 15%

profile of v5, /device:TPU:5, one launch (start us, length us, event | category | flops | bytes accessed | tf_op | source)
XLA Modules:
  0.0 76.9 jit_solution(3630920814626781641)
XLA Ops:
  0.0 2.0 %pack_kv.1.earlier_ref = bf16[16,144,128]{2,1,0:T(8,128)(2,1)} custom-call(s32[2,512]{1,0:T(2,128)} %bitcast.19, s32[4,128]{1,0:T(4,128)} %bitcast.22, bf16[1024,128]{1,0:T(8,128)(2,1)} %bitcast.18), custom_call_target="tpu_custom_call" | custom-call | tf_op jit(solution)/shard_map/pack_kv/pallas_call | solution.py:80
  2.0 6.5 %all-to-all-start = ((bf16[16,144,128]{2,1,0:T(8,128)(2,1)}), bf16[16,144,128]{2,1,0:T(8,128)(2,1)S(1)}, u32[]{:S(2)}, u32[]{:S(2)}) async-start(bf16[16,144,128]{2,1,0:T(8,128)(2,1)} %pack_kv.1.earlier_ref), calls=%async_computation | async-start | bytes 1179648 | tf_op jit(solution)/shard_map/all_to_all | solution.py:354
  8.5 2.2 %pack_q.1 = (bf16[8,64,1024]{2,1,0:T(8,128)(2,1)}, bf16[64,1024]{1,0:T(8,128)(2,1)S(1)}, bf16[64,1024]{1,0:T(8,128)(2,1)S(1)}, bf16[64,1024]{1,0:T(8,128)(2,1)S(...) custom-call(s32[2,512]{1,0:T(2,128)} %bitcast.20, ...), custom_call_target="tpu_custom_call" | custom-call | tf_op jit(solution)/shard_map/pack_q/pallas_call | solution.py:132
  10.7 3.5 %collective-permute-start.3 = (bf16[64,1024]{1,0:T(8,128)(2,1)}, bf16[64,1024]{1,0:T(8,128)(2,1)S(1)}, u32[]{:S(2)}, u32[]{:S(2)}) collective-permute-start(bf16[64,1024]{1,0:T(8,128)(2,1)} %get-tuple-element.23), channel_id=1, source_target_pairs={{0,22},{2,20},{4,18},{6,16},{8,30},{10,28},{12,26},{14,24},{16,6},... | collective-permute-start | bytes 393224 | tf_op jit(solution)/shard_map/ppermute | solution.py:388
  14.2 0.3 collective-permute-start.4
  14.5 2.4 %collective-permute-start.6 = (bf16[64,1024]{1,0:T(8,128)(2,1)S(1)}, bf16[64,1024]{1,0:T(8,128)(2,1)S(1)}, u32[]{:S(2)}, u32[]{:S(2)}) collective-permute-start(bf16[64,1024]{1,0:T(8,128)(2,1)S(1)} %get-tuple-element.28), channel_id=1, source_target_pairs={{0,18},{2,16},{4,22},{6,20},{8,26},{10,24},{12,30},{14,28},{16,2},... | collective-permute-start | bytes 393224 | tf_op jit(solution)/shard_map/ppermute | solution.py:388
  16.9 0.1 collective-permute-start.8
  17.0 0.1 slice_xor_fusion
  17.0 0.1 pad_add_fusion
  17.1 17.7 %all-to-all-done.in_ref = bf16[16,144,128]{2,1,0:T(8,128)(2,1)S(1)} async-done(((bf16[16,144,128]{2,1,0:T(8,128)(2,1)}), bf16[16,144,128]{2,1,0:T(8,128)(2,1)S(1)}, u32[]{:S(2)}, u32[]{:S(2)}) %all-to-all-start) | async-done | bytes 589856 | tf_op jit(solution)/shard_map/all_to_all | solution.py:354
  34.8 4.3 %all-to-all-start.1 = ((bf16[8,64,1024]{2,1,0:T(8,128)(2,1)}), bf16[8,64,1024]{2,1,0:T(8,128)(2,1)S(1)}, u32[]{:S(2)}, u32[]{:S(2)}) async-start(bf16[8,64,1024]{2,1,0:T(8,128)(2,1)} %get-tuple-element.22), calls=%async_computation.1 | async-start | bytes 2097152 | tf_op jit(solution)/shard_map/all_to_all | solution.py:357
  39.2 0.7 slice_reduce_fusion.1
  39.9 0.1 select_reduce_fusion.2.source_ref
  40.0 0.1 add.112
  40.1 0.1 select_reduce_fusion
  40.2 0.1 reshape.420
  40.3 0.1 broadcast_in_dim_reshape.2
  40.4 1.0 %place_kv.1 = bf16[1040,128]{1,0:T(8,128)(2,1)S(1)} custom-call(s32[8]{0:T(128)S(1)} %select_reduce_fusion.2.source_ref, bf16[16,144,128]{2,1,0:T(8,128)(2,1)S(1)} %all-to-all-done.in_ref, bf16[16,128]{1,0:T(8,128)(2,1)S(1)} %pad.4.begin_ref), custom_call_target="tpu_custom_call" | custom-call | tf_op jit(solution)/shard_map/place_kv/pallas_call | solution.py:173
  41.4 1.3 %collective-permute-start = (bf16[1040,128]{1,0:T(8,128)(2,1)S(1)}, bf16[1040,128]{1,0:T(8,128)(2,1)}, u32[]{:S(2)}, u32[]{:S(2)}) collective-permute-start(bf16[1040,128]{1,0:T(8,128)(2,1)S(1)} %place_kv.1), channel_id=1, source_target_pairs={{0,1},{2,3},{4,5},{6,7},{8,9},{10,11},{12,13},{14,15},{16,17},{18,... | collective-permute-start | bytes 798728 | tf_op jit(solution)/shard_map/ppermute | solution.py:373
  42.7 0.1 reduce_min.9
  42.9 0.4 fusion.6
  43.2 0.0 collective-permute-done.4.rest_0_
  43.2 3.6 %collective-permute-start.5 = (bf16[64,1024]{1,0:T(8,128)(2,1)S(1)}, bf16[64,1024]{1,0:T(8,128)(2,1)S(1)}, u32[]{:S(2)}, u32[]{:S(2)}) collective-permute-start(bf16[64,1024]{1,0:T(8,128)(2,1)S(1)} %get-tuple-element.26), channel_id=1, source_target_pairs={{0,24},{2,26},{4,28},{6,30},{8,16},{10,18},{12,20},{14,22},{16,8},... | collective-permute-start | bytes 393224 | tf_op jit(solution)/shard_map/ppermute | solution.py:388
  46.8 0.0 collective-permute-done.6.rest_1_
  46.8 0.3 collective-permute-start.7
  47.2 0.2 select_convert_fusion.1
  47.4 0.2 select_reduce_fusion.1
  47.6 0.1 pad_add_fusion.1.meta_ref
  47.7 3.8 %collective-permute-done = bf16[1040,128]{1,0:T(8,128)(2,1)} collective-permute-done((bf16[1040,128]{1,0:T(8,128)(2,1)S(1)}, bf16[1040,128]{1,0:T(8,128)(2,1)}, u32[]{:S(2)}, u32[]{:S(2)}) %collective-permute-start) | collective-permute-done | bytes 266272 | tf_op jit(solution)/shard_map/ppermute | solution.py:373
  51.5 1.0 %slice.75 = bf16[1,1024,128]{2,1,0:T(8,128)(2,1)S(1)} slice(bf16[1,1040,128]{2,1,0:T(8,128)(2,1)} %bitcast.7), slice={[0:1], [0:1024], [0:128]} | slice | bytes 524288 | tf_op jit(solution)/shard_map/slice | solution.py:378
  52.4 0.7 convert_convert_fusion.1
  53.1 5.1 %collective-permute-start.2 = (bf16[64,1024]{1,0:T(8,128)(2,1)S(1)}, bf16[64,1024]{1,0:T(8,128)(2,1)S(1)}, u32[]{:S(2)}, u32[]{:S(2)}) collective-permute-start(bf16[64,1024]{1,0:T(8,128)(2,1)S(1)} %get-tuple-element.21), channel_id=1, source_target_pairs={{0,30},{2,28},{4,26},{6,24},{8,22},{10,20},{12,18},{14,16},{16,14}... | collective-permute-start | bytes 393224 | tf_op jit(solution)/shard_map/ppermute | solution.py:388
  58.2 0.4 fusion.5
  58.6 0.2 select_convert_fusion.pd_ref
  58.9 0.0 collective-permute-done.8.rest_2_
  58.9 0.1 collective-permute-start.1
  58.9 1.8 %attend.4.rest_3_ = bf16[512,1024]{1,0:T(8,128)(2,1)} custom-call(s32[25]{0:T(128)S(1)} %pad_add_fusion.1.meta_ref, bf16[512,128]{1,0:T(8,128)(2,1)S(1)} %get-tuple-element.38.qd_ref, bf16[512,128]{1,0:T(8,128)(2,1)S(1)} %get-tuple-element.48.ok_ref, bf16[512,128]{1,0:T(8,128)(2,1)S(1)} %get-tuple-element.37.od_ref, ...), custom_call_target="tpu_custom_call" | custom-call | flops 536870912 | bytes 786432 | tf_op jit(solution)/shard_map/attend/pallas_call | solution.py:311
  60.8 0.0 collective-permute-done.3.rest_0_
  60.8 0.0 collective-permute-done.5.rest_1_
  60.8 0.7 collective-permute-done.7.rest_2_
  61.5 2.1 %attend.5.rest_1_ = bf16[512,1024]{1,0:T(8,128)(2,1)} custom-call(s32[25]{0:T(128)S(1)} %pad_add_fusion.1.meta_ref, bf16[512,128]{1,0:T(8,128)(2,1)S(1)} %get-tuple-element.38.qd_ref, bf16[512,128]{1,0:T(8,128)(2,1)S(1)} %get-tuple-element.48.ok_ref, bf16[512,128]{1,0:T(8,128)(2,1)S(1)} %get-tuple-element.37.od_ref, ...), custom_call_target="tpu_custom_call", output_to_operand_aliasing={{}: (11, {})} | custom-call | flops 536870912 | bytes 786432 | tf_op jit(solution)/shard_map/attend/pallas_call | solution.py:311
  63.7 6.2 %all-to-all-done.1.rest_0_ = bf16[8,64,1024]{2,1,0:T(8,128)(2,1)S(1)} async-done(((bf16[8,64,1024]{2,1,0:T(8,128)(2,1)}), bf16[8,64,1024]{2,1,0:T(8,128)(2,1)S(1)}, u32[]{:S(2)}, u32[]{:S(2)}) %all-to-all-start.1) | async-done | bytes 1048608 | tf_op jit(solution)/shard_map/all_to_all | solution.py:357
  69.8 4.7 %attend.6.rest_2_ = bf16[512,1024]{1,0:T(8,128)(2,1)} custom-call(s32[25]{0:T(128)S(1)} %pad_add_fusion.1.meta_ref, bf16[512,128]{1,0:T(8,128)(2,1)S(1)} %get-tuple-element.38.qd_ref, bf16[512,128]{1,0:T(8,128)(2,1)S(1)} %get-tuple-element.48.ok_ref, bf16[512,128]{1,0:T(8,128)(2,1)S(1)} %get-tuple-element.37.od_ref, ...), custom_call_target="tpu_custom_call", output_to_operand_aliasing={{}: (9, {})} | custom-call | flops 2147483648 | bytes 2097152 | tf_op jit(solution)/shard_map/attend/pallas_call | solution.py:311
  74.5 0.0 collective-permute-done.2.rest_1_
  74.5 0.0 collective-permute-done.1.rest_0_
  74.5 2.3 %attend.7 = bf16[512,1024]{1,0:T(8,128)(2,1)} custom-call(s32[25]{0:T(128)S(1)} %pad_add_fusion.1.meta_ref, bf16[512,128]{1,0:T(8,128)(2,1)S(1)} %get-tuple-element.38.qd_ref, bf16[512,128]{1,0:T(8,128)(2,1)S(1)} %get-tuple-element.48.ok_ref, bf16[512,128]{1,0:T(8,128)(2,1)S(1)} %get-tuple-element.37.od_ref, ...), custom_call_target="tpu_custom_call", output_to_operand_aliasing={{}: (10, {})} | custom-call | flops 536870912 | bytes 524288 | tf_op jit(solution)/shard_map/attend/pallas_call | solution.py:311
  (21 shorter events, 0.2 us)
Async XLA Ops:
  2.0 32.9 %all-to-all-start = ((bf16[16,144,128]{2,1,0:T(8,128)(2,1)}), bf16[16,144,128]{2,1,0:T(8,128)(2,1)S(1)}, u32[]{:S(2)}, u32[]{:S(2)}) async-start(bf16[16,144,128]{2,1,0:T(8,128)(2,1)} %pack_kv.1.earlier_ref), calls=%async_computation | async-start | bytes 1179648 | tf_op jit(solution)/shard_map/all_to_all | solution.py:354
  10.7 50.1 %collective-permute-start.3 = (bf16[64,1024]{1,0:T(8,128)(2,1)}, bf16[64,1024]{1,0:T(8,128)(2,1)S(1)}, u32[]{:S(2)}, u32[]{:S(2)}) collective-permute-start(bf16[64,1024]{1,0:T(8,128)(2,1)} %get-tuple-element.23), channel_id=1, source_target_pairs={{0,22},{2,20},{4,18},{6,16},{8,30},{10,28},{12,26},{14,24},{16,6},... | collective-permute-start | bytes 393224 | tf_op jit(solution)/shard_map/ppermute | solution.py:388
  14.2 29.0 %collective-permute-start.4 = (bf16[64,1024]{1,0:T(8,128)(2,1)S(1)}, bf16[64,1024]{1,0:T(8,128)(2,1)S(1)}, u32[]{:S(2)}, u32[]{:S(2)}) collective-permute-start(bf16[64,1024]{1,0:T(8,128)(2,1)S(1)} %get-tuple-element.25), channel_id=1, source_target_pairs={{0,16},{2,18},{4,20},{6,22},{8,24},{10,26},{12,28},{14,30},{16,0},... | collective-permute-start | bytes 393224 | tf_op jit(solution)/shard_map/ppermute | solution.py:388
  14.5 32.3 %collective-permute-start.6 = (bf16[64,1024]{1,0:T(8,128)(2,1)S(1)}, bf16[64,1024]{1,0:T(8,128)(2,1)S(1)}, u32[]{:S(2)}, u32[]{:S(2)}) collective-permute-start(bf16[64,1024]{1,0:T(8,128)(2,1)S(1)} %get-tuple-element.28), channel_id=1, source_target_pairs={{0,18},{2,16},{4,22},{6,20},{8,26},{10,24},{12,30},{14,28},{16,2},... | collective-permute-start | bytes 393224 | tf_op jit(solution)/shard_map/ppermute | solution.py:388
  16.9 42.0 %collective-permute-start.8 = (bf16[64,1024]{1,0:T(8,128)(2,1)S(1)}, bf16[64,1024]{1,0:T(8,128)(2,1)S(1)}, u32[]{:S(2)}, u32[]{:S(2)}) collective-permute-start(bf16[64,1024]{1,0:T(8,128)(2,1)S(1)} %get-tuple-element.30), channel_id=1, source_target_pairs={{0,20},{2,22},{4,16},{6,18},{8,28},{10,30},{12,24},{14,26},{16,4},... | collective-permute-start | bytes 393224 | tf_op jit(solution)/shard_map/ppermute | solution.py:388
  34.8 35.0 %all-to-all-start.1 = ((bf16[8,64,1024]{2,1,0:T(8,128)(2,1)}), bf16[8,64,1024]{2,1,0:T(8,128)(2,1)S(1)}, u32[]{:S(2)}, u32[]{:S(2)}) async-start(bf16[8,64,1024]{2,1,0:T(8,128)(2,1)} %get-tuple-element.22), calls=%async_computation.1 | async-start | bytes 2097152 | tf_op jit(solution)/shard_map/all_to_all | solution.py:357
  41.4 10.0 %collective-permute-start = (bf16[1040,128]{1,0:T(8,128)(2,1)S(1)}, bf16[1040,128]{1,0:T(8,128)(2,1)}, u32[]{:S(2)}, u32[]{:S(2)}) collective-permute-start(bf16[1040,128]{1,0:T(8,128)(2,1)S(1)} %place_kv.1), channel_id=1, source_target_pairs={{0,1},{2,3},{4,5},{6,7},{8,9},{10,11},{12,13},{14,15},{16,17},{18,... | collective-permute-start | bytes 798728 | tf_op jit(solution)/shard_map/ppermute | solution.py:373
  43.2 17.5 %collective-permute-start.5 = (bf16[64,1024]{1,0:T(8,128)(2,1)S(1)}, bf16[64,1024]{1,0:T(8,128)(2,1)S(1)}, u32[]{:S(2)}, u32[]{:S(2)}) collective-permute-start(bf16[64,1024]{1,0:T(8,128)(2,1)S(1)} %get-tuple-element.26), channel_id=1, source_target_pairs={{0,24},{2,26},{4,28},{6,30},{8,16},{10,18},{12,20},{14,22},{16,8},... | collective-permute-start | bytes 393224 | tf_op jit(solution)/shard_map/ppermute | solution.py:388
  46.8 14.7 %collective-permute-start.7 = (bf16[64,1024]{1,0:T(8,128)(2,1)S(1)}, bf16[64,1024]{1,0:T(8,128)(2,1)S(1)}, u32[]{:S(2)}, u32[]{:S(2)}) collective-permute-start(bf16[64,1024]{1,0:T(8,128)(2,1)S(1)} %get-tuple-element.29), channel_id=1, source_target_pairs={{0,26},{2,24},{4,30},{6,28},{8,18},{10,16},{12,22},{14,20},{16,10}... | collective-permute-start | bytes 393224 | tf_op jit(solution)/shard_map/ppermute | solution.py:388
  53.1 21.4 %collective-permute-start.2 = (bf16[64,1024]{1,0:T(8,128)(2,1)S(1)}, bf16[64,1024]{1,0:T(8,128)(2,1)S(1)}, u32[]{:S(2)}, u32[]{:S(2)}) collective-permute-start(bf16[64,1024]{1,0:T(8,128)(2,1)S(1)} %get-tuple-element.21), channel_id=1, source_target_pairs={{0,30},{2,28},{4,26},{6,24},{8,22},{10,20},{12,18},{14,16},{16,14}... | collective-permute-start | bytes 393224 | tf_op jit(solution)/shard_map/ppermute | solution.py:388
  58.9 15.6 %collective-permute-start.1 = (bf16[64,1024]{1,0:T(8,128)(2,1)S(1)}, bf16[64,1024]{1,0:T(8,128)(2,1)S(1)}, u32[]{:S(2)}, u32[]{:S(2)}) collective-permute-start(bf16[64,1024]{1,0:T(8,128)(2,1)S(1)} %get-tuple-element.19), channel_id=1, source_target_pairs={{0,28},{2,30},{4,24},{6,26},{8,20},{10,22},{12,16},{14,18},{16,12}... | collective-permute-start | bytes 393224 | tf_op jit(solution)/shard_map/ppermute | solution.py:388

commit v6 on v5

--- a/solution.py
+++ b/solution.py
@@ -196,7 +196,7 @@
 
     def kernel(meta_ref, qd_ref, ok_ref, od_ref, ov_ref, pk_ref, pd_ref, pv_ref, *rest):
         array_refs = rest[: len(arrays)]
-        out_any, stage_ref, result_ref, sem = rest[-4:]
+        out_any, stage_ref, result_ref, list_ref, sem = rest[-5:]
 
         def keys(k_ref, d_ref):
             return jnp.concatenate([k_ref, d_ref], axis=1)
@@ -224,27 +224,22 @@
             at = pl.multiple_of(jnp.minimum(place_of(index), blocks - 1) * cap, cap)
             return pltpu.make_async_copy(result_ref.at[index], out_any.at[pl.ds(at, cap)], sem.at[index])
 
-        def one_block(index, place, lower, with_low, with_past):
-            block_q = stage_ref[index]
-            same = qd_ref[pl.ds(pl.multiple_of(place * cap, cap), cap), :]
-            same = jnp.concatenate([same] * TOGETHER, axis=0)
-            row_at = lax.broadcasted_iota(jnp.int32, (cap, half), 0) + (place * cap - lower * half)
-            seen = lax.broadcasted_iota(jnp.int32, (cap, half), 1) <= row_at
-            last = pl.ds(lower * half, half)
-
-            def causal(raw):
-                return jnp.where(seen[None], raw.reshape(TOGETHER, cap, half), NEVER).reshape(TOGETHER * cap, half)
-
-            tile_qs = []
-            for begin in range(0, heads, TOGETHER):
-                tiles = [block_q[:, head * LANES : (head + 1) * LANES] for head in range(begin, begin + TOGETHER)]
-                tile_qs.append(jnp.concatenate([jnp.concatenate(tiles, axis=0), same], axis=1))
-            raws = [[causal(scores(tile_q, keys(ok_ref[last], od_ref[last])))] for tile_q in tile_qs]
-            tile_vs = [ov_ref[last]]
-            if with_low:
-                for several, tile_q in zip(raws, tile_qs):
-                    several.append(scores(tile_q, keys(ok_ref[:half], od_ref[:half])))
-                tile_vs.append(ov_ref[:half])
+        def some_blocks(indices, places, seen_keys, with_past):
+            tile_qs, raws = [], []
+            for index, place in zip(indices, places):
+                block_q = stage_ref[index]
+                same = qd_ref[pl.ds(pl.multiple_of(place * cap, cap), cap), :]
+                same = jnp.concatenate([same] * TOGETHER, axis=0)
+                row_at = lax.broadcasted_iota(jnp.int32, (cap, seen_keys), 0) + place * cap
+                seen = lax.broadcasted_iota(jnp.int32, (cap, seen_keys), 1) <= row_at
+                for begin in range(0, heads, TOGETHER):
+                    tiles = [block_q[:, head * LANES : (head + 1) * LANES] for head in range(begin, begin + TOGETHER)]
+                    tile_q = jnp.concatenate([jnp.concatenate(tiles, axis=0), same], axis=1)
+                    raw = scores(tile_q, keys(ok_ref[:seen_keys], od_ref[:seen_keys]))
+                    raw = jnp.where(seen[None], raw.reshape(TOGETHER, cap, seen_keys), NEVER)
+                    tile_qs.append(tile_q)
+                    raws.append([raw.reshape(TOGETHER * cap, seen_keys)])
+            tile_vs = [ov_ref[:seen_keys]]
             if with_past:
                 for several, tile_q in zip(raws, tile_qs):
                     several.append(scores(tile_q, keys(pk_ref[0], pd_ref[0])))
@@ -265,30 +260,36 @@
                         result.append((higher, mixed * decay + mix(raw, higher, values(pv_ref[earlier]))))
                     return result
 
-                least = jnp.maximum(low_of(place) + meta_ref[0] * rows, 0) // rows
+                low = functools.reduce(jnp.minimum, [low_of(place) for place in places])
+                least = jnp.maximum(low + meta_ref[0] * rows, 0) // rows
                 mixes = [mixed for _, mixed in lax.fori_loop(least, meta_ref[0], step, list(zip(peaks, mixes)))]
+            groups = heads // TOGETHER
             for at, mixed in enumerate(mixes):
                 result = (mixed[:, :LANES] / mixed[:, LANES:]).astype(jnp.bfloat16)
                 for head in range(TOGETHER):
-                    column = (at * TOGETHER + head) * LANES
-                    result_ref[index, :, column : column + LANES] = result[head * cap : (head + 1) * cap]
-
-        def body(index, carry):
-            place, low = place_of(index), low_of(place_of(index))
-            upper = place < blocks // 2
-            lower = (place < blocks) & (place >= blocks // 2)
-            variants = [
-                (upper, 0, False, False),
-                (lower & (low >= half), 1, False, False),
-                (lower & (low < half), 1, True, False),
-            ]
-            if count == 1:
-                variants = [(here & (low >= 0), *what) for here, *what in variants]
-                variants += [(upper & (low < 0), 0, False, True), (lower & (low < 0), 1, True, True)]
-            for here, *what in variants:
-                pl.when(here)(functools.partial(one_block, index, place, *what))
-            pl.when(place < blocks)(result_copy(index).start)
+                    column = (at % groups * TOGETHER + head) * LANES
+                    result_ref[indices[at // groups], :, column : column + LANES] = result[head * cap : (head + 1) * cap]
+
+        def body(pair, carry):
+            indices = [list_ref[2 * pair], list_ref[2 * pair + 1]]
+            places = [place_of(index) for index in indices]
+            low = jnp.minimum(*[low_of(place) for place in places])
+            short = jnp.maximum(*places) < blocks // 2
+            for seen_keys, here in ((half, short), (rows, jnp.logical_not(short))):
+                if count > 1:
+                    pl.when(here)(functools.partial(some_blocks, indices, places, seen_keys, False))
+                else:
+                    pl.when(here & (low >= 0))(functools.partial(some_blocks, indices, places, seen_keys, False))
+                    pl.when(here & (low < 0))(functools.partial(some_blocks, indices, places, seen_keys, True))
+            result_copy(indices[0]).start()
+            pl.when(indices[0] != indices[1])(result_copy(indices[1]).start)
             return carry
+
+        held = jnp.int32(0)
+        for index in range(parcels):
+            list_ref[held] = index
+            held += jnp.where(place_of(index) < blocks, 1, 0)
+        list_ref[held] = list_ref[jnp.maximum(held - 1, 0)]
 
         for index in range(parcels):
 
@@ -296,7 +297,7 @@
             def _():
                 stage_ref[index] = array_refs[0][index] if index < slots else array_refs[index - slots + (slots > 0)][...]
 
-        lax.fori_loop(0, parcels, body, 0)
+        lax.fori_loop(0, (held + 1) // 2, body, 0)
         for index in range(parcels):
             pl.when(place_of(index) < blocks)(result_copy(index).wait)
 
@@ -317,6 +318,7 @@
         scratch_shapes=[
             pltpu.VMEM((parcels, cap, width), jnp.bfloat16),
             pltpu.VMEM((parcels, cap, width), jnp.bfloat16),
+            pltpu.SMEM((parcels + 1,), jnp.int32),
             pltpu.SemaphoreType.DMA((parcels,)),
         ],
         compiler_params=params(28),

time: 77.6 us -> 78 us (level); the launches traced: 76.9 us -> 76.5 us
  waiting for transfers between devices: 28.4 us -> 26.7 us
  Pallas kernels: 16.1 us -> 17.3 us
    pallas_call x4, Pallas kernels: 10.9 us -> 12 us  [attend(): pl.pallas_call(kernel, out_shape=jax.ShapeDtypeStruct((rows, width), jnp....]
    all_to_all x1, waiting for transfers between devices: 6.16 us -> 5.17 us  [local(): lax.all_to_all(near, 'dp', split_axis=0, concat_axis=0, axis_index_groups...]
  transfers between devices with their start and end apart: 11 -> 11, of which waited for: 4 -> 4; matrix products, arithmetic and copies ran while one was open for 6% -> 6% of each run, Pallas kernels for 15% -> 17%
where the time goes in v6:
time: 78 us; the launch traced here: 76.5 us
  starting transfers between devices  27.5 us (35%)
  waiting for transfers between devices  26.7 us (34%)
  Pallas kernels  17.3 us (22%)
  local copies, waits for them, and re-layouts  2.71 us (3%)
  other arithmetic  1.96 us (3%)
    all_to_all x1, waiting for transfers between devices, local(): lax.all_to_all(send_kv, 'dp', split_axis=0, concat_axis=0, tiled=True)  17.5 us
    ppermute x8, starting transfers between devices, local(): lax.ppermute(parcel, 'dp', [(owner, owner ^ half + index) for owner in ra...  15.3 us
    pallas_call x4, Pallas kernels, attend(): pl.pallas_call(kernel, out_shape=jax.ShapeDtypeStruct((rows, width), jnp....  12 us
    all_to_all x1, starting transfers between devices, local(): lax.all_to_all(send_kv, 'dp', split_axis=0, concat_axis=0, tiled=True)  6.5 us
    all_to_all x1, waiting for transfers between devices, local(): lax.all_to_all(near, 'dp', split_axis=0, concat_axis=0, axis_index_groups...  5.17 us
    all_to_all x1, starting transfers between devices, local(): lax.all_to_all(near, 'dp', split_axis=0, concat_axis=0, axis_index_groups...  4.32 us
    ppermute x1, waiting for transfers between devices, local(): lax.ppermute(own_kv, 'ctx', [(0, 1)])[None]  3.79 us
    pallas_call x1, Pallas kernels, pack_q(): pl.pallas_call(kernel, out_shape=[pltpu.HBM((half, cap, width), queries.d...  2.41 us
  transfers between devices with their start and end apart: 11, of which 4 were waited for; matrix products, arithmetic and copies ran while one was open for 6% of the time, Pallas kernels for 17%

profile of v6, /device:TPU:5, one launch (start us, length us, event | category | flops | bytes accessed | tf_op | source)
XLA Modules:
  0.0 76.5 jit_solution(17674649043825862648)
XLA Ops:
  0.0 2.0 %pack_kv.1.earlier_ref = bf16[16,144,128]{2,1,0:T(8,128)(2,1)} custom-call(s32[2,512]{1,0:T(2,128)} %bitcast.19, s32[4,128]{1,0:T(4,128)} %bitcast.22, bf16[1024,128]{1,0:T(8,128)(2,1)} %bitcast.18), custom_call_target="tpu_custom_call" | custom-call | tf_op jit(solution)/shard_map/pack_kv/pallas_call | solution.py:80
  2.0 6.5 %all-to-all-start = ((bf16[16,144,128]{2,1,0:T(8,128)(2,1)}), bf16[16,144,128]{2,1,0:T(8,128)(2,1)S(1)}, u32[]{:S(2)}, u32[]{:S(2)}) async-start(bf16[16,144,128]{2,1,0:T(8,128)(2,1)} %pack_kv.1.earlier_ref), calls=%async_computation | async-start | bytes 1179648 | tf_op jit(solution)/shard_map/all_to_all | solution.py:356
  8.5 2.4 %pack_q.1 = (bf16[8,64,1024]{2,1,0:T(8,128)(2,1)}, bf16[64,1024]{1,0:T(8,128)(2,1)S(1)}, bf16[64,1024]{1,0:T(8,128)(2,1)S(1)}, bf16[64,1024]{1,0:T(8,128)(2,1)S(...) custom-call(s32[2,512]{1,0:T(2,128)} %bitcast.20, ...), custom_call_target="tpu_custom_call" | custom-call | tf_op jit(solution)/shard_map/pack_q/pallas_call | solution.py:132
  10.9 3.3 %collective-permute-start.3 = (bf16[64,1024]{1,0:T(8,128)(2,1)}, bf16[64,1024]{1,0:T(8,128)(2,1)S(1)}, u32[]{:S(2)}, u32[]{:S(2)}) collective-permute-start(bf16[64,1024]{1,0:T(8,128)(2,1)} %get-tuple-element.23), channel_id=1, source_target_pairs={{0,22},{2,20},{4,18},{6,16},{8,30},{10,28},{12,26},{14,24},{16,6},... | collective-permute-start | bytes 393224 | tf_op jit(solution)/shard_map/ppermute | solution.py:390
  14.2 0.3 collective-permute-start.4
  14.5 2.4 %collective-permute-start.6 = (bf16[64,1024]{1,0:T(8,128)(2,1)S(1)}, bf16[64,1024]{1,0:T(8,128)(2,1)S(1)}, u32[]{:S(2)}, u32[]{:S(2)}) collective-permute-start(bf16[64,1024]{1,0:T(8,128)(2,1)S(1)} %get-tuple-element.28), channel_id=1, source_target_pairs={{0,18},{2,16},{4,22},{6,20},{8,26},{10,24},{12,30},{14,28},{16,2},... | collective-permute-start | bytes 393224 | tf_op jit(solution)/shard_map/ppermute | solution.py:390
  16.9 0.3 collective-permute-start.8
  17.2 0.1 slice_xor_fusion
  17.3 0.1 pad_add_fusion
  17.4 17.5 %all-to-all-done.in_ref = bf16[16,144,128]{2,1,0:T(8,128)(2,1)S(1)} async-done(((bf16[16,144,128]{2,1,0:T(8,128)(2,1)}), bf16[16,144,128]{2,1,0:T(8,128)(2,1)S(1)}, u32[]{:S(2)}, u32[]{:S(2)}) %all-to-all-start) | async-done | bytes 589856 | tf_op jit(solution)/shard_map/all_to_all | solution.py:356
  34.8 4.3 %all-to-all-start.1 = ((bf16[8,64,1024]{2,1,0:T(8,128)(2,1)}), bf16[8,64,1024]{2,1,0:T(8,128)(2,1)S(1)}, u32[]{:S(2)}, u32[]{:S(2)}) async-start(bf16[8,64,1024]{2,1,0:T(8,128)(2,1)} %get-tuple-element.22), calls=%async_computation.1 | async-start | bytes 2097152 | tf_op jit(solution)/shard_map/all_to_all | solution.py:359
  39.2 0.7 slice_reduce_fusion.1
  39.9 0.1 select_reduce_fusion.2.source_ref
  40.0 0.1 add.112
  40.1 0.1 select_reduce_fusion
  40.2 0.1 reshape.420
  40.3 0.1 broadcast_in_dim_reshape.2
  40.4 1.0 %place_kv.1 = bf16[1040,128]{1,0:T(8,128)(2,1)S(1)} custom-call(s32[8]{0:T(128)S(1)} %select_reduce_fusion.2.source_ref, bf16[16,144,128]{2,1,0:T(8,128)(2,1)S(1)} %all-to-all-done.in_ref, bf16[16,128]{1,0:T(8,128)(2,1)S(1)} %pad.4.begin_ref), custom_call_target="tpu_custom_call" | custom-call | tf_op jit(solution)/shard_map/place_kv/pallas_call | solution.py:173
  41.4 1.3 %collective-permute-start = (bf16[1040,128]{1,0:T(8,128)(2,1)S(1)}, bf16[1040,128]{1,0:T(8,128)(2,1)}, u32[]{:S(2)}, u32[]{:S(2)}) collective-permute-start(bf16[1040,128]{1,0:T(8,128)(2,1)S(1)} %place_kv.1), channel_id=1, source_target_pairs={{0,1},{2,3},{4,5},{6,7},{8,9},{10,11},{12,13},{14,15},{16,17},{18,... | collective-permute-start | bytes 798728 | tf_op jit(solution)/shard_map/ppermute | solution.py:375
  42.7 0.1 reduce_min.9
  42.9 0.4 fusion.6
  43.2 0.0 collective-permute-done.4.rest_0_
  43.2 3.6 %collective-permute-start.5 = (bf16[64,1024]{1,0:T(8,128)(2,1)S(1)}, bf16[64,1024]{1,0:T(8,128)(2,1)S(1)}, u32[]{:S(2)}, u32[]{:S(2)}) collective-permute-start(bf16[64,1024]{1,0:T(8,128)(2,1)S(1)} %get-tuple-element.26), channel_id=1, source_target_pairs={{0,24},{2,26},{4,28},{6,30},{8,16},{10,18},{12,20},{14,22},{16,8},... | collective-permute-start | bytes 393224 | tf_op jit(solution)/shard_map/ppermute | solution.py:390
  46.8 0.0 collective-permute-done.6.rest_1_
  46.8 0.3 collective-permute-start.7
  47.2 0.2 select_convert_fusion.1
  47.4 0.2 select_reduce_fusion.1
  47.6 0.1 pad_add_fusion.1.meta_ref
  47.7 3.8 %collective-permute-done = bf16[1040,128]{1,0:T(8,128)(2,1)} collective-permute-done((bf16[1040,128]{1,0:T(8,128)(2,1)S(1)}, bf16[1040,128]{1,0:T(8,128)(2,1)}, u32[]{:S(2)}, u32[]{:S(2)}) %collective-permute-start) | collective-permute-done | bytes 266272 | tf_op jit(solution)/shard_map/ppermute | solution.py:375
  51.5 1.0 %slice.75 = bf16[1,1024,128]{2,1,0:T(8,128)(2,1)S(1)} slice(bf16[1,1040,128]{2,1,0:T(8,128)(2,1)} %bitcast.7), slice={[0:1], [0:1024], [0:128]} | slice | bytes 524288 | tf_op jit(solution)/shard_map/slice | solution.py:380
  52.4 0.7 convert_convert_fusion.1
  53.1 5.1 %collective-permute-start.2 = (bf16[64,1024]{1,0:T(8,128)(2,1)S(1)}, bf16[64,1024]{1,0:T(8,128)(2,1)S(1)}, u32[]{:S(2)}, u32[]{:S(2)}) collective-permute-start(bf16[64,1024]{1,0:T(8,128)(2,1)S(1)} %get-tuple-element.21), channel_id=1, source_target_pairs={{0,30},{2,28},{4,26},{6,24},{8,22},{10,20},{12,18},{14,16},{16,14}... | collective-permute-start | bytes 393224 | tf_op jit(solution)/shard_map/ppermute | solution.py:390
  58.2 0.4 fusion.5
  58.6 0.2 select_convert_fusion.pd_ref
  58.9 0.0 collective-permute-done.8.rest_2_
  58.9 0.1 collective-permute-start.1
  58.9 2.3 %attend.4.rest_3_ = bf16[512,1024]{1,0:T(8,128)(2,1)} custom-call(s32[25]{0:T(128)S(1)} %pad_add_fusion.1.meta_ref, bf16[512,128]{1,0:T(8,128)(2,1)S(1)} %get-tuple-element.38.qd_ref, bf16[512,128]{1,0:T(8,128)(2,1)S(1)} %get-tuple-element.48.ok_ref, bf16[512,128]{1,0:T(8,128)(2,1)S(1)} %get-tuple-element.37.od_ref, ...), custom_call_target="tpu_custom_call" | custom-call | flops 536870912 | bytes 786432 | tf_op jit(solution)/shard_map/attend/pallas_call | solution.py:312
  61.3 0.0 collective-permute-done.3.rest_0_
  61.3 0.0 collective-permute-done.5.rest_1_
  61.3 0.2 collective-permute-done.7.rest_2_
  61.5 3.1 %attend.5.rest_1_ = bf16[512,1024]{1,0:T(8,128)(2,1)} custom-call(s32[25]{0:T(128)S(1)} %pad_add_fusion.1.meta_ref, bf16[512,128]{1,0:T(8,128)(2,1)S(1)} %get-tuple-element.38.qd_ref, bf16[512,128]{1,0:T(8,128)(2,1)S(1)} %get-tuple-element.48.ok_ref, bf16[512,128]{1,0:T(8,128)(2,1)S(1)} %get-tuple-element.37.od_ref, ...), custom_call_target="tpu_custom_call", output_to_operand_aliasing={{}: (11, {})} | custom-call | flops 536870912 | bytes 786432 | tf_op jit(solution)/shard_map/attend/pallas_call | solution.py:312
  64.6 5.2 %all-to-all-done.1.rest_0_ = bf16[8,64,1024]{2,1,0:T(8,128)(2,1)S(1)} async-done(((bf16[8,64,1024]{2,1,0:T(8,128)(2,1)}), bf16[8,64,1024]{2,1,0:T(8,128)(2,1)S(1)}, u32[]{:S(2)}, u32[]{:S(2)}) %all-to-all-start.1) | async-done | bytes 1048608 | tf_op jit(solution)/shard_map/all_to_all | solution.py:359
  69.8 4.2 %attend.6.rest_2_ = bf16[512,1024]{1,0:T(8,128)(2,1)} custom-call(s32[25]{0:T(128)S(1)} %pad_add_fusion.1.meta_ref, bf16[512,128]{1,0:T(8,128)(2,1)S(1)} %get-tuple-element.38.qd_ref, bf16[512,128]{1,0:T(8,128)(2,1)S(1)} %get-tuple-element.48.ok_ref, bf16[512,128]{1,0:T(8,128)(2,1)S(1)} %get-tuple-element.37.od_ref, ...), custom_call_target="tpu_custom_call", output_to_operand_aliasing={{}: (9, {})} | custom-call | flops 2147483648 | bytes 2097152 | tf_op jit(solution)/shard_map/attend/pallas_call | solution.py:312
  74.1 0.0 collective-permute-done.2.rest_1_
  74.1 0.0 collective-permute-done.1.rest_0_
  74.1 2.3 %attend.7 = bf16[512,1024]{1,0:T(8,128)(2,1)} custom-call(s32[25]{0:T(128)S(1)} %pad_add_fusion.1.meta_ref, bf16[512,128]{1,0:T(8,128)(2,1)S(1)} %get-tuple-element.38.qd_ref, bf16[512,128]{1,0:T(8,128)(2,1)S(1)} %get-tuple-element.48.ok_ref, bf16[512,128]{1,0:T(8,128)(2,1)S(1)} %get-tuple-element.37.od_ref, ...), custom_call_target="tpu_custom_call", output_to_operand_aliasing={{}: (10, {})} | custom-call | flops 536870912 | bytes 524288 | tf_op jit(solution)/shard_map/attend/pallas_call | solution.py:312
  (21 shorter events, 0.2 us)
Async XLA Ops:
  2.0 32.9 %all-to-all-start = ((bf16[16,144,128]{2,1,0:T(8,128)(2,1)}), bf16[16,144,128]{2,1,0:T(8,128)(2,1)S(1)}, u32[]{:S(2)}, u32[]{:S(2)}) async-start(bf16[16,144,128]{2,1,0:T(8,128)(2,1)} %pack_kv.1.earlier_ref), calls=%async_computation | async-start | bytes 1179648 | tf_op jit(solution)/shard_map/all_to_all | solution.py:356
  10.9 50.4 %collective-permute-start.3 = (bf16[64,1024]{1,0:T(8,128)(2,1)}, bf16[64,1024]{1,0:T(8,128)(2,1)S(1)}, u32[]{:S(2)}, u32[]{:S(2)}) collective-permute-start(bf16[64,1024]{1,0:T(8,128)(2,1)} %get-tuple-element.23), channel_id=1, source_target_pairs={{0,22},{2,20},{4,18},{6,16},{8,30},{10,28},{12,26},{14,24},{16,6},... | collective-permute-start | bytes 393224 | tf_op jit(solution)/shard_map/ppermute | solution.py:390
  14.2 29.0 %collective-permute-start.4 = (bf16[64,1024]{1,0:T(8,128)(2,1)S(1)}, bf16[64,1024]{1,0:T(8,128)(2,1)S(1)}, u32[]{:S(2)}, u32[]{:S(2)}) collective-permute-start(bf16[64,1024]{1,0:T(8,128)(2,1)S(1)} %get-tuple-element.25), channel_id=1, source_target_pairs={{0,16},{2,18},{4,20},{6,22},{8,24},{10,26},{12,28},{14,30},{16,0},... | collective-permute-start | bytes 393224 | tf_op jit(solution)/shard_map/ppermute | solution.py:390
  14.5 32.3 %collective-permute-start.6 = (bf16[64,1024]{1,0:T(8,128)(2,1)S(1)}, bf16[64,1024]{1,0:T(8,128)(2,1)S(1)}, u32[]{:S(2)}, u32[]{:S(2)}) collective-permute-start(bf16[64,1024]{1,0:T(8,128)(2,1)S(1)} %get-tuple-element.28), channel_id=1, source_target_pairs={{0,18},{2,16},{4,22},{6,20},{8,26},{10,24},{12,30},{14,28},{16,2},... | collective-permute-start | bytes 393224 | tf_op jit(solution)/shard_map/ppermute | solution.py:390
  16.9 42.0 %collective-permute-start.8 = (bf16[64,1024]{1,0:T(8,128)(2,1)S(1)}, bf16[64,1024]{1,0:T(8,128)(2,1)S(1)}, u32[]{:S(2)}, u32[]{:S(2)}) collective-permute-start(bf16[64,1024]{1,0:T(8,128)(2,1)S(1)} %get-tuple-element.30), channel_id=1, source_target_pairs={{0,20},{2,22},{4,16},{6,18},{8,28},{10,30},{12,24},{14,26},{16,4},... | collective-permute-start | bytes 393224 | tf_op jit(solution)/shard_map/ppermute | solution.py:390
  34.8 35.0 %all-to-all-start.1 = ((bf16[8,64,1024]{2,1,0:T(8,128)(2,1)}), bf16[8,64,1024]{2,1,0:T(8,128)(2,1)S(1)}, u32[]{:S(2)}, u32[]{:S(2)}) async-start(bf16[8,64,1024]{2,1,0:T(8,128)(2,1)} %get-tuple-element.22), calls=%async_computation.1 | async-start | bytes 2097152 | tf_op jit(solution)/shard_map/all_to_all | solution.py:359
  41.4 10.0 %collective-permute-start = (bf16[1040,128]{1,0:T(8,128)(2,1)S(1)}, bf16[1040,128]{1,0:T(8,128)(2,1)}, u32[]{:S(2)}, u32[]{:S(2)}) collective-permute-start(bf16[1040,128]{1,0:T(8,128)(2,1)S(1)} %place_kv.1), channel_id=1, source_target_pairs={{0,1},{2,3},{4,5},{6,7},{8,9},{10,11},{12,13},{14,15},{16,17},{18,... | collective-permute-start | bytes 798728 | tf_op jit(solution)/shard_map/ppermute | solution.py:375
  43.2 18.0 %collective-permute-start.5 = (bf16[64,1024]{1,0:T(8,128)(2,1)S(1)}, bf16[64,1024]{1,0:T(8,128)(2,1)S(1)}, u32[]{:S(2)}, u32[]{:S(2)}) collective-permute-start(bf16[64,1024]{1,0:T(8,128)(2,1)S(1)} %get-tuple-element.26), channel_id=1, source_target_pairs={{0,24},{2,26},{4,28},{6,30},{8,16},{10,18},{12,20},{14,22},{16,8},... | collective-permute-start | bytes 393224 | tf_op jit(solution)/shard_map/ppermute | solution.py:390
  46.8 14.7 %collective-permute-start.7 = (bf16[64,1024]{1,0:T(8,128)(2,1)S(1)}, bf16[64,1024]{1,0:T(8,128)(2,1)S(1)}, u32[]{:S(2)}, u32[]{:S(2)}) collective-permute-start(bf16[64,1024]{1,0:T(8,128)(2,1)S(1)} %get-tuple-element.29), channel_id=1, source_target_pairs={{0,26},{2,24},{4,30},{6,28},{8,18},{10,16},{12,22},{14,20},{16,10}... | collective-permute-start | bytes 393224 | tf_op jit(solution)/shard_map/ppermute | solution.py:390
  53.1 20.9 %collective-permute-start.2 = (bf16[64,1024]{1,0:T(8,128)(2,1)S(1)}, bf16[64,1024]{1,0:T(8,128)(2,1)S(1)}, u32[]{:S(2)}, u32[]{:S(2)}) collective-permute-start(bf16[64,1024]{1,0:T(8,128)(2,1)S(1)} %get-tuple-element.21), channel_id=1, source_target_pairs={{0,30},{2,28},{4,26},{6,24},{8,22},{10,20},{12,18},{14,16},{16,14}... | collective-permute-start | bytes 393224 | tf_op jit(solution)/shard_map/ppermute | solution.py:390
  58.9 15.2 %collective-permute-start.1 = (bf16[64,1024]{1,0:T(8,128)(2,1)S(1)}, bf16[64,1024]{1,0:T(8,128)(2,1)S(1)}, u32[]{:S(2)}, u32[]{:S(2)}) collective-permute-start(bf16[64,1024]{1,0:T(8,128)(2,1)S(1)} %get-tuple-element.19), channel_id=1, source_target_pairs={{0,28},{2,30},{4,24},{6,26},{8,20},{10,22},{12,16},{14,18},{16,12}... | collective-permute-start | bytes 393224 | tf_op jit(solution)/shard_map/ppermute | solution.py:390

commit v7 on v6

--- a/solution.py
+++ b/solution.py
@@ -384,8 +384,8 @@
     meta = jnp.concatenate([column[None], places, lows])
     sent, far = far, []
     for index, parcel in enumerate(sent):
-        if index >= 4:
-            ties = (past_kv,) if index >= half - 2 else (far[index - 4], own_kv)
+        if index >= 3:
+            ties = (past_kv,) if index >= half - 2 else (far[index - 3], own_kv)
             parcel = lax.optimization_barrier((parcel, *ties))[0]
         far.append(lax.ppermute(parcel, "dp", [(owner, owner ^ (half + index)) for owner in range(owners)]))
     out = attend(meta, half, None, far[: half - 5], own, past, None)

time: 78 us -> 79.2 us (1.015)
  the two profiles are of different devices: /device:TPU:5 before, /device:TPU:22 now
where the time goes in v7:
time: 79.2 us; the launch traced here: 78.5 us
  waiting for transfers between devices  34 us (43%)
  starting transfers between devices  20.9 us (26%)
  Pallas kernels  17.7 us (22%)
  local copies, waits for them, and re-layouts  3.42 us (4%)
  other arithmetic  1.99 us (3%)
    all_to_all x1, waiting for transfers between devices, local(): lax.all_to_all(send_kv, 'dp', split_axis=0, concat_axis=0, tiled=True)  17 us
    pallas_call x4, Pallas kernels, attend(): pl.pallas_call(kernel, out_shape=jax.ShapeDtypeStruct((rows, width), jnp....  12.5 us
    ppermute x8, waiting for transfers between devices, local(): lax.ppermute(parcel, 'dp', [(owner, owner ^ half + index) for owner in ra...  12 us
    ppermute x8, starting transfers between devices, local(): lax.ppermute(parcel, 'dp', [(owner, owner ^ half + index) for owner in ra...  7.73 us
    all_to_all x1, starting transfers between devices, local(): lax.all_to_all(send_kv, 'dp', split_axis=0, concat_axis=0, tiled=True)  6.14 us
    all_to_all x1, starting transfers between devices, local(): lax.all_to_all(near, 'dp', split_axis=0, concat_axis=0, axis_index_groups...  5.74 us
    ppermute x1, waiting for transfers between devices, local(): lax.ppermute(own_kv, 'ctx', [(0, 1)])[None]  5.07 us
    pallas_call x1, Pallas kernels, pack_q(): pl.pallas_call(kernel, out_shape=[pltpu.HBM((half, cap, width), queries.d...  2.24 us
  transfers between devices with their start and end apart: 11, of which 4 were waited for; matrix products, arithmetic and copies ran while one was open for 6% of the time, Pallas kernels for 16%

profile of v7, /device:TPU:22, one launch (start us, length us, event | category | flops | bytes accessed | tf_op | source)
XLA Modules:
  0.0 78.5 jit_solution(6279566178920472731)
XLA Ops:
  0.0 2.0 %pack_kv.1.earlier_ref = bf16[16,144,128]{2,1,0:T(8,128)(2,1)} custom-call(s32[2,512]{1,0:T(2,128)} %bitcast.21, s32[4,128]{1,0:T(4,128)} %bitcast.24, bf16[1024,128]{1,0:T(8,128)(2,1)} %bitcast.20), custom_call_target="tpu_custom_call" | custom-call | tf_op jit(solution)/shard_map/pack_kv/pallas_call | solution.py:80
  2.0 6.1 %all-to-all-start = ((bf16[16,144,128]{2,1,0:T(8,128)(2,1)}), bf16[16,144,128]{2,1,0:T(8,128)(2,1)S(1)}, u32[]{:S(2)}, u32[]{:S(2)}) async-start(bf16[16,144,128]{2,1,0:T(8,128)(2,1)} %pack_kv.1.earlier_ref), calls=%async_computation | async-start | bytes 1179648 | tf_op jit(solution)/shard_map/all_to_all | solution.py:356
  8.1 2.2 %pack_q.1 = (bf16[8,64,1024]{2,1,0:T(8,128)(2,1)}, bf16[64,1024]{1,0:T(8,128)(2,1)S(1)}, bf16[64,1024]{1,0:T(8,128)(2,1)S(1)}, bf16[64,1024]{1,0:T(8,128)(2,1)S(...) custom-call(s32[2,512]{1,0:T(2,128)} %bitcast.22, ...), custom_call_target="tpu_custom_call" | custom-call | tf_op jit(solution)/shard_map/pack_q/pallas_call | solution.py:132
  10.3 0.6 collective-permute-start.3
  11.0 1.8 %collective-permute-start.5 = (bf16[64,1024]{1,0:T(8,128)(2,1)S(1)}, bf16[64,1024]{1,0:T(8,128)(2,1)S(1)}, u32[]{:S(2)}, u32[]{:S(2)}) collective-permute-start(bf16[64,1024]{1,0:T(8,128)(2,1)S(1)} %get-tuple-element.28), channel_id=1, source_target_pairs={{0,18},{2,16},{4,22},{6,20},{8,26},{10,24},{12,30},{14,28},{16,2},... | collective-permute-start | bytes 393224 | tf_op jit(solution)/shard_map/ppermute | solution.py:390
  12.8 0.5 collective-permute-start.7
  13.4 0.1 slice_xor_fusion
  13.4 0.1 pad_add_fusion
  13.5 17.0 %all-to-all-done.in_ref = bf16[16,144,128]{2,1,0:T(8,128)(2,1)S(1)} async-done(((bf16[16,144,128]{2,1,0:T(8,128)(2,1)}), bf16[16,144,128]{2,1,0:T(8,128)(2,1)S(1)}, u32[]{:S(2)}, u32[]{:S(2)}) %all-to-all-start) | async-done | bytes 589856 | tf_op jit(solution)/shard_map/all_to_all | solution.py:356
  30.5 5.7 %all-to-all-start.1 = ((bf16[8,64,1024]{2,1,0:T(8,128)(2,1)}), bf16[8,64,1024]{2,1,0:T(8,128)(2,1)S(1)}, u32[]{:S(2)}, u32[]{:S(2)}) async-start(bf16[8,64,1024]{2,1,0:T(8,128)(2,1)} %get-tuple-element.23), calls=%async_computation.1 | async-start | bytes 2097152 | tf_op jit(solution)/shard_map/all_to_all | solution.py:359
  36.3 0.7 slice_reduce_fusion.1
  37.0 0.1 add.112
  37.1 0.1 select_reduce_fusion
  37.2 0.1 reshape.420
  37.4 0.1 broadcast_in_dim_reshape.2
  37.4 0.1 select_reduce_fusion.2.source_ref
  37.5 1.0 %place_kv.1 = bf16[1040,128]{1,0:T(8,128)(2,1)S(1)} custom-call(s32[8]{0:T(128)S(1)} %select_reduce_fusion.2.source_ref, bf16[16,144,128]{2,1,0:T(8,128)(2,1)S(1)} %all-to-all-done.in_ref, bf16[16,128]{1,0:T(8,128)(2,1)S(1)} %pad.4.begin_ref), custom_call_target="tpu_custom_call" | custom-call | tf_op jit(solution)/shard_map/place_kv/pallas_call | solution.py:173
  38.6 1.3 %collective-permute-start = (bf16[1040,128]{1,0:T(8,128)(2,1)S(1)}, bf16[1040,128]{1,0:T(8,128)(2,1)S(1)}, u32[]{:S(2)}, u32[]{:S(2)}) collective-permute-start(bf16[1040,128]{1,0:T(8,128)(2,1)S(1)} %place_kv.1), channel_id=1, source_target_pairs={{0,1},{2,3},{4,5},{6,7},{8,9},{10,11},{12,13},{14,15},{16,17},{18,... | collective-permute-start | bytes 798728 | tf_op jit(solution)/shard_map/ppermute | solution.py:375
  39.9 0.1 reduce_min.9
  40.0 0.0 collective-permute-done.3.rest_0_
  40.0 0.1 collective-permute-start.4
  40.1 0.4 fusion.6
  40.5 0.0 collective-permute-done.5.rest_1_
  40.5 2.8 %collective-permute-start.6 = (bf16[64,1024]{1,0:T(8,128)(2,1)S(1)}, bf16[64,1024]{1,0:T(8,128)(2,1)S(1)}, u32[]{:S(2)}, u32[]{:S(2)}) collective-permute-start(bf16[64,1024]{1,0:T(8,128)(2,1)S(1)} %get-tuple-element.29), channel_id=1, source_target_pairs={{0,24},{2,26},{4,28},{6,30},{8,16},{10,18},{12,20},{14,22},{16,8},... | collective-permute-start | bytes 393224 | tf_op jit(solution)/shard_map/ppermute | solution.py:390
  43.2 0.0 collective-permute-done.7.rest_2_
  43.2 0.1 collective-permute-start.8
  43.3 0.2 select_convert_fusion.1
  43.5 0.2 select_reduce_fusion.1
  43.7 0.1 pad_add_fusion.1.meta_ref
  43.9 5.1 %collective-permute-done = bf16[1040,128]{1,0:T(8,128)(2,1)S(1)} collective-permute-done((bf16[1040,128]{1,0:T(8,128)(2,1)S(1)}, bf16[1040,128]{1,0:T(8,128)(2,1)S(1)}, u32[]{:S(2)}, u32[]{:S(2)}) %collective-permute-start) | collective-permute-done | bytes 266272 | tf_op jit(solution)/shard_map/ppermute | solution.py:375
  48.9 0.0 copy-start
  48.9 0.7 copy-done
  49.6 1.0 %slice.75 = bf16[1,1024,128]{2,1,0:T(8,128)(2,1)S(1)} slice(bf16[1,1040,128]{2,1,0:T(8,128)(2,1)} %bitcast.18), slice={[0:1], [0:1024], [0:128]} | slice | bytes 524288 | tf_op jit(solution)/shard_map/slice | solution.py:380
  50.6 0.7 convert_convert_fusion.1
  51.3 0.0 collective-permute-start.2
  51.3 1.8 %collective-permute-start.1 = (bf16[64,1024]{1,0:T(8,128)(2,1)S(1)}, bf16[64,1024]{1,0:T(8,128)(2,1)S(1)}, u32[]{:S(2)}, u32[]{:S(2)}) collective-permute-start(bf16[64,1024]{1,0:T(8,128)(2,1)S(1)} %get-tuple-element.20), channel_id=1, source_target_pairs={{0,28},{2,30},{4,24},{6,26},{8,20},{10,22},{12,16},{14,18},{16,12}... | collective-permute-start | bytes 393224 | tf_op jit(solution)/shard_map/ppermute | solution.py:390
  53.2 0.4 fusion.5
  53.6 0.2 select_convert_fusion.pd_ref
  53.8 0.6 attend.4.rest_3_
  54.4 0.0 collective-permute-done.4.rest_0_
  54.4 9.8 %collective-permute-done.6.rest_1_ = bf16[64,1024]{1,0:T(8,128)(2,1)S(1)} collective-permute-done((bf16[64,1024]{1,0:T(8,128)(2,1)S(1)}, bf16[64,1024]{1,0:T(8,128)(2,1)S(1)}, u32[]{:S(2)}, u32[]{:S(2)}) %collective-permute-start.6) | collective-permute-done | bytes 131104 | tf_op jit(solution)/shard_map/ppermute | solution.py:390
  64.2 2.2 %collective-permute-done.8.rest_2_ = bf16[64,1024]{1,0:T(8,128)(2,1)S(1)} collective-permute-done((bf16[64,1024]{1,0:T(8,128)(2,1)S(1)}, bf16[64,1024]{1,0:T(8,128)(2,1)S(1)}, u32[]{:S(2)}, u32[]{:S(2)}) %collective-permute-start.8) | collective-permute-done | bytes 131104 | tf_op jit(solution)/shard_map/ppermute | solution.py:390
  66.4 2.9 %attend.5.rest_1_ = bf16[512,1024]{1,0:T(8,128)(2,1)} custom-call(s32[25]{0:T(128)S(1)} %pad_add_fusion.1.meta_ref, bf16[512,128]{1,0:T(8,128)(2,1)S(1)} %get-tuple-element.40.qd_ref, bf16[512,128]{1,0:T(8,128)(2,1)S(1)} %get-tuple-element.50.ok_ref, bf16[512,128]{1,0:T(8,128)(2,1)S(1)} %get-tuple-element.39.od_ref, ...), custom_call_target="tpu_custom_call", output_to_operand_aliasing={{}: (11, {})} | custom-call | flops 536870912 | bytes 786432 | tf_op jit(solution)/shard_map/attend/pallas_call | solution.py:312
  69.3 0.0 all-to-all-done.1.rest_0_
  69.3 6.1 %attend.6.rest_2_ = bf16[512,1024]{1,0:T(8,128)(2,1)} custom-call(s32[25]{0:T(128)S(1)} %pad_add_fusion.1.meta_ref, bf16[512,128]{1,0:T(8,128)(2,1)S(1)} %get-tuple-element.40.qd_ref, bf16[512,128]{1,0:T(8,128)(2,1)S(1)} %get-tuple-element.50.ok_ref, bf16[512,128]{1,0:T(8,128)(2,1)S(1)} %get-tuple-element.39.od_ref, ...), custom_call_target="tpu_custom_call", output_to_operand_aliasing={{}: (9, {})} | custom-call | flops 2147483648 | bytes 2097152 | tf_op jit(solution)/shard_map/attend/pallas_call | solution.py:312
  75.4 0.0 collective-permute-done.2.rest_1_
  75.4 0.0 collective-permute-done.1.rest_0_
  75.4 2.9 %attend.7 = bf16[512,1024]{1,0:T(8,128)(2,1)} custom-call(s32[25]{0:T(128)S(1)} %pad_add_fusion.1.meta_ref, bf16[512,128]{1,0:T(8,128)(2,1)S(1)} %get-tuple-element.40.qd_ref, bf16[512,128]{1,0:T(8,128)(2,1)S(1)} %get-tuple-element.50.ok_ref, bf16[512,128]{1,0:T(8,128)(2,1)S(1)} %get-tuple-element.39.od_ref, ...), custom_call_target="tpu_custom_call", output_to_operand_aliasing={{}: (10, {})} | custom-call | flops 536870912 | bytes 524288 | tf_op jit(solution)/shard_map/attend/pallas_call | solution.py:312
  (21 shorter events, 0.3 us)
Async XLA Ops:
  2.0 28.6 %all-to-all-start = ((bf16[16,144,128]{2,1,0:T(8,128)(2,1)}), bf16[16,144,128]{2,1,0:T(8,128)(2,1)S(1)}, u32[]{:S(2)}, u32[]{:S(2)}) async-start(bf16[16,144,128]{2,1,0:T(8,128)(2,1)} %pack_kv.1.earlier_ref), calls=%async_computation | async-start | bytes 1179648 | tf_op jit(solution)/shard_map/all_to_all | solution.py:356
  10.3 29.6 %collective-permute-start.3 = (bf16[64,1024]{1,0:T(8,128)(2,1)S(1)}, bf16[64,1024]{1,0:T(8,128)(2,1)S(1)}, u32[]{:S(2)}, u32[]{:S(2)}) collective-permute-start(bf16[64,1024]{1,0:T(8,128)(2,1)S(1)} %get-tuple-element.25), channel_id=1, source_target_pairs={{0,16},{2,18},{4,20},{6,22},{8,24},{10,26},{12,28},{14,30},{16,0},... | collective-permute-start | bytes 393224 | tf_op jit(solution)/shard_map/ppermute | solution.py:390
  11.0 29.5 %collective-permute-start.5 = (bf16[64,1024]{1,0:T(8,128)(2,1)S(1)}, bf16[64,1024]{1,0:T(8,128)(2,1)S(1)}, u32[]{:S(2)}, u32[]{:S(2)}) collective-permute-start(bf16[64,1024]{1,0:T(8,128)(2,1)S(1)} %get-tuple-element.28), channel_id=1, source_target_pairs={{0,18},{2,16},{4,22},{6,20},{8,26},{10,24},{12,30},{14,28},{16,2},... | collective-permute-start | bytes 393224 | tf_op jit(solution)/shard_map/ppermute | solution.py:390
  12.8 30.4 %collective-permute-start.7 = (bf16[64,1024]{1,0:T(8,128)(2,1)S(1)}, bf16[64,1024]{1,0:T(8,128)(2,1)S(1)}, u32[]{:S(2)}, u32[]{:S(2)}) collective-permute-start(bf16[64,1024]{1,0:T(8,128)(2,1)S(1)} %get-tuple-element.31), channel_id=1, source_target_pairs={{0,20},{2,22},{4,16},{6,18},{8,28},{10,30},{12,24},{14,26},{16,4},... | collective-permute-start | bytes 393224 | tf_op jit(solution)/shard_map/ppermute | solution.py:390
  30.5 38.8 %all-to-all-start.1 = ((bf16[8,64,1024]{2,1,0:T(8,128)(2,1)}), bf16[8,64,1024]{2,1,0:T(8,128)(2,1)S(1)}, u32[]{:S(2)}, u32[]{:S(2)}) async-start(bf16[8,64,1024]{2,1,0:T(8,128)(2,1)} %get-tuple-element.23), calls=%async_computation.1 | async-start | bytes 2097152 | tf_op jit(solution)/shard_map/all_to_all | solution.py:359
  38.6 10.3 %collective-permute-start = (bf16[1040,128]{1,0:T(8,128)(2,1)S(1)}, bf16[1040,128]{1,0:T(8,128)(2,1)S(1)}, u32[]{:S(2)}, u32[]{:S(2)}) collective-permute-start(bf16[1040,128]{1,0:T(8,128)(2,1)S(1)} %place_kv.1), channel_id=1, source_target_pairs={{0,1},{2,3},{4,5},{6,7},{8,9},{10,11},{12,13},{14,15},{16,17},{18,... | collective-permute-start | bytes 798728 | tf_op jit(solution)/shard_map/ppermute | solution.py:375
  40.0 14.4 %collective-permute-start.4 = (bf16[64,1024]{1,0:T(8,128)(2,1)}, bf16[64,1024]{1,0:T(8,128)(2,1)S(1)}, u32[]{:S(2)}, u32[]{:S(2)}) collective-permute-start(bf16[64,1024]{1,0:T(8,128)(2,1)} %get-tuple-element.26), channel_id=1, source_target_pairs={{0,22},{2,20},{4,18},{6,16},{8,30},{10,28},{12,26},{14,24},{16,6},... | collective-permute-start | bytes 393224 | tf_op jit(solution)/shard_map/ppermute | solution.py:390
  40.5 23.7 %collective-permute-start.6 = (bf16[64,1024]{1,0:T(8,128)(2,1)S(1)}, bf16[64,1024]{1,0:T(8,128)(2,1)S(1)}, u32[]{:S(2)}, u32[]{:S(2)}) collective-permute-start(bf16[64,1024]{1,0:T(8,128)(2,1)S(1)} %get-tuple-element.29), channel_id=1, source_target_pairs={{0,24},{2,26},{4,28},{6,30},{8,16},{10,18},{12,20},{14,22},{16,8},... | collective-permute-start | bytes 393224 | tf_op jit(solution)/shard_map/ppermute | solution.py:390
  43.2 23.1 %collective-permute-start.8 = (bf16[64,1024]{1,0:T(8,128)(2,1)S(1)}, bf16[64,1024]{1,0:T(8,128)(2,1)S(1)}, u32[]{:S(2)}, u32[]{:S(2)}) collective-permute-start(bf16[64,1024]{1,0:T(8,128)(2,1)S(1)} %get-tuple-element.32), channel_id=1, source_target_pairs={{0,26},{2,24},{4,30},{6,28},{8,18},{10,16},{12,22},{14,20},{16,10}... | collective-permute-start | bytes 393224 | tf_op jit(solution)/shard_map/ppermute | solution.py:390
  48.9 0.7 copy-start
  51.3 24.1 %collective-permute-start.2 = (bf16[64,1024]{1,0:T(8,128)(2,1)S(1)}, bf16[64,1024]{1,0:T(8,128)(2,1)S(1)}, u32[]{:S(2)}, u32[]{:S(2)}) collective-permute-start(bf16[64,1024]{1,0:T(8,128)(2,1)S(1)} %get-tuple-element.22), channel_id=1, source_target_pairs={{0,30},{2,28},{4,26},{6,24},{8,22},{10,20},{12,18},{14,16},{16,14}... | collective-permute-start | bytes 393224 | tf_op jit(solution)/shard_map/ppermute | solution.py:390
  51.3 24.1 %collective-permute-start.1 = (bf16[64,1024]{1,0:T(8,128)(2,1)S(1)}, bf16[64,1024]{1,0:T(8,128)(2,1)S(1)}, u32[]{:S(2)}, u32[]{:S(2)}) collective-permute-start(bf16[64,1024]{1,0:T(8,128)(2,1)S(1)} %get-tuple-element.20), channel_id=1, source_target_pairs={{0,28},{2,30},{4,24},{6,26},{8,20},{10,22},{12,16},{14,18},{16,12}... | collective-permute-start | bytes 393224 | tf_op jit(solution)/shard_map/ppermute | solution.py:390

commit v8 on v6

--- a/solution.py
+++ b/solution.py
@@ -11,7 +11,7 @@
 LANES = 128
 LABEL_ROWS = 16
 DIGIT = 64
-TOGETHER = 4
+TOGETHER = 8
 APART = 16384.0
 NEVER = -1e30
 ANY = pl.BlockSpec(memory_space=pl.ANY)

time: 78 us -> 77.1 us (0.988)
  Pallas kernels: 17.3 us -> 16.2 us
  waiting for transfers between devices: 26.7 us -> 27.5 us
    pallas_call x4, Pallas kernels: 12 us -> 11 us  [attend(): pl.pallas_call(kernel, out_shape=jax.ShapeDtypeStruct((rows, width), jnp....]
  transfers between devices with their start and end apart: 11 -> 11, of which waited for: 4 -> 4; matrix products, arithmetic and copies ran while one was open for 6% -> 6% of each run, Pallas kernels for 17% -> 18%
where the time goes in v8:
time: 77.1 us; the launch traced here: 76.2 us
  waiting for transfers between devices  27.5 us (36%)
  starting transfers between devices  27.4 us (36%)
  Pallas kernels  16.2 us (21%)
  local copies, waits for them, and re-layouts  2.71 us (4%)
  other arithmetic  1.96 us (3%)
    all_to_all x1, waiting for transfers between devices, local(): lax.all_to_all(send_kv, 'dp', split_axis=0, concat_axis=0, tiled=True)  17.7 us
    ppermute x8, starting transfers between devices, local(): lax.ppermute(parcel, 'dp', [(owner, owner ^ half + index) for owner in ra...  15.3 us
    pallas_call x4, Pallas kernels, attend(): pl.pallas_call(kernel, out_shape=jax.ShapeDtypeStruct((rows, width), jnp....  11 us
    all_to_all x1, starting transfers between devices, local(): lax.all_to_all(send_kv, 'dp', split_axis=0, concat_axis=0, tiled=True)  6.5 us
    all_to_all x1, waiting for transfers between devices, local(): lax.all_to_all(near, 'dp', split_axis=0, concat_axis=0, axis_index_groups...  5.76 us
    all_to_all x1, starting transfers between devices, local(): lax.all_to_all(near, 'dp', split_axis=0, concat_axis=0, axis_index_groups...  4.32 us
    ppermute x1, waiting for transfers between devices, local(): lax.ppermute(own_kv, 'ctx', [(0, 1)])[None]  3.79 us
    pallas_call x1, Pallas kernels, pack_q(): pl.pallas_call(kernel, out_shape=[pltpu.HBM((half, cap, width), queries.d...  2.23 us
  transfers between devices with their start and end apart: 11, of which 4 were waited for; matrix products, arithmetic and copies ran while one was open for 6% of the time, Pallas kernels for 18%

profile of v8, /device:TPU:5, one launch (start us, length us, event | category | flops | bytes accessed | tf_op | source)
XLA Modules:
  0.0 76.2 jit_solution(8574439417484476200)
XLA Ops:
  0.0 2.0 %pack_kv.1.earlier_ref = bf16[16,144,128]{2,1,0:T(8,128)(2,1)} custom-call(s32[2,512]{1,0:T(2,128)} %bitcast.19, s32[4,128]{1,0:T(4,128)} %bitcast.22, bf16[1024,128]{1,0:T(8,128)(2,1)} %bitcast.18), custom_call_target="tpu_custom_call" | custom-call | tf_op jit(solution)/shard_map/pack_kv/pallas_call | solution.py:80
  2.0 6.5 %all-to-all-start = ((bf16[16,144,128]{2,1,0:T(8,128)(2,1)}), bf16[16,144,128]{2,1,0:T(8,128)(2,1)S(1)}, u32[]{:S(2)}, u32[]{:S(2)}) async-start(bf16[16,144,128]{2,1,0:T(8,128)(2,1)} %pack_kv.1.earlier_ref), calls=%async_computation | async-start | bytes 1179648 | tf_op jit(solution)/shard_map/all_to_all | solution.py:356
  8.5 2.2 %pack_q.1 = (bf16[8,64,1024]{2,1,0:T(8,128)(2,1)}, bf16[64,1024]{1,0:T(8,128)(2,1)S(1)}, bf16[64,1024]{1,0:T(8,128)(2,1)S(1)}, bf16[64,1024]{1,0:T(8,128)(2,1)S(...) custom-call(s32[2,512]{1,0:T(2,128)} %bitcast.20, ...), custom_call_target="tpu_custom_call" | custom-call | tf_op jit(solution)/shard_map/pack_q/pallas_call | solution.py:132
  10.7 3.5 %collective-permute-start.3 = (bf16[64,1024]{1,0:T(8,128)(2,1)}, bf16[64,1024]{1,0:T(8,128)(2,1)S(1)}, u32[]{:S(2)}, u32[]{:S(2)}) collective-permute-start(bf16[64,1024]{1,0:T(8,128)(2,1)} %get-tuple-element.23), channel_id=1, source_target_pairs={{0,22},{2,20},{4,18},{6,16},{8,30},{10,28},{12,26},{14,24},{16,6},... | collective-permute-start | bytes 393224 | tf_op jit(solution)/shard_map/ppermute | solution.py:390
  14.2 0.3 collective-permute-start.4
  14.5 2.5 %collective-permute-start.6 = (bf16[64,1024]{1,0:T(8,128)(2,1)S(1)}, bf16[64,1024]{1,0:T(8,128)(2,1)S(1)}, u32[]{:S(2)}, u32[]{:S(2)}) collective-permute-start(bf16[64,1024]{1,0:T(8,128)(2,1)S(1)} %get-tuple-element.28), channel_id=1, source_target_pairs={{0,18},{2,16},{4,22},{6,20},{8,26},{10,24},{12,30},{14,28},{16,2},... | collective-permute-start | bytes 393224 | tf_op jit(solution)/shard_map/ppermute | solution.py:390
  17.0 0.0 collective-permute-start.8
  17.0 0.1 slice_xor_fusion
  17.1 0.1 pad_add_fusion
  17.2 17.7 %all-to-all-done.in_ref = bf16[16,144,128]{2,1,0:T(8,128)(2,1)S(1)} async-done(((bf16[16,144,128]{2,1,0:T(8,128)(2,1)}), bf16[16,144,128]{2,1,0:T(8,128)(2,1)S(1)}, u32[]{:S(2)}, u32[]{:S(2)}) %all-to-all-start) | async-done | bytes 589856 | tf_op jit(solution)/shard_map/all_to_all | solution.py:356
  34.8 4.3 %all-to-all-start.1 = ((bf16[8,64,1024]{2,1,0:T(8,128)(2,1)}), bf16[8,64,1024]{2,1,0:T(8,128)(2,1)S(1)}, u32[]{:S(2)}, u32[]{:S(2)}) async-start(bf16[8,64,1024]{2,1,0:T(8,128)(2,1)} %get-tuple-element.22), calls=%async_computation.1 | async-start | bytes 2097152 | tf_op jit(solution)/shard_map/all_to_all | solution.py:359
  39.2 0.7 slice_reduce_fusion.1
  39.9 0.1 select_reduce_fusion.2.source_ref
  40.0 0.1 add.112
  40.1 0.1 select_reduce_fusion
  40.2 0.1 reshape.420
  40.3 0.1 broadcast_in_dim_reshape.2
  40.4 1.0 %place_kv.1 = bf16[1040,128]{1,0:T(8,128)(2,1)S(1)} custom-call(s32[8]{0:T(128)S(1)} %select_reduce_fusion.2.source_ref, bf16[16,144,128]{2,1,0:T(8,128)(2,1)S(1)} %all-to-all-done.in_ref, bf16[16,128]{1,0:T(8,128)(2,1)S(1)} %pad.4.begin_ref), custom_call_target="tpu_custom_call" | custom-call | tf_op jit(solution)/shard_map/place_kv/pallas_call | solution.py:173
  41.4 1.3 %collective-permute-start = (bf16[1040,128]{1,0:T(8,128)(2,1)S(1)}, bf16[1040,128]{1,0:T(8,128)(2,1)}, u32[]{:S(2)}, u32[]{:S(2)}) collective-permute-start(bf16[1040,128]{1,0:T(8,128)(2,1)S(1)} %place_kv.1), channel_id=1, source_target_pairs={{0,1},{2,3},{4,5},{6,7},{8,9},{10,11},{12,13},{14,15},{16,17},{18,... | collective-permute-start | bytes 798728 | tf_op jit(solution)/shard_map/ppermute | solution.py:375
  42.7 0.1 reduce_min.9
  42.9 0.4 fusion.6
  43.2 0.0 collective-permute-done.4.rest_0_
  43.2 3.6 %collective-permute-start.5 = (bf16[64,1024]{1,0:T(8,128)(2,1)S(1)}, bf16[64,1024]{1,0:T(8,128)(2,1)S(1)}, u32[]{:S(2)}, u32[]{:S(2)}) collective-permute-start(bf16[64,1024]{1,0:T(8,128)(2,1)S(1)} %get-tuple-element.26), channel_id=1, source_target_pairs={{0,24},{2,26},{4,28},{6,30},{8,16},{10,18},{12,20},{14,22},{16,8},... | collective-permute-start | bytes 393224 | tf_op jit(solution)/shard_map/ppermute | solution.py:390
  46.8 0.0 collective-permute-done.6.rest_1_
  46.8 0.3 collective-permute-start.7
  47.2 0.2 select_convert_fusion.1
  47.4 0.2 select_reduce_fusion.1
  47.6 0.1 pad_add_fusion.1.meta_ref
  47.7 3.8 %collective-permute-done = bf16[1040,128]{1,0:T(8,128)(2,1)} collective-permute-done((bf16[1040,128]{1,0:T(8,128)(2,1)S(1)}, bf16[1040,128]{1,0:T(8,128)(2,1)}, u32[]{:S(2)}, u32[]{:S(2)}) %collective-permute-start) | collective-permute-done | bytes 266272 | tf_op jit(solution)/shard_map/ppermute | solution.py:375
  51.5 1.0 %slice.75 = bf16[1,1024,128]{2,1,0:T(8,128)(2,1)S(1)} slice(bf16[1,1040,128]{2,1,0:T(8,128)(2,1)} %bitcast.7), slice={[0:1], [0:1024], [0:128]} | slice | bytes 524288 | tf_op jit(solution)/shard_map/slice | solution.py:380
  52.4 0.7 convert_convert_fusion.1
  53.1 5.1 %collective-permute-start.2 = (bf16[64,1024]{1,0:T(8,128)(2,1)S(1)}, bf16[64,1024]{1,0:T(8,128)(2,1)S(1)}, u32[]{:S(2)}, u32[]{:S(2)}) collective-permute-start(bf16[64,1024]{1,0:T(8,128)(2,1)S(1)} %get-tuple-element.21), channel_id=1, source_target_pairs={{0,30},{2,28},{4,26},{6,24},{8,22},{10,20},{12,18},{14,16},{16,14}... | collective-permute-start | bytes 393224 | tf_op jit(solution)/shard_map/ppermute | solution.py:390
  58.2 0.4 fusion.5
  58.6 0.2 select_convert_fusion.pd_ref
  58.9 0.0 collective-permute-done.8.rest_2_
  58.9 0.1 collective-permute-start.1
  58.9 2.3 %attend.4.rest_3_ = bf16[512,1024]{1,0:T(8,128)(2,1)} custom-call(s32[25]{0:T(128)S(1)} %pad_add_fusion.1.meta_ref, bf16[512,128]{1,0:T(8,128)(2,1)S(1)} %get-tuple-element.38.qd_ref, bf16[512,128]{1,0:T(8,128)(2,1)S(1)} %get-tuple-element.48.ok_ref, bf16[512,128]{1,0:T(8,128)(2,1)S(1)} %get-tuple-element.37.od_ref, ...), custom_call_target="tpu_custom_call" | custom-call | flops 536870912 | bytes 786432 | tf_op jit(solution)/shard_map/attend/pallas_call | solution.py:312
  61.3 0.0 collective-permute-done.3.rest_0_
  61.3 0.0 collective-permute-done.5.rest_1_
  61.3 0.2 collective-permute-done.7.rest_2_
  61.5 2.5 %attend.5.rest_1_ = bf16[512,1024]{1,0:T(8,128)(2,1)} custom-call(s32[25]{0:T(128)S(1)} %pad_add_fusion.1.meta_ref, bf16[512,128]{1,0:T(8,128)(2,1)S(1)} %get-tuple-element.38.qd_ref, bf16[512,128]{1,0:T(8,128)(2,1)S(1)} %get-tuple-element.48.ok_ref, bf16[512,128]{1,0:T(8,128)(2,1)S(1)} %get-tuple-element.37.od_ref, ...), custom_call_target="tpu_custom_call", output_to_operand_aliasing={{}: (11, {})} | custom-call | flops 536870912 | bytes 786432 | tf_op jit(solution)/shard_map/attend/pallas_call | solution.py:312
  64.1 5.8 %all-to-all-done.1.rest_0_ = bf16[8,64,1024]{2,1,0:T(8,128)(2,1)S(1)} async-done(((bf16[8,64,1024]{2,1,0:T(8,128)(2,1)}), bf16[8,64,1024]{2,1,0:T(8,128)(2,1)S(1)}, u32[]{:S(2)}, u32[]{:S(2)}) %all-to-all-start.1) | async-done | bytes 1048608 | tf_op jit(solution)/shard_map/all_to_all | solution.py:359
  69.8 5.3 %attend.6.rest_2_ = bf16[512,1024]{1,0:T(8,128)(2,1)} custom-call(s32[25]{0:T(128)S(1)} %pad_add_fusion.1.meta_ref, bf16[512,128]{1,0:T(8,128)(2,1)S(1)} %get-tuple-element.38.qd_ref, bf16[512,128]{1,0:T(8,128)(2,1)S(1)} %get-tuple-element.48.ok_ref, bf16[512,128]{1,0:T(8,128)(2,1)S(1)} %get-tuple-element.37.od_ref, ...), custom_call_target="tpu_custom_call", output_to_operand_aliasing={{}: (9, {})} | custom-call | flops 2147483648 | bytes 2097152 | tf_op jit(solution)/shard_map/attend/pallas_call | solution.py:312
  75.2 0.0 collective-permute-done.2.rest_1_
  75.2 0.0 collective-permute-done.1.rest_0_
  75.2 0.8 %attend.7 = bf16[512,1024]{1,0:T(8,128)(2,1)} custom-call(s32[25]{0:T(128)S(1)} %pad_add_fusion.1.meta_ref, bf16[512,128]{1,0:T(8,128)(2,1)S(1)} %get-tuple-element.38.qd_ref, bf16[512,128]{1,0:T(8,128)(2,1)S(1)} %get-tuple-element.48.ok_ref, bf16[512,128]{1,0:T(8,128)(2,1)S(1)} %get-tuple-element.37.od_ref, ...), custom_call_target="tpu_custom_call", output_to_operand_aliasing={{}: (10, {})} | custom-call | flops 536870912 | bytes 524288 | tf_op jit(solution)/shard_map/attend/pallas_call | solution.py:312
  (21 shorter events, 0.2 us)
Async XLA Ops:
  2.0 32.9 %all-to-all-start = ((bf16[16,144,128]{2,1,0:T(8,128)(2,1)}), bf16[16,144,128]{2,1,0:T(8,128)(2,1)S(1)}, u32[]{:S(2)}, u32[]{:S(2)}) async-start(bf16[16,144,128]{2,1,0:T(8,128)(2,1)} %pack_kv.1.earlier_ref), calls=%async_computation | async-start | bytes 1179648 | tf_op jit(solution)/shard_map/all_to_all | solution.py:356
  10.7 50.6 %collective-permute-start.3 = (bf16[64,1024]{1,0:T(8,128)(2,1)}, bf16[64,1024]{1,0:T(8,128)(2,1)S(1)}, u32[]{:S(2)}, u32[]{:S(2)}) collective-permute-start(bf16[64,1024]{1,0:T(8,128)(2,1)} %get-tuple-element.23), channel_id=1, source_target_pairs={{0,22},{2,20},{4,18},{6,16},{8,30},{10,28},{12,26},{14,24},{16,6},... | collective-permute-start | bytes 393224 | tf_op jit(solution)/shard_map/ppermute | solution.py:390
  14.2 29.0 %collective-permute-start.4 = (bf16[64,1024]{1,0:T(8,128)(2,1)S(1)}, bf16[64,1024]{1,0:T(8,128)(2,1)S(1)}, u32[]{:S(2)}, u32[]{:S(2)}) collective-permute-start(bf16[64,1024]{1,0:T(8,128)(2,1)S(1)} %get-tuple-element.25), channel_id=1, source_target_pairs={{0,16},{2,18},{4,20},{6,22},{8,24},{10,26},{12,28},{14,30},{16,0},... | collective-permute-start | bytes 393224 | tf_op jit(solution)/shard_map/ppermute | solution.py:390
  14.5 32.4 %collective-permute-start.6 = (bf16[64,1024]{1,0:T(8,128)(2,1)S(1)}, bf16[64,1024]{1,0:T(8,128)(2,1)S(1)}, u32[]{:S(2)}, u32[]{:S(2)}) collective-permute-start(bf16[64,1024]{1,0:T(8,128)(2,1)S(1)} %get-tuple-element.28), channel_id=1, source_target_pairs={{0,18},{2,16},{4,22},{6,20},{8,26},{10,24},{12,30},{14,28},{16,2},... | collective-permute-start | bytes 393224 | tf_op jit(solution)/shard_map/ppermute | solution.py:390
  17.0 41.9 %collective-permute-start.8 = (bf16[64,1024]{1,0:T(8,128)(2,1)S(1)}, bf16[64,1024]{1,0:T(8,128)(2,1)S(1)}, u32[]{:S(2)}, u32[]{:S(2)}) collective-permute-start(bf16[64,1024]{1,0:T(8,128)(2,1)S(1)} %get-tuple-element.30), channel_id=1, source_target_pairs={{0,20},{2,22},{4,16},{6,18},{8,28},{10,30},{12,24},{14,26},{16,4},... | collective-permute-start | bytes 393224 | tf_op jit(solution)/shard_map/ppermute | solution.py:390
  34.8 35.0 %all-to-all-start.1 = ((bf16[8,64,1024]{2,1,0:T(8,128)(2,1)}), bf16[8,64,1024]{2,1,0:T(8,128)(2,1)S(1)}, u32[]{:S(2)}, u32[]{:S(2)}) async-start(bf16[8,64,1024]{2,1,0:T(8,128)(2,1)} %get-tuple-element.22), calls=%async_computation.1 | async-start | bytes 2097152 | tf_op jit(solution)/shard_map/all_to_all | solution.py:359
  41.4 10.0 %collective-permute-start = (bf16[1040,128]{1,0:T(8,128)(2,1)S(1)}, bf16[1040,128]{1,0:T(8,128)(2,1)}, u32[]{:S(2)}, u32[]{:S(2)}) collective-permute-start(bf16[1040,128]{1,0:T(8,128)(2,1)S(1)} %place_kv.1), channel_id=1, source_target_pairs={{0,1},{2,3},{4,5},{6,7},{8,9},{10,11},{12,13},{14,15},{16,17},{18,... | collective-permute-start | bytes 798728 | tf_op jit(solution)/shard_map/ppermute | solution.py:375
  43.2 18.0 %collective-permute-start.5 = (bf16[64,1024]{1,0:T(8,128)(2,1)S(1)}, bf16[64,1024]{1,0:T(8,128)(2,1)S(1)}, u32[]{:S(2)}, u32[]{:S(2)}) collective-permute-start(bf16[64,1024]{1,0:T(8,128)(2,1)S(1)} %get-tuple-element.26), channel_id=1, source_target_pairs={{0,24},{2,26},{4,28},{6,30},{8,16},{10,18},{12,20},{14,22},{16,8},... | collective-permute-start | bytes 393224 | tf_op jit(solution)/shard_map/ppermute | solution.py:390
  46.8 14.7 %collective-permute-start.7 = (bf16[64,1024]{1,0:T(8,128)(2,1)S(1)}, bf16[64,1024]{1,0:T(8,128)(2,1)S(1)}, u32[]{:S(2)}, u32[]{:S(2)}) collective-permute-start(bf16[64,1024]{1,0:T(8,128)(2,1)S(1)} %get-tuple-element.29), channel_id=1, source_target_pairs={{0,26},{2,24},{4,30},{6,28},{8,18},{10,16},{12,22},{14,20},{16,10}... | collective-permute-start | bytes 393224 | tf_op jit(solution)/shard_map/ppermute | solution.py:390
  53.1 22.0 %collective-permute-start.2 = (bf16[64,1024]{1,0:T(8,128)(2,1)S(1)}, bf16[64,1024]{1,0:T(8,128)(2,1)S(1)}, u32[]{:S(2)}, u32[]{:S(2)}) collective-permute-start(bf16[64,1024]{1,0:T(8,128)(2,1)S(1)} %get-tuple-element.21), channel_id=1, source_target_pairs={{0,30},{2,28},{4,26},{6,24},{8,22},{10,20},{12,18},{14,16},{16,14}... | collective-permute-start | bytes 393224 | tf_op jit(solution)/shard_map/ppermute | solution.py:390
  58.9 16.3 %collective-permute-start.1 = (bf16[64,1024]{1,0:T(8,128)(2,1)S(1)}, bf16[64,1024]{1,0:T(8,128)(2,1)S(1)}, u32[]{:S(2)}, u32[]{:S(2)}) collective-permute-start(bf16[64,1024]{1,0:T(8,128)(2,1)S(1)} %get-tuple-element.19), channel_id=1, source_target_pairs={{0,28},{2,30},{4,24},{6,26},{8,20},{10,22},{12,16},{14,18},{16,12}... | collective-permute-start | bytes 393224 | tf_op jit(solution)/shard_map/ppermute | solution.py:390

commit v9 on v6

--- a/solution.py
+++ b/solution.py
@@ -47,22 +47,7 @@
             held_ref[slot] = blocks
         for block in range(blocks):
             held_ref[routing_ref[0, block * cap]] = block
-        fetches[1].wait()
-        row_at = lax.broadcasted_iota(jnp.int32, (LABEL_ROWS, LANES), 0)
-        label_ref[blocks] = jnp.full((LABEL_ROWS, LANES), 255.0, jnp.bfloat16)
-        for block in range(blocks):
-            group, part = divmod(block, per_group)
-            begin = doc_ref[group : group + 1, :] - routing_ref[0, block * cap] * seq_len
-            place = routing_ref[1, block * cap] // cap
-            label = jnp.where(row_at == 0, begin // DIGIT, jnp.where(row_at == 1, begin % DIGIT, part))
-            label = jnp.where(row_at == 2, place, label)
-            label_ref[block] = label.astype(jnp.float32).astype(jnp.bfloat16)
-        copies = [
-            pltpu.make_async_copy(
-                label_ref.at[held_ref[slot]], out_ref.at[slot, pl.ds(0, LABEL_ROWS)], label_sem.at[slot]
-            )
-            for slot in range(owners)
-        ]
+        copies = []
         for block in range(blocks):
             copies.append(
                 pltpu.make_async_copy(
@@ -74,7 +59,25 @@
         fetches[2].wait()
         for copy in copies:
             copy.start()
-        for copy in copies:
+        fetches[1].wait()
+        row_at = lax.broadcasted_iota(jnp.int32, (LABEL_ROWS, LANES), 0)
+        label_ref[blocks] = jnp.full((LABEL_ROWS, LANES), 255.0, jnp.bfloat16)
+        for block in range(blocks):
+            group, part = divmod(block, per_group)
+            begin = doc_ref[group : group + 1, :] - routing_ref[0, block * cap] * seq_len
+            place = routing_ref[1, block * cap] // cap
+            label = jnp.where(row_at == 0, begin // DIGIT, jnp.where(row_at == 1, begin % DIGIT, part))
+            label = jnp.where(row_at == 2, place, label)
+            label_ref[block] = label.astype(jnp.float32).astype(jnp.bfloat16)
+        labels = [
+            pltpu.make_async_copy(
+                label_ref.at[held_ref[slot]], out_ref.at[slot, pl.ds(0, LABEL_ROWS)], label_sem.at[slot]
+            )
+            for slot in range(owners)
+        ]
+        for label in labels:
+            label.start()
+        for copy in copies + labels:
             copy.wait()
 
     return pl.pallas_call(

time: 78 us -> 77.9 us (level); the launches traced: 76.5 us -> 77.3 us
  transfers between devices with their start and end apart: 11 -> 11, of which waited for: 4 -> 3; matrix products, arithmetic and copies ran while one was open for 6% -> 6% of each run, Pallas kernels for 17% -> 17%
where the time goes in v9:
time: 77.9 us; the launch traced here: 77.3 us
  starting transfers between devices  27.4 us (35%)
  waiting for transfers between devices  27.4 us (35%)
  Pallas kernels  17.4 us (22%)
  local copies, waits for them, and re-layouts  2.71 us (3%)
  other arithmetic  1.96 us (3%)
    all_to_all x1, waiting for transfers between devices, local(): lax.all_to_all(send_kv, 'dp', split_axis=0, concat_axis=0, tiled=True)  17.6 us
    ppermute x8, starting transfers between devices, local(): lax.ppermute(parcel, 'dp', [(owner, owner ^ half + index) for owner in ra...  15.3 us
    pallas_call x4, Pallas kernels, attend(): pl.pallas_call(kernel, out_shape=jax.ShapeDtypeStruct((rows, width), jnp....  12.2 us
    all_to_all x1, starting transfers between devices, local(): lax.all_to_all(send_kv, 'dp', split_axis=0, concat_axis=0, tiled=True)  6.5 us
    all_to_all x1, waiting for transfers between devices, local(): lax.all_to_all(near, 'dp', split_axis=0, concat_axis=0, axis_index_groups...  5.94 us
    all_to_all x1, starting transfers between devices, local(): lax.all_to_all(near, 'dp', split_axis=0, concat_axis=0, axis_index_groups...  4.32 us
    ppermute x1, waiting for transfers between devices, local(): lax.ppermute(own_kv, 'ctx', [(0, 1)])[None]  3.79 us
    pallas_call x1, Pallas kernels, pack_q(): pl.pallas_call(kernel, out_shape=[pltpu.HBM((half, cap, width), queries.d...  2.26 us
  transfers between devices with their start and end apart: 11, of which 3 were waited for; matrix products, arithmetic and copies ran while one was open for 6% of the time, Pallas kernels for 17%

profile of v9, /device:TPU:5, one launch (start us, length us, event | category | flops | bytes accessed | tf_op | source)
XLA Modules:
  0.0 77.3 jit_solution(12586882867101667797)
XLA Ops:
  0.0 1.9 %pack_kv.1.earlier_ref = bf16[16,144,128]{2,1,0:T(8,128)(2,1)} custom-call(s32[2,512]{1,0:T(2,128)} %bitcast.19, s32[4,128]{1,0:T(4,128)} %bitcast.22, bf16[1024,128]{1,0:T(8,128)(2,1)} %bitcast.18), custom_call_target="tpu_custom_call" | custom-call | tf_op jit(solution)/shard_map/pack_kv/pallas_call | solution.py:83
  1.9 6.5 %all-to-all-start = ((bf16[16,144,128]{2,1,0:T(8,128)(2,1)}), bf16[16,144,128]{2,1,0:T(8,128)(2,1)S(1)}, u32[]{:S(2)}, u32[]{:S(2)}) async-start(bf16[16,144,128]{2,1,0:T(8,128)(2,1)} %pack_kv.1.earlier_ref), calls=%async_computation | async-start | bytes 1179648 | tf_op jit(solution)/shard_map/all_to_all | solution.py:359
  8.4 2.3 %pack_q.1 = (bf16[8,64,1024]{2,1,0:T(8,128)(2,1)}, bf16[64,1024]{1,0:T(8,128)(2,1)S(1)}, bf16[64,1024]{1,0:T(8,128)(2,1)S(1)}, bf16[64,1024]{1,0:T(8,128)(2,1)S(...) custom-call(s32[2,512]{1,0:T(2,128)} %bitcast.20, ...), custom_call_target="tpu_custom_call" | custom-call | tf_op jit(solution)/shard_map/pack_q/pallas_call | solution.py:135
  10.7 3.5 %collective-permute-start.3 = (bf16[64,1024]{1,0:T(8,128)(2,1)}, bf16[64,1024]{1,0:T(8,128)(2,1)S(1)}, u32[]{:S(2)}, u32[]{:S(2)}) collective-permute-start(bf16[64,1024]{1,0:T(8,128)(2,1)} %get-tuple-element.23), channel_id=1, source_target_pairs={{0,22},{2,20},{4,18},{6,16},{8,30},{10,28},{12,26},{14,24},{16,6},... | collective-permute-start | bytes 393224 | tf_op jit(solution)/shard_map/ppermute | solution.py:393
  14.2 0.3 collective-permute-start.4
  14.5 2.3 %collective-permute-start.6 = (bf16[64,1024]{1,0:T(8,128)(2,1)S(1)}, bf16[64,1024]{1,0:T(8,128)(2,1)S(1)}, u32[]{:S(2)}, u32[]{:S(2)}) collective-permute-start(bf16[64,1024]{1,0:T(8,128)(2,1)S(1)} %get-tuple-element.28), channel_id=1, source_target_pairs={{0,18},{2,16},{4,22},{6,20},{8,26},{10,24},{12,30},{14,28},{16,2},... | collective-permute-start | bytes 393224 | tf_op jit(solution)/shard_map/ppermute | solution.py:393
  16.9 0.1 collective-permute-start.8
  17.0 0.1 slice_xor_fusion
  17.1 0.1 pad_add_fusion
  17.2 17.6 %all-to-all-done.in_ref = bf16[16,144,128]{2,1,0:T(8,128)(2,1)S(1)} async-done(((bf16[16,144,128]{2,1,0:T(8,128)(2,1)}), bf16[16,144,128]{2,1,0:T(8,128)(2,1)S(1)}, u32[]{:S(2)}, u32[]{:S(2)}) %all-to-all-start) | async-done | bytes 589856 | tf_op jit(solution)/shard_map/all_to_all | solution.py:359
  34.8 4.3 %all-to-all-start.1 = ((bf16[8,64,1024]{2,1,0:T(8,128)(2,1)}), bf16[8,64,1024]{2,1,0:T(8,128)(2,1)S(1)}, u32[]{:S(2)}, u32[]{:S(2)}) async-start(bf16[8,64,1024]{2,1,0:T(8,128)(2,1)} %get-tuple-element.22), calls=%async_computation.1 | async-start | bytes 2097152 | tf_op jit(solution)/shard_map/all_to_all | solution.py:362
  39.1 0.7 slice_reduce_fusion.1
  39.9 0.1 select_reduce_fusion.2.source_ref
  40.0 0.1 add.112
  40.1 0.1 select_reduce_fusion
  40.2 0.1 reshape.420
  40.3 0.1 broadcast_in_dim_reshape.2
  40.4 1.0 %place_kv.1 = bf16[1040,128]{1,0:T(8,128)(2,1)S(1)} custom-call(s32[8]{0:T(128)S(1)} %select_reduce_fusion.2.source_ref, bf16[16,144,128]{2,1,0:T(8,128)(2,1)S(1)} %all-to-all-done.in_ref, bf16[16,128]{1,0:T(8,128)(2,1)S(1)} %pad.4.begin_ref), custom_call_target="tpu_custom_call" | custom-call | tf_op jit(solution)/shard_map/place_kv/pallas_call | solution.py:176
  41.4 1.3 %collective-permute-start = (bf16[1040,128]{1,0:T(8,128)(2,1)S(1)}, bf16[1040,128]{1,0:T(8,128)(2,1)}, u32[]{:S(2)}, u32[]{:S(2)}) collective-permute-start(bf16[1040,128]{1,0:T(8,128)(2,1)S(1)} %place_kv.1), channel_id=1, source_target_pairs={{0,1},{2,3},{4,5},{6,7},{8,9},{10,11},{12,13},{14,15},{16,17},{18,... | collective-permute-start | bytes 798728 | tf_op jit(solution)/shard_map/ppermute | solution.py:378
  42.7 0.1 reduce_min.9
  42.9 0.4 fusion.6
  43.2 0.0 collective-permute-done.4.rest_0_
  43.2 3.6 %collective-permute-start.5 = (bf16[64,1024]{1,0:T(8,128)(2,1)S(1)}, bf16[64,1024]{1,0:T(8,128)(2,1)S(1)}, u32[]{:S(2)}, u32[]{:S(2)}) collective-permute-start(bf16[64,1024]{1,0:T(8,128)(2,1)S(1)} %get-tuple-element.26), channel_id=1, source_target_pairs={{0,24},{2,26},{4,28},{6,30},{8,16},{10,18},{12,20},{14,22},{16,8},... | collective-permute-start | bytes 393224 | tf_op jit(solution)/shard_map/ppermute | solution.py:393
  46.8 0.0 collective-permute-done.6.rest_1_
  46.8 0.3 collective-permute-start.7
  47.2 0.2 select_convert_fusion.1
  47.4 0.2 select_reduce_fusion.1
  47.5 0.1 pad_add_fusion.1.meta_ref
  47.7 3.8 %collective-permute-done = bf16[1040,128]{1,0:T(8,128)(2,1)} collective-permute-done((bf16[1040,128]{1,0:T(8,128)(2,1)S(1)}, bf16[1040,128]{1,0:T(8,128)(2,1)}, u32[]{:S(2)}, u32[]{:S(2)}) %collective-permute-start) | collective-permute-done | bytes 266272 | tf_op jit(solution)/shard_map/ppermute | solution.py:378
  51.5 1.0 %slice.75 = bf16[1,1024,128]{2,1,0:T(8,128)(2,1)S(1)} slice(bf16[1,1040,128]{2,1,0:T(8,128)(2,1)} %bitcast.7), slice={[0:1], [0:1024], [0:128]} | slice | bytes 524288 | tf_op jit(solution)/shard_map/slice | solution.py:383
  52.4 0.7 convert_convert_fusion.1
  53.1 5.1 %collective-permute-start.2 = (bf16[64,1024]{1,0:T(8,128)(2,1)S(1)}, bf16[64,1024]{1,0:T(8,128)(2,1)S(1)}, u32[]{:S(2)}, u32[]{:S(2)}) collective-permute-start(bf16[64,1024]{1,0:T(8,128)(2,1)S(1)} %get-tuple-element.21), channel_id=1, source_target_pairs={{0,30},{2,28},{4,26},{6,24},{8,22},{10,20},{12,18},{14,16},{16,14}... | collective-permute-start | bytes 393224 | tf_op jit(solution)/shard_map/ppermute | solution.py:393
  58.2 0.4 fusion.5
  58.6 0.2 select_convert_fusion.pd_ref
  58.8 0.0 collective-permute-done.8.rest_2_
  58.9 0.1 collective-permute-start.1
  58.9 2.5 %attend.4.rest_3_ = bf16[512,1024]{1,0:T(8,128)(2,1)} custom-call(s32[25]{0:T(128)S(1)} %pad_add_fusion.1.meta_ref, bf16[512,128]{1,0:T(8,128)(2,1)S(1)} %get-tuple-element.38.qd_ref, bf16[512,128]{1,0:T(8,128)(2,1)S(1)} %get-tuple-element.48.ok_ref, bf16[512,128]{1,0:T(8,128)(2,1)S(1)} %get-tuple-element.37.od_ref, ...), custom_call_target="tpu_custom_call" | custom-call | flops 536870912 | bytes 786432 | tf_op jit(solution)/shard_map/attend/pallas_call | solution.py:315
  61.4 0.0 collective-permute-done.3.rest_0_
  61.4 0.0 collective-permute-done.5.rest_1_
  61.5 0.0 collective-permute-done.7.rest_2_
  61.5 2.3 %attend.5.rest_1_ = bf16[512,1024]{1,0:T(8,128)(2,1)} custom-call(s32[25]{0:T(128)S(1)} %pad_add_fusion.1.meta_ref, bf16[512,128]{1,0:T(8,128)(2,1)S(1)} %get-tuple-element.38.qd_ref, bf16[512,128]{1,0:T(8,128)(2,1)S(1)} %get-tuple-element.48.ok_ref, bf16[512,128]{1,0:T(8,128)(2,1)S(1)} %get-tuple-element.37.od_ref, ...), custom_call_target="tpu_custom_call", output_to_operand_aliasing={{}: (11, {})} | custom-call | flops 536870912 | bytes 786432 | tf_op jit(solution)/shard_map/attend/pallas_call | solution.py:315
  63.9 5.9 %all-to-all-done.1.rest_0_ = bf16[8,64,1024]{2,1,0:T(8,128)(2,1)S(1)} async-done(((bf16[8,64,1024]{2,1,0:T(8,128)(2,1)}), bf16[8,64,1024]{2,1,0:T(8,128)(2,1)S(1)}, u32[]{:S(2)}, u32[]{:S(2)}) %all-to-all-start.1) | async-done | bytes 1048608 | tf_op jit(solution)/shard_map/all_to_all | solution.py:362
  69.8 4.9 %attend.6.rest_2_ = bf16[512,1024]{1,0:T(8,128)(2,1)} custom-call(s32[25]{0:T(128)S(1)} %pad_add_fusion.1.meta_ref, bf16[512,128]{1,0:T(8,128)(2,1)S(1)} %get-tuple-element.38.qd_ref, bf16[512,128]{1,0:T(8,128)(2,1)S(1)} %get-tuple-element.48.ok_ref, bf16[512,128]{1,0:T(8,128)(2,1)S(1)} %get-tuple-element.37.od_ref, ...), custom_call_target="tpu_custom_call", output_to_operand_aliasing={{}: (9, {})} | custom-call | flops 2147483648 | bytes 2097152 | tf_op jit(solution)/shard_map/attend/pallas_call | solution.py:315
  74.7 0.0 collective-permute-done.2.rest_1_
  74.7 0.0 collective-permute-done.1.rest_0_
  74.7 2.5 %attend.7 = bf16[512,1024]{1,0:T(8,128)(2,1)} custom-call(s32[25]{0:T(128)S(1)} %pad_add_fusion.1.meta_ref, bf16[512,128]{1,0:T(8,128)(2,1)S(1)} %get-tuple-element.38.qd_ref, bf16[512,128]{1,0:T(8,128)(2,1)S(1)} %get-tuple-element.48.ok_ref, bf16[512,128]{1,0:T(8,128)(2,1)S(1)} %get-tuple-element.37.od_ref, ...), custom_call_target="tpu_custom_call", output_to_operand_aliasing={{}: (10, {})} | custom-call | flops 536870912 | bytes 524288 | tf_op jit(solution)/shard_map/attend/pallas_call | solution.py:315
  (21 shorter events, 0.2 us)
Async XLA Ops:
  1.9 32.9 %all-to-all-start = ((bf16[16,144,128]{2,1,0:T(8,128)(2,1)}), bf16[16,144,128]{2,1,0:T(8,128)(2,1)S(1)}, u32[]{:S(2)}, u32[]{:S(2)}) async-start(bf16[16,144,128]{2,1,0:T(8,128)(2,1)} %pack_kv.1.earlier_ref), calls=%async_computation | async-start | bytes 1179648 | tf_op jit(solution)/shard_map/all_to_all | solution.py:359
  10.7 50.7 %collective-permute-start.3 = (bf16[64,1024]{1,0:T(8,128)(2,1)}, bf16[64,1024]{1,0:T(8,128)(2,1)S(1)}, u32[]{:S(2)}, u32[]{:S(2)}) collective-permute-start(bf16[64,1024]{1,0:T(8,128)(2,1)} %get-tuple-element.23), channel_id=1, source_target_pairs={{0,22},{2,20},{4,18},{6,16},{8,30},{10,28},{12,26},{14,24},{16,6},... | collective-permute-start | bytes 393224 | tf_op jit(solution)/shard_map/ppermute | solution.py:393
  14.2 29.0 %collective-permute-start.4 = (bf16[64,1024]{1,0:T(8,128)(2,1)S(1)}, bf16[64,1024]{1,0:T(8,128)(2,1)S(1)}, u32[]{:S(2)}, u32[]{:S(2)}) collective-permute-start(bf16[64,1024]{1,0:T(8,128)(2,1)S(1)} %get-tuple-element.25), channel_id=1, source_target_pairs={{0,16},{2,18},{4,20},{6,22},{8,24},{10,26},{12,28},{14,30},{16,0},... | collective-permute-start | bytes 393224 | tf_op jit(solution)/shard_map/ppermute | solution.py:393
  14.5 32.3 %collective-permute-start.6 = (bf16[64,1024]{1,0:T(8,128)(2,1)S(1)}, bf16[64,1024]{1,0:T(8,128)(2,1)S(1)}, u32[]{:S(2)}, u32[]{:S(2)}) collective-permute-start(bf16[64,1024]{1,0:T(8,128)(2,1)S(1)} %get-tuple-element.28), channel_id=1, source_target_pairs={{0,18},{2,16},{4,22},{6,20},{8,26},{10,24},{12,30},{14,28},{16,2},... | collective-permute-start | bytes 393224 | tf_op jit(solution)/shard_map/ppermute | solution.py:393
  16.9 42.0 %collective-permute-start.8 = (bf16[64,1024]{1,0:T(8,128)(2,1)S(1)}, bf16[64,1024]{1,0:T(8,128)(2,1)S(1)}, u32[]{:S(2)}, u32[]{:S(2)}) collective-permute-start(bf16[64,1024]{1,0:T(8,128)(2,1)S(1)} %get-tuple-element.30), channel_id=1, source_target_pairs={{0,20},{2,22},{4,16},{6,18},{8,28},{10,30},{12,24},{14,26},{16,4},... | collective-permute-start | bytes 393224 | tf_op jit(solution)/shard_map/ppermute | solution.py:393
  34.8 35.0 %all-to-all-start.1 = ((bf16[8,64,1024]{2,1,0:T(8,128)(2,1)}), bf16[8,64,1024]{2,1,0:T(8,128)(2,1)S(1)}, u32[]{:S(2)}, u32[]{:S(2)}) async-start(bf16[8,64,1024]{2,1,0:T(8,128)(2,1)} %get-tuple-element.22), calls=%async_computation.1 | async-start | bytes 2097152 | tf_op jit(solution)/shard_map/all_to_all | solution.py:362
  41.4 10.0 %collective-permute-start = (bf16[1040,128]{1,0:T(8,128)(2,1)S(1)}, bf16[1040,128]{1,0:T(8,128)(2,1)}, u32[]{:S(2)}, u32[]{:S(2)}) collective-permute-start(bf16[1040,128]{1,0:T(8,128)(2,1)S(1)} %place_kv.1), channel_id=1, source_target_pairs={{0,1},{2,3},{4,5},{6,7},{8,9},{10,11},{12,13},{14,15},{16,17},{18,... | collective-permute-start | bytes 798728 | tf_op jit(solution)/shard_map/ppermute | solution.py:378
  43.2 18.2 %collective-permute-start.5 = (bf16[64,1024]{1,0:T(8,128)(2,1)S(1)}, bf16[64,1024]{1,0:T(8,128)(2,1)S(1)}, u32[]{:S(2)}, u32[]{:S(2)}) collective-permute-start(bf16[64,1024]{1,0:T(8,128)(2,1)S(1)} %get-tuple-element.26), channel_id=1, source_target_pairs={{0,24},{2,26},{4,28},{6,30},{8,16},{10,18},{12,20},{14,22},{16,8},... | collective-permute-start | bytes 393224 | tf_op jit(solution)/shard_map/ppermute | solution.py:393
  46.8 14.7 %collective-permute-start.7 = (bf16[64,1024]{1,0:T(8,128)(2,1)S(1)}, bf16[64,1024]{1,0:T(8,128)(2,1)S(1)}, u32[]{:S(2)}, u32[]{:S(2)}) collective-permute-start(bf16[64,1024]{1,0:T(8,128)(2,1)S(1)} %get-tuple-element.29), channel_id=1, source_target_pairs={{0,26},{2,24},{4,30},{6,28},{8,18},{10,16},{12,22},{14,20},{16,10}... | collective-permute-start | bytes 393224 | tf_op jit(solution)/shard_map/ppermute | solution.py:393
  53.1 21.6 %collective-permute-start.2 = (bf16[64,1024]{1,0:T(8,128)(2,1)S(1)}, bf16[64,1024]{1,0:T(8,128)(2,1)S(1)}, u32[]{:S(2)}, u32[]{:S(2)}) collective-permute-start(bf16[64,1024]{1,0:T(8,128)(2,1)S(1)} %get-tuple-element.21), channel_id=1, source_target_pairs={{0,30},{2,28},{4,26},{6,24},{8,22},{10,20},{12,18},{14,16},{16,14}... | collective-permute-start | bytes 393224 | tf_op jit(solution)/shard_map/ppermute | solution.py:393
  58.9 15.8 %collective-permute-start.1 = (bf16[64,1024]{1,0:T(8,128)(2,1)S(1)}, bf16[64,1024]{1,0:T(8,128)(2,1)S(1)}, u32[]{:S(2)}, u32[]{:S(2)}) collective-permute-start(bf16[64,1024]{1,0:T(8,128)(2,1)S(1)} %get-tuple-element.19), channel_id=1, source_target_pairs={{0,28},{2,30},{4,24},{6,26},{8,20},{10,22},{12,16},{14,18},{16,12}... | collective-permute-start | bytes 393224 | tf_op jit(solution)/shard_map/ppermute | solution.py:393

commit v10 on v9

--- a/solution.py
+++ b/solution.py
@@ -391,8 +391,8 @@
             ties = (past_kv,) if index >= half - 2 else (far[index - 4], own_kv)
             parcel = lax.optimization_barrier((parcel, *ties))[0]
         far.append(lax.ppermute(parcel, "dp", [(owner, owner ^ (half + index)) for owner in range(owners)]))
-    out = attend(meta, half, None, far[: half - 5], own, past, None)
-    out = attend(meta, half + half - 5, None, far[half - 5 : half - 2], own, past, out)
+    out = attend(meta, half, None, far[: half - 4], own, past, None)
+    out = attend(meta, half + half - 4, None, far[half - 4 : half - 2], own, past, out)
     out = attend(meta, 0, near, [], own, past, out)
     return attend(meta, half + half - 2, None, far[half - 2 :], own, past, out)
 

time: 77.9 us -> 77.8 us (level)
  waiting for transfers between devices: 27.4 us -> 24.6 us
  local copies, waits for them, and re-layouts: 2.71 us -> 4.46 us
  Pallas kernels: 17.4 us -> 18.7 us
    ppermute x1, waiting for transfers between devices: 3.79 us -> 2.06 us  [local(): lax.ppermute(own_kv, 'ctx', [(0, 1)])[None]]
    pallas_call x4, Pallas kernels: 12.2 us -> 13.6 us  [attend(): pl.pallas_call(kernel, out_shape=jax.ShapeDtypeStruct((rows, width), jnp....]
    squeeze x1, local copies, waits for them, and re-layouts: 0.04 us -> 0.99 us  [local(): own_kv[:2 * rows].reshape(rows, 2, LANES)[:, 1]]
    all_to_all x1, waiting for transfers between devices: 5.94 us -> 5.01 us  [local(): lax.all_to_all(near, 'dp', split_axis=0, concat_axis=0, axis_index_groups...]
    slice x1, local copies, waits for them, and re-layouts: 0.37 us -> 1.15 us  [local(): own_kv[:2 * rows].reshape(rows, 2, LANES)[:, 1]]
  transfers between devices with their start and end apart: 11 -> 11, of which waited for: 3 -> 3; matrix products, arithmetic and copies ran while one was open for 6% -> 8% of each run, Pallas kernels for 17% -> 18%
where the time goes in v10:
time: 77.8 us
  starting transfers between devices  27.6 us (35%)
  waiting for transfers between devices  24.6 us (32%)
  Pallas kernels  18.7 us (24%)
  local copies, waits for them, and re-layouts  4.46 us (6%)
  other arithmetic  1.96 us (3%)
    all_to_all x1, waiting for transfers between devices, local(): lax.all_to_all(send_kv, 'dp', split_axis=0, concat_axis=0, tiled=True)  17.5 us
    ppermute x8, starting transfers between devices, local(): lax.ppermute(parcel, 'dp', [(owner, owner ^ half + index) for owner in ra...  15.5 us
    pallas_call x4, Pallas kernels, attend(): pl.pallas_call(kernel, out_shape=jax.ShapeDtypeStruct((rows, width), jnp....  13.6 us
    all_to_all x1, starting transfers between devices, local(): lax.all_to_all(send_kv, 'dp', split_axis=0, concat_axis=0, tiled=True)  6.5 us
    all_to_all x1, waiting for transfers between devices, local(): lax.all_to_all(near, 'dp', split_axis=0, concat_axis=0, axis_index_groups...  5.01 us
    all_to_all x1, starting transfers between devices, local(): lax.all_to_all(near, 'dp', split_axis=0, concat_axis=0, axis_index_groups...  4.32 us
    pallas_call x1, Pallas kernels, pack_q(): pl.pallas_call(kernel, out_shape=[pltpu.HBM((half, cap, width), queries.d...  2.24 us
    ppermute x1, waiting for transfers between devices, local(): lax.ppermute(own_kv, 'ctx', [(0, 1)])[None]  2.06 us
  transfers between devices with their start and end apart: 11, of which 3 were waited for; matrix products, arithmetic and copies ran while one was open for 8% of the time, Pallas kernels for 18%

profile of v10, /device:TPU:5, one launch (start us, length us, event | category | flops | bytes accessed | tf_op | source)
XLA Modules:
  0.0 77.8 jit_solution(7928739154090448808)
XLA Ops:
  0.0 1.9 %pack_kv.1.earlier_ref = bf16[16,144,128]{2,1,0:T(8,128)(2,1)} custom-call(s32[2,512]{1,0:T(2,128)} %bitcast.19, s32[4,128]{1,0:T(4,128)} %bitcast.22, bf16[1024,128]{1,0:T(8,128)(2,1)} %bitcast.18), custom_call_target="tpu_custom_call" | custom-call | tf_op jit(solution)/shard_map/pack_kv/pallas_call | solution.py:83
  1.9 6.5 %all-to-all-start = ((bf16[16,144,128]{2,1,0:T(8,128)(2,1)}), bf16[16,144,128]{2,1,0:T(8,128)(2,1)S(1)}, u32[]{:S(2)}, u32[]{:S(2)}) async-start(bf16[16,144,128]{2,1,0:T(8,128)(2,1)} %pack_kv.1.earlier_ref), calls=%async_computation | async-start | bytes 1179648 | tf_op jit(solution)/shard_map/all_to_all | solution.py:359
  8.4 2.2 %pack_q.1 = (bf16[8,64,1024]{2,1,0:T(8,128)(2,1)}, bf16[64,1024]{1,0:T(8,128)(2,1)S(1)}, bf16[64,1024]{1,0:T(8,128)(2,1)S(1)}, bf16[64,1024]{1,0:T(8,128)(2,1)S(...) custom-call(s32[2,512]{1,0:T(2,128)} %bitcast.20, ...), custom_call_target="tpu_custom_call" | custom-call | tf_op jit(solution)/shard_map/pack_q/pallas_call | solution.py:135
  10.7 2.4 %collective-permute-start.3 = (bf16[64,1024]{1,0:T(8,128)(2,1)S(1)}, bf16[64,1024]{1,0:T(8,128)(2,1)S(1)}, u32[]{:S(2)}, u32[]{:S(2)}) collective-permute-start(bf16[64,1024]{1,0:T(8,128)(2,1)S(1)} %get-tuple-element.24), channel_id=1, source_target_pairs={{0,16},{2,18},{4,20},{6,22},{8,24},{10,26},{12,28},{14,30},{16,0},... | collective-permute-start | bytes 393224 | tf_op jit(solution)/shard_map/ppermute | solution.py:393
  13.1 0.4 collective-permute-start.5
  13.4 3.4 %collective-permute-start.7 = (bf16[64,1024]{1,0:T(8,128)(2,1)S(1)}, bf16[64,1024]{1,0:T(8,128)(2,1)S(1)}, u32[]{:S(2)}, u32[]{:S(2)}) collective-permute-start(bf16[64,1024]{1,0:T(8,128)(2,1)S(1)} %get-tuple-element.29), channel_id=1, source_target_pairs={{0,20},{2,22},{4,16},{6,18},{8,28},{10,30},{12,24},{14,26},{16,4},... | collective-permute-start | bytes 393224 | tf_op jit(solution)/shard_map/ppermute | solution.py:393
  16.9 0.3 collective-permute-start.8
  17.2 0.1 slice_xor_fusion
  17.2 0.1 pad_add_fusion
  17.3 17.5 %all-to-all-done.in_ref = bf16[16,144,128]{2,1,0:T(8,128)(2,1)S(1)} async-done(((bf16[16,144,128]{2,1,0:T(8,128)(2,1)}), bf16[16,144,128]{2,1,0:T(8,128)(2,1)S(1)}, u32[]{:S(2)}, u32[]{:S(2)}) %all-to-all-start) | async-done | bytes 589856 | tf_op jit(solution)/shard_map/all_to_all | solution.py:359
  34.8 4.3 %all-to-all-start.1 = ((bf16[8,64,1024]{2,1,0:T(8,128)(2,1)}), bf16[8,64,1024]{2,1,0:T(8,128)(2,1)S(1)}, u32[]{:S(2)}, u32[]{:S(2)}) async-start(bf16[8,64,1024]{2,1,0:T(8,128)(2,1)} %get-tuple-element.22), calls=%async_computation.1 | async-start | bytes 2097152 | tf_op jit(solution)/shard_map/all_to_all | solution.py:362
  39.1 0.7 slice_reduce_fusion.1
  39.9 0.1 select_reduce_fusion.2.source_ref
  40.0 0.1 add.112
  40.1 0.1 select_reduce_fusion
  40.2 0.1 reshape.420
  40.3 0.1 broadcast_in_dim_reshape.2
  40.4 1.0 %place_kv.1 = bf16[1040,128]{1,0:T(8,128)(2,1)S(1)} custom-call(s32[8]{0:T(128)S(1)} %select_reduce_fusion.2.source_ref, bf16[16,144,128]{2,1,0:T(8,128)(2,1)S(1)} %all-to-all-done.in_ref, bf16[16,128]{1,0:T(8,128)(2,1)S(1)} %pad.4.begin_ref), custom_call_target="tpu_custom_call" | custom-call | tf_op jit(solution)/shard_map/place_kv/pallas_call | solution.py:176
  41.4 1.3 %collective-permute-start = (bf16[1040,128]{1,0:T(8,128)(2,1)S(1)}, bf16[1040,128]{1,0:T(8,128)(2,1)}, u32[]{:S(2)}, u32[]{:S(2)}) collective-permute-start(bf16[1040,128]{1,0:T(8,128)(2,1)S(1)} %place_kv.1), channel_id=1, source_target_pairs={{0,1},{2,3},{4,5},{6,7},{8,9},{10,11},{12,13},{14,15},{16,17},{18,... | collective-permute-start | bytes 798728 | tf_op jit(solution)/shard_map/ppermute | solution.py:378
  42.7 1.2 %fusion.6 = (bf16[512,1,128]{2,1,0:T(2,128)(2,1)}, bf16[512,1,128]{2,1,0:T(2,128)(2,1)}) fusion(bf16[512,2,128]{2,1,0:T(2,128)(2,1)S(1)} %bitcast.17), kind=kLoop, calls=%fused_computation.59 | loop fusion | bytes 524288 | tf_op jit(solution)/shard_map/slice | solution.py:380
  43.9 0.1 reduce_min.9
  44.0 0.0 collective-permute-done.3.rest_0_
  44.0 3.6 %collective-permute-start.4 = (bf16[64,1024]{1,0:T(8,128)(2,1)S(1)}, bf16[64,1024]{1,0:T(8,128)(2,1)S(1)}, u32[]{:S(2)}, u32[]{:S(2)}) collective-permute-start(bf16[64,1024]{1,0:T(8,128)(2,1)S(1)} %get-tuple-element.25), channel_id=1, source_target_pairs={{0,24},{2,26},{4,28},{6,30},{8,16},{10,18},{12,20},{14,22},{16,8},... | collective-permute-start | bytes 393224 | tf_op jit(solution)/shard_map/ppermute | solution.py:393
  47.6 0.2 select_reduce_fusion.1
  47.8 0.0 collective-permute-done.5.rest_1_
  47.8 0.3 collective-permute-start.6
  48.1 0.2 select_convert_fusion.1
  48.3 0.1 pad_add_fusion.1.meta_ref
  48.4 0.0 copy-done
  48.4 1.0 %copy_bitcast_fusion.2 = (bf16[512,128]{1,0:T(8,128)(2,1)S(1)}, bf16[512,128]{1,0:T(8,128)(2,1)S(1)}) fusion(bf16[512,1,128]{2,1,0:T(2,128)(2,1)S(1)} %copy-done, bf16[512,1,128]{2,1,0:T(2,128)(2,1)} %get-tuple-element.36), kind=kLoop, calls=%fused_computation.7 | loop fusion | bytes 524288 | tf_op jit(solution)/shard_map/squeeze | solution.py:380
  49.4 2.1 %collective-permute-done = bf16[1040,128]{1,0:T(8,128)(2,1)} collective-permute-done((bf16[1040,128]{1,0:T(8,128)(2,1)S(1)}, bf16[1040,128]{1,0:T(8,128)(2,1)}, u32[]{:S(2)}, u32[]{:S(2)}) %collective-permute-start) | collective-permute-done | bytes 266272 | tf_op jit(solution)/shard_map/ppermute | solution.py:378
  51.5 1.0 %slice.75 = bf16[1,1024,128]{2,1,0:T(8,128)(2,1)S(1)} slice(bf16[1,1040,128]{2,1,0:T(8,128)(2,1)} %bitcast.7), slice={[0:1], [0:1024], [0:128]} | slice | bytes 524288 | tf_op jit(solution)/shard_map/slice | solution.py:383
  52.4 0.7 convert_convert_fusion.1
  53.1 5.1 %collective-permute-start.2 = (bf16[64,1024]{1,0:T(8,128)(2,1)S(1)}, bf16[64,1024]{1,0:T(8,128)(2,1)S(1)}, u32[]{:S(2)}, u32[]{:S(2)}) collective-permute-start(bf16[64,1024]{1,0:T(8,128)(2,1)S(1)} %get-tuple-element.21), channel_id=1, source_target_pairs={{0,30},{2,28},{4,26},{6,24},{8,22},{10,20},{12,18},{14,16},{16,14}... | collective-permute-start | bytes 393224 | tf_op jit(solution)/shard_map/ppermute | solution.py:393
  58.2 0.4 fusion.5
  58.6 0.2 select_convert_fusion.pd_ref
  58.8 0.0 collective-permute-done.7.rest_2_
  58.9 0.1 collective-permute-start.1
  58.9 0.0 collective-permute-done.8.rest_3_
  58.9 2.9 %attend.4.rest_2_ = bf16[512,1024]{1,0:T(8,128)(2,1)} custom-call(s32[25]{0:T(128)S(1)} %pad_add_fusion.1.meta_ref, bf16[512,128]{1,0:T(8,128)(2,1)S(1)} %get-tuple-element.38.qd_ref, bf16[512,128]{1,0:T(8,128)(2,1)S(1)} %get-tuple-element.48.ok_ref, bf16[512,128]{1,0:T(8,128)(2,1)S(1)} %get-tuple-element.37.od_ref, ...), custom_call_target="tpu_custom_call" | custom-call | flops 1073741824 | bytes 1048576 | tf_op jit(solution)/shard_map/attend/pallas_call | solution.py:315
  61.8 0.0 collective-permute-done.4.rest_0_
  61.9 0.0 collective-permute-done.6.rest_1_
  61.9 2.9 %attend.5.rest_1_ = bf16[512,1024]{1,0:T(8,128)(2,1)} custom-call(s32[25]{0:T(128)S(1)} %pad_add_fusion.1.meta_ref, bf16[512,128]{1,0:T(8,128)(2,1)S(1)} %get-tuple-element.38.qd_ref, bf16[512,128]{1,0:T(8,128)(2,1)S(1)} %get-tuple-element.48.ok_ref, bf16[512,128]{1,0:T(8,128)(2,1)S(1)} %get-tuple-element.37.od_ref, ...), custom_call_target="tpu_custom_call", output_to_operand_aliasing={{}: (10, {})} | custom-call | flops 536870912 | bytes 524288 | tf_op jit(solution)/shard_map/attend/pallas_call | solution.py:315
  64.8 5.0 %all-to-all-done.1.rest_0_ = bf16[8,64,1024]{2,1,0:T(8,128)(2,1)S(1)} async-done(((bf16[8,64,1024]{2,1,0:T(8,128)(2,1)}), bf16[8,64,1024]{2,1,0:T(8,128)(2,1)S(1)}, u32[]{:S(2)}, u32[]{:S(2)}) %all-to-all-start.1) | async-done | bytes 1048608 | tf_op jit(solution)/shard_map/all_to_all | solution.py:362
  69.8 4.9 %attend.6.rest_2_ = bf16[512,1024]{1,0:T(8,128)(2,1)} custom-call(s32[25]{0:T(128)S(1)} %pad_add_fusion.1.meta_ref, bf16[512,128]{1,0:T(8,128)(2,1)S(1)} %get-tuple-element.38.qd_ref, bf16[512,128]{1,0:T(8,128)(2,1)S(1)} %get-tuple-element.48.ok_ref, bf16[512,128]{1,0:T(8,128)(2,1)S(1)} %get-tuple-element.37.od_ref, ...), custom_call_target="tpu_custom_call", output_to_operand_aliasing={{}: (9, {})} | custom-call | flops 2147483648 | bytes 2097152 | tf_op jit(solution)/shard_map/attend/pallas_call | solution.py:315
  74.6 0.0 collective-permute-done.2.rest_1_
  74.7 0.0 collective-permute-done.1.rest_0_
  74.7 2.9 %attend.7 = bf16[512,1024]{1,0:T(8,128)(2,1)} custom-call(s32[25]{0:T(128)S(1)} %pad_add_fusion.1.meta_ref, bf16[512,128]{1,0:T(8,128)(2,1)S(1)} %get-tuple-element.38.qd_ref, bf16[512,128]{1,0:T(8,128)(2,1)S(1)} %get-tuple-element.48.ok_ref, bf16[512,128]{1,0:T(8,128)(2,1)S(1)} %get-tuple-element.37.od_ref, ...), custom_call_target="tpu_custom_call", output_to_operand_aliasing={{}: (10, {})} | custom-call | flops 536870912 | bytes 524288 | tf_op jit(solution)/shard_map/attend/pallas_call | solution.py:315
  (21 shorter events, 0.2 us)
Async XLA Ops:
  1.9 32.9 %all-to-all-start = ((bf16[16,144,128]{2,1,0:T(8,128)(2,1)}), bf16[16,144,128]{2,1,0:T(8,128)(2,1)S(1)}, u32[]{:S(2)}, u32[]{:S(2)}) async-start(bf16[16,144,128]{2,1,0:T(8,128)(2,1)} %pack_kv.1.earlier_ref), calls=%async_computation | async-start | bytes 1179648 | tf_op jit(solution)/shard_map/all_to_all | solution.py:359
  10.7 33.3 %collective-permute-start.3 = (bf16[64,1024]{1,0:T(8,128)(2,1)S(1)}, bf16[64,1024]{1,0:T(8,128)(2,1)S(1)}, u32[]{:S(2)}, u32[]{:S(2)}) collective-permute-start(bf16[64,1024]{1,0:T(8,128)(2,1)S(1)} %get-tuple-element.24), channel_id=1, source_target_pairs={{0,16},{2,18},{4,20},{6,22},{8,24},{10,26},{12,28},{14,30},{16,0},... | collective-permute-start | bytes 393224 | tf_op jit(solution)/shard_map/ppermute | solution.py:393
  13.1 34.7 %collective-permute-start.5 = (bf16[64,1024]{1,0:T(8,128)(2,1)S(1)}, bf16[64,1024]{1,0:T(8,128)(2,1)S(1)}, u32[]{:S(2)}, u32[]{:S(2)}) collective-permute-start(bf16[64,1024]{1,0:T(8,128)(2,1)S(1)} %get-tuple-element.27), channel_id=1, source_target_pairs={{0,18},{2,16},{4,22},{6,20},{8,26},{10,24},{12,30},{14,28},{16,2},... | collective-permute-start | bytes 393224 | tf_op jit(solution)/shard_map/ppermute | solution.py:393
  13.4 45.4 %collective-permute-start.7 = (bf16[64,1024]{1,0:T(8,128)(2,1)S(1)}, bf16[64,1024]{1,0:T(8,128)(2,1)S(1)}, u32[]{:S(2)}, u32[]{:S(2)}) collective-permute-start(bf16[64,1024]{1,0:T(8,128)(2,1)S(1)} %get-tuple-element.29), channel_id=1, source_target_pairs={{0,20},{2,22},{4,16},{6,18},{8,28},{10,30},{12,24},{14,26},{16,4},... | collective-permute-start | bytes 393224 | tf_op jit(solution)/shard_map/ppermute | solution.py:393
  16.9 42.1 %collective-permute-start.8 = (bf16[64,1024]{1,0:T(8,128)(2,1)S(1)}, bf16[64,1024]{1,0:T(8,128)(2,1)}, u32[]{:S(2)}, u32[]{:S(2)}) collective-permute-start(bf16[64,1024]{1,0:T(8,128)(2,1)S(1)} %get-tuple-element.30), channel_id=1, source_target_pairs={{0,22},{2,20},{4,18},{6,16},{8,30},{10,28},{12,26},{14,24},{16,6},... | collective-permute-start | bytes 393224 | tf_op jit(solution)/shard_map/ppermute | solution.py:393
  34.8 34.9 %all-to-all-start.1 = ((bf16[8,64,1024]{2,1,0:T(8,128)(2,1)}), bf16[8,64,1024]{2,1,0:T(8,128)(2,1)S(1)}, u32[]{:S(2)}, u32[]{:S(2)}) async-start(bf16[8,64,1024]{2,1,0:T(8,128)(2,1)} %get-tuple-element.22), calls=%async_computation.1 | async-start | bytes 2097152 | tf_op jit(solution)/shard_map/all_to_all | solution.py:362
  41.4 10.0 %collective-permute-start = (bf16[1040,128]{1,0:T(8,128)(2,1)S(1)}, bf16[1040,128]{1,0:T(8,128)(2,1)}, u32[]{:S(2)}, u32[]{:S(2)}) collective-permute-start(bf16[1040,128]{1,0:T(8,128)(2,1)S(1)} %place_kv.1), channel_id=1, source_target_pairs={{0,1},{2,3},{4,5},{6,7},{8,9},{10,11},{12,13},{14,15},{16,17},{18,... | collective-permute-start | bytes 798728 | tf_op jit(solution)/shard_map/ppermute | solution.py:378
  44.0 4.4 %copy-start = (bf16[512,1,128]{2,1,0:T(2,128)(2,1)S(1)}, bf16[512,1,128]{2,1,0:T(2,128)(2,1)}, u32[]{:S(2)}) copy-start(bf16[512,1,128]{2,1,0:T(2,128)(2,1)} %get-tuple-element.35) | copy-start | bytes 393220
  44.0 17.8 %collective-permute-start.4 = (bf16[64,1024]{1,0:T(8,128)(2,1)S(1)}, bf16[64,1024]{1,0:T(8,128)(2,1)S(1)}, u32[]{:S(2)}, u32[]{:S(2)}) collective-permute-start(bf16[64,1024]{1,0:T(8,128)(2,1)S(1)} %get-tuple-element.25), channel_id=1, source_target_pairs={{0,24},{2,26},{4,28},{6,30},{8,16},{10,18},{12,20},{14,22},{16,8},... | collective-permute-start | bytes 393224 | tf_op jit(solution)/shard_map/ppermute | solution.py:393
  47.8 14.1 %collective-permute-start.6 = (bf16[64,1024]{1,0:T(8,128)(2,1)S(1)}, bf16[64,1024]{1,0:T(8,128)(2,1)S(1)}, u32[]{:S(2)}, u32[]{:S(2)}) collective-permute-start(bf16[64,1024]{1,0:T(8,128)(2,1)S(1)} %get-tuple-element.28), channel_id=1, source_target_pairs={{0,26},{2,24},{4,30},{6,28},{8,18},{10,16},{12,22},{14,20},{16,10}... | collective-permute-start | bytes 393224 | tf_op jit(solution)/shard_map/ppermute | solution.py:393
  53.1 21.5 %collective-permute-start.2 = (bf16[64,1024]{1,0:T(8,128)(2,1)S(1)}, bf16[64,1024]{1,0:T(8,128)(2,1)S(1)}, u32[]{:S(2)}, u32[]{:S(2)}) collective-permute-start(bf16[64,1024]{1,0:T(8,128)(2,1)S(1)} %get-tuple-element.21), channel_id=1, source_target_pairs={{0,30},{2,28},{4,26},{6,24},{8,22},{10,20},{12,18},{14,16},{16,14}... | collective-permute-start | bytes 393224 | tf_op jit(solution)/shard_map/ppermute | solution.py:393
  58.9 15.8 %collective-permute-start.1 = (bf16[64,1024]{1,0:T(8,128)(2,1)S(1)}, bf16[64,1024]{1,0:T(8,128)(2,1)S(1)}, u32[]{:S(2)}, u32[]{:S(2)}) collective-permute-start(bf16[64,1024]{1,0:T(8,128)(2,1)S(1)} %get-tuple-element.19), channel_id=1, source_target_pairs={{0,28},{2,30},{4,24},{6,26},{8,20},{10,22},{12,16},{14,18},{16,12}... | collective-permute-start | bytes 393224 | tf_op jit(solution)/shard_map/ppermute | solution.py:393
